TPU v7x, 32 devices: a whole 2x2x4 slice. The times are simulated.
32 devices in a mesh: dp: 16 (over z, x, core), mp: 2 (over y).
Axes of the slice: x: 2, y: 2, z: 4, core: 2. Of those that a mesh axis runs over, the one named last changes fastest.
Arguments:
- tokens: bfloat16 [16384, 1024], P(('dp', 'mp')), may hold values from -6 to 6
- memory: bfloat16 [65536, 1024], P(('dp', 'mp')), may hold values from -6 to 6
- cotangent: bfloat16 [16384, 1024], P(('dp', 'mp')), may hold values from -6 to 6
- target_lengths: int32 [64], P('dp'), may hold values from 1 to 256, as said below
- memory_lengths: int32 [64], P('dp'), may hold values from 40 to 1024, as said below
- norm_self: bfloat16 [1024], replicated, may hold values from 0.099609375 to 1.8984375
- query_self: bfloat16 [1024, 1024], P(None, 'mp'), may hold values from -0.046875 to 0.046875
- key_self: bfloat16 [1024, 1024], P(None, 'mp'), may hold values from -0.1875 to 0.1875
- value_self: bfloat16 [1024, 1024], P(None, 'mp'), may hold values from -0.1875 to 0.1875
- out_self: bfloat16 [1024, 1024], P('mp'), may hold values from -0.75 to 0.75
- bias_table: bfloat16 [32, 16], P(None, 'mp'), may hold values from -4 to 4
- norm_cross: bfloat16 [1024], replicated, may hold values from 0.099609375 to 1.8984375
- query_cross: bfloat16 [1024, 1024], P(None, 'mp'), may hold values from -0.046875 to 0.046875
- key_cross: bfloat16 [1024, 1024], P(None, 'mp'), may hold values from -0.1875 to 0.1875
- value_cross: bfloat16 [1024, 1024], P(None, 'mp'), may hold values from -0.1875 to 0.1875
- out_cross: bfloat16 [1024, 1024], P('mp'), may hold values from -1 to 1
- norm_ffn: bfloat16 [1024], replicated, may hold values from 0.099609375 to 1.8984375
- ffn_in: bfloat16 [1024, 4096], P(None, 'mp'), may hold values from -0.1875 to 0.1875
- ffn_out: bfloat16 [4096, 1024], P('mp'), may hold values from -0.09375 to 0.09375
Outputs:
- block_out: bfloat16 [16384, 1024], P(('dp', 'mp'))
- tokens_grad: bfloat16 [16384, 1024], P(('dp', 'mp'))
- memory_grad: bfloat16 [65536, 1024], P(('dp', 'mp'))
- norm_self_grad: float32 [1024], replicated
- query_self_grad: float32 [1024, 1024], P(None, 'mp')
- key_self_grad: float32 [1024, 1024], P(None, 'mp')
- value_self_grad: float32 [1024, 1024], P(None, 'mp')
- out_self_grad: float32 [1024, 1024], P('mp')
- bias_table_grad: float32 [32, 16], P(None, 'mp')
- norm_cross_grad: float32 [1024], replicated
- query_cross_grad: float32 [1024, 1024], P(None, 'mp')
- key_cross_grad: float32 [1024, 1024], P(None, 'mp')
- value_cross_grad: float32 [1024, 1024], P(None, 'mp')
- out_cross_grad: float32 [1024, 1024], P('mp')
- norm_ffn_grad: float32 [1024], replicated
- ffn_in_grad: float32 [1024, 4096], P(None, 'mp')
- ffn_out_grad: float32 [4096, 1024], P('mp')
Inputs may be any that keep to these rules, and one draw needn't show every extreme that they name: `target_lengths`: in every group of 4 consecutive examples one example has target length 256. `memory_lengths`: the example of each group that has target length 256 has memory length 1024.
All inputs are finite; a program needn't handle non-finite values.
Results may differ from a plain program's by a relative error of at most 0.024.
The roundings to bfloat16 on the way count: a program that leaves them out, or rounds other values in their place, can miss the bound.
Values may be sent and summed in bfloat16 or wider, within the bound.
A program may use at most 384 MiB of HBM per device.

v0:
```python
import functools
import math

import jax
import jax.numpy as jnp
import numpy as np
from jax import lax
from jax.experimental import pallas as pl
from jax.experimental.pallas import tpu as pltpu
from jax.sharding import PartitionSpec as P

HEAD_DIM = 64
BUCKETS = 32


epsilon = 1e-06
masked_score = -1e30
highest = lax.Precision.HIGHEST


def bucket_edges():
    exact = list(range(1, 17))
    spaced = [int(math.ceil(16.0 * 8.0 ** ((level - 16) / 16.0))) for level in range(17, 32)]
    return np.array(exact + spaced, dtype=np.int32)


def rms_norm(value, gain):
    factor = lax.rsqrt(jnp.mean(value * value, axis=-1, keepdims=True) + epsilon)
    return value * factor * gain


def gather_rows(value):
    return lax.all_gather(value, "mp", axis=0, tiled=True)


def spread_rows(value):
    return lax.psum_scatter(value, "mp", scatter_dimension=0, tiled=True)


def matmul(left, right):
    return jnp.dot(left, right, preferred_element_type=jnp.float32)


def left_product(left, right):
    return lax.dot_general(
        left, right, (((0,), (0,)), ((), ())), preferred_element_type=jnp.float32
    )


def right_product(left, right):
    return lax.dot_general(
        left, right, (((1,), (1,)), ((), ())), preferred_element_type=jnp.float32
    )


def attend_forward(query, key_rows, value_rows, score_bias, mask):
    scores = jnp.einsum("pehd,kehd->ehpk", query, key_rows, preferred_element_type=jnp.float32)
    if score_bias is not None:
        scores = scores + score_bias[None]
    scores = jnp.where(mask, scores, masked_score)
    row_max = jnp.max(scores, axis=-1, keepdims=True)
    weights = jnp.exp(scores - row_max)
    probs = weights / jnp.sum(weights, axis=-1, keepdims=True)
    probs_low = probs.astype(jnp.bfloat16)
    output = jnp.einsum(
        "ehpk,kehd->pehd", probs_low, value_rows, preferred_element_type=jnp.float32
    )
    return (probs, probs_low, output.astype(jnp.bfloat16))


def attend_backward(query, key_rows, value_rows, probs, probs_low, grad_mixed):
    grad_probs = jnp.einsum(
        "pehd,kehd->ehpk", grad_mixed, value_rows, preferred_element_type=jnp.float32
    )
    inner_sum = jnp.sum(probs * grad_probs, axis=-1, keepdims=True)
    grad_scores = (probs * (grad_probs - inner_sum)).astype(jnp.bfloat16)
    grad_query = jnp.einsum(
        "ehpk,kehd->pehd", grad_scores, key_rows, preferred_element_type=jnp.float32
    )
    grad_keys = jnp.einsum(
        "ehpk,pehd->kehd", grad_scores, query, preferred_element_type=jnp.float32
    )
    grad_values = jnp.einsum(
        "ehpk,pehd->kehd", probs_low, grad_mixed, preferred_element_type=jnp.float32
    )
    return (
        grad_scores,
        grad_query.astype(jnp.bfloat16),
        grad_keys.astype(jnp.bfloat16),
        grad_values.astype(jnp.bfloat16),
    )


def norm_backward(value, gain, grad_normed):
    pullback = jax.vjp(rms_norm, value, gain.astype(jnp.float32))[1]
    return pullback(grad_normed)


def on_device(
    tokens,
    memory,
    cotangent,
    target_lengths,
    memory_lengths,
    norm_self,
    query_self,
    key_self,
    value_self,
    out_self,
    bias_table,
    norm_cross,
    query_cross,
    key_cross,
    value_cross,
    out_cross,
    norm_ffn,
    ffn_in,
    ffn_out,
):
    examples = target_lengths.shape[0]
    local_rows = tokens.shape[0]
    parts = lax.axis_size("mp")
    device_rank = lax.axis_index("mp")
    local_pos = local_rows // examples
    total_pos = local_pos * parts
    memory_local = memory.shape[0]
    memory_total = memory_local * parts
    memory_pos = memory_total // examples
    inner_local = query_self.shape[1]
    heads = inner_local // HEAD_DIM
    total_rows = local_rows * parts
    group_count = jnp.sum(target_lengths).astype(jnp.float32)
    total_count = lax.psum(group_count, "dp")
    token_scale = lax.axis_size("dp") * group_count / total_count
    positions = device_rank * local_pos + jnp.arange(local_pos, dtype=jnp.int32)
    live_rows = (
        (positions[:, None] < target_lengths[None, :]).astype(jnp.float32).reshape(local_rows, 1)
    )
    target_pos = jnp.arange(total_pos, dtype=jnp.int32)
    distance = jnp.maximum(target_pos[:, None] - target_pos[None, :], 0)
    buckets = jnp.sum(
        (distance[:, :, None] >= jnp.asarray(bucket_edges())[None, None, :]).astype(jnp.int32),
        axis=-1,
    )
    table_hot = (buckets[:, :, None] == jnp.arange(BUCKETS, dtype=jnp.int32)[None, None, :]).astype(
        jnp.float32
    )
    causal = target_pos[None, :] <= target_pos[:, None]
    self_mask = causal[None, None] & (
        target_pos[None, None, None, :] < target_lengths[:, None, None, None]
    )
    cross_pos = jnp.arange(memory_pos, dtype=jnp.int32)
    cross_mask = cross_pos[None, None, None, :] < memory_lengths[:, None, None, None]
    score_bias = jnp.einsum(
        "qkb,bh->hqk", table_hot, bias_table.astype(jnp.float32), precision=highest
    )

    def target_view(value):
        return value.reshape(total_pos, examples, heads, HEAD_DIM)

    def memory_view(value):
        return value.reshape(memory_pos, examples, heads, HEAD_DIM)

    tokens_float = tokens.astype(jnp.float32)
    normed_one = rms_norm(tokens_float, norm_self.astype(jnp.float32)).astype(jnp.bfloat16)
    rows_one = gather_rows(normed_one)
    self_weights = jnp.concatenate([query_self, key_self, value_self], axis=1)
    projected = matmul(rows_one, self_weights).astype(jnp.bfloat16)
    query_one = target_view(projected[:, :inner_local])
    keys_one = target_view(projected[:, inner_local : 2 * inner_local])
    values_one = target_view(projected[:, 2 * inner_local :])
    probs_one, low_one, mixed_one = attend_forward(
        query_one, keys_one, values_one, score_bias, self_mask
    )
    mixed_rows_one = mixed_one.reshape(total_rows, inner_local)
    resid_one = tokens_float + spread_rows(matmul(mixed_rows_one, out_self))
    normed_two = rms_norm(resid_one, norm_cross.astype(jnp.float32)).astype(jnp.bfloat16)
    rows_two = gather_rows(normed_two)
    query_two = target_view(matmul(rows_two, query_cross).astype(jnp.bfloat16))
    memory_all = lax.all_gather(memory, "mp", axis=0, tiled=True)
    cross_kv = matmul(memory_all, jnp.concatenate([key_cross, value_cross], axis=1)).astype(
        jnp.bfloat16
    )
    keys_flat = cross_kv[:, :inner_local]
    values_flat = cross_kv[:, inner_local:]
    keys_two = memory_view(keys_flat)
    values_two = memory_view(values_flat)
    probs_two, low_two, mixed_two = attend_forward(
        query_two, keys_two, values_two, None, cross_mask
    )
    mixed_rows_two = mixed_two.reshape(total_rows, inner_local)
    resid_two = resid_one + spread_rows(matmul(mixed_rows_two, out_cross))
    normed_three = rms_norm(resid_two, norm_ffn.astype(jnp.float32)).astype(jnp.bfloat16)
    rows_three = gather_rows(normed_three)
    pre_act = matmul(rows_three, ffn_in)
    hidden = jax.nn.gelu(pre_act).astype(jnp.bfloat16)
    block_out = resid_two + spread_rows(matmul(hidden, ffn_out))
    grad_out = cotangent.astype(jnp.float32) * live_rows * token_scale
    grad_rows_three = gather_rows(grad_out.astype(jnp.bfloat16))
    ffn_out_grad = left_product(hidden, grad_rows_three)
    grad_hidden = right_product(grad_rows_three, ffn_out)
    gelu_back = jax.vjp(jax.nn.gelu, pre_act)[1]
    grad_pre = gelu_back(grad_hidden)[0].astype(jnp.bfloat16)
    ffn_in_grad = left_product(rows_three, grad_pre)
    grad_normed_three = spread_rows(right_product(grad_pre, ffn_in))
    grad_resid_three, gain_three = norm_backward(resid_two, norm_ffn, grad_normed_three)
    grad_two = grad_out + grad_resid_three
    grad_rows_two = gather_rows(grad_two.astype(jnp.bfloat16))
    out_cross_grad = left_product(mixed_rows_two, grad_rows_two)
    grad_mixed_two = target_view(right_product(grad_rows_two, out_cross).astype(jnp.bfloat16))
    cross_back = attend_backward(
        query_two, keys_two, values_two, probs_two, low_two, grad_mixed_two
    )
    grad_query_two = cross_back[1].reshape(total_rows, inner_local)
    grad_keys_two = cross_back[2].reshape(memory_total, inner_local)
    grad_values_two = cross_back[3].reshape(memory_total, inner_local)
    query_cross_grad = left_product(rows_two, grad_query_two)
    grad_normed_two = spread_rows(right_product(grad_query_two, query_cross))
    key_cross_grad = left_product(memory_all, grad_keys_two)
    value_cross_grad = left_product(memory_all, grad_values_two)
    memory_terms = right_product(grad_keys_two, key_cross) + right_product(
        grad_values_two, value_cross
    )
    memory_grad = lax.psum_scatter(memory_terms, "mp", scatter_dimension=0, tiled=True)
    grad_resid_two, gain_two = norm_backward(resid_one, norm_cross, grad_normed_two)
    grad_one = grad_two + grad_resid_two
    grad_rows_one = gather_rows(grad_one.astype(jnp.bfloat16))
    out_self_grad = left_product(mixed_rows_one, grad_rows_one)
    grad_mixed_one = target_view(right_product(grad_rows_one, out_self).astype(jnp.bfloat16))
    self_back = attend_backward(query_one, keys_one, values_one, probs_one, low_one, grad_mixed_one)
    bias_table_grad = jnp.einsum(
        "ehqk,qkb->bh", self_back[0].astype(jnp.float32), table_hot, precision=highest
    )
    grad_projected = jnp.concatenate(
        [
            self_back[1].reshape(total_rows, inner_local),
            self_back[2].reshape(total_rows, inner_local),
            self_back[3].reshape(total_rows, inner_local),
        ],
        axis=1,
    )
    self_weight_grad = left_product(rows_one, grad_projected)
    grad_normed_one = spread_rows(right_product(grad_projected, self_weights))
    grad_resid_one, gain_one = norm_backward(tokens_float, norm_self, grad_normed_one)
    tokens_grad = grad_one + grad_resid_one
    summed = lax.psum(
        (
            self_weight_grad[:, :inner_local],
            self_weight_grad[:, inner_local : 2 * inner_local],
            self_weight_grad[:, 2 * inner_local :],
            out_self_grad,
            bias_table_grad,
            query_cross_grad,
            key_cross_grad,
            value_cross_grad,
            out_cross_grad,
            ffn_in_grad,
            ffn_out_grad,
        ),
        "dp",
    )
    gains = lax.psum((gain_one, gain_two, gain_three), ("dp", "mp"))
    return (
        block_out.astype(jnp.bfloat16),
        tokens_grad.astype(jnp.bfloat16),
        memory_grad.astype(jnp.bfloat16),
        gains[0],
        summed[0],
        summed[1],
        summed[2],
        summed[3],
        summed[4],
        gains[1],
        summed[5],
        summed[6],
        summed[7],
        summed[8],
        gains[2],
        summed[9],
        summed[10],
    )


def links(dp_size):
    total = 2 * dp_size

    def swap(bit):
        return [(at, at ^ bit) for at in range(total)]

    def off_swap(bit):
        return [(at, at ^ bit) for at in range(total) if (at & 1) != ((at >> 1) & 1)]

    def turned(at):
        return (at & ~3) | ((at & 1) << 1) | ((at >> 1) & 1)

    def crossed(at):
        return (at & ~3) | ((1 - (at & 1)) << 1) | ((at >> 1) & 1)

    return {
        "turn": [(at, turned(at)) for at in range(total) if at != turned(at)],
        "cross": [(at, crossed(at)) for at in range(total)],
        "y": swap(1),
        "core": swap(2),
        "x": swap(4),
        "zl": swap(8),
        "zh": swap(16),
        "off_x": off_swap(4),
        "off_zl": off_swap(8),
    }


def permute(value, pairs):
    return lax.ppermute(value, ("dp", "mp"), pairs)


def reorder_kernel(inverse, examples, info, held, arrived, target):
    def write(source):
        if inverse:
            value = source[...].reshape(-1, source.shape[2])
        else:
            value = source[...]
        rows = value.shape[0]
        chunk = rows // examples
        high = lax.broadcasted_iota(jnp.int32, (rows, rows), 0)
        low = lax.broadcasted_iota(jnp.int32, (rows, rows), 1)
        if inverse:
            hot = low == (high % examples) * chunk + high // examples
        else:
            hot = low == (high % chunk) * examples + high // chunk
        moved = nn(hot.astype(jnp.bfloat16), value).astype(jnp.bfloat16)
        target[...] = moved.reshape(target.shape)

    @pl.when(info[0] == 1)
    def _():
        write(held)

    @pl.when(info[0] == 0)
    def _():
        write(arrived)


def reorder(inverse, held, arrived, settled, examples):
    rows, width = held.shape
    block = 256
    flat = pl.BlockSpec((block, width), lambda i, s: (i, 0))
    flat_shape = (rows, width)
    split_shape = (examples, rows // examples, width)
    split_block = (examples, block // examples, width)
    if inverse:
        held, arrived = held.reshape(split_shape), arrived.reshape(split_shape)
        in_specs = [
            pl.BlockSpec(split_block, lambda i, s: (0, i * s[0], 0)),
            pl.BlockSpec(split_block, lambda i, s: (0, i * (1 - s[0]), 0)),
        ]
        out_spec, out_shape = flat, flat_shape
    else:
        in_specs = [
            pl.BlockSpec((block, width), lambda i, s: (i * s[0], 0)),
            pl.BlockSpec((block, width), lambda i, s: (i * (1 - s[0]), 0)),
        ]
        out_spec = pl.BlockSpec(split_block, lambda i, s: (0, i, 0))
        out_shape = split_shape
    return pl.pallas_call(
        functools.partial(reorder_kernel, inverse, examples),
        grid_spec=pltpu.PrefetchScalarGridSpec(
            num_scalar_prefetch=1,
            grid=(rows // block,),
            in_specs=in_specs,
            out_specs=out_spec,
        ),
        out_shape=jax.ShapeDtypeStruct(out_shape, held.dtype),
        cost_estimate=cost(2 * rows * width * block, 4 * rows * width),
        compiler_params=pltpu.CompilerParams(vmem_limit_bytes=SMALL_VMEM),
    )(settled, held, arrived).reshape(flat_shape)


def nt(left, right):
    return lax.dot_general(
        left, right, (((1,), (1,)), ((), ())), preferred_element_type=jnp.float32
    )


def tn(left, right):
    return lax.dot_general(
        left, right, (((0,), (0,)), ((), ())), preferred_element_type=jnp.float32
    )


def nn(left, right):
    return jnp.dot(left, right, preferred_element_type=jnp.float32)


def one_head(value, head):
    lane = lax.broadcasted_iota(jnp.int32, value.shape, 1)
    return jnp.where(lane // HEAD_DIM == head, value, jnp.zeros_like(value))


def softmax_columns(scores):
    top = jnp.max(scores, axis=0, keepdims=True)
    weights = jnp.exp(scores - top)
    return weights * (1.0 / jnp.sum(weights, axis=0, keepdims=True))


def toeplitz(row, size):
    return pltpu.roll(jnp.broadcast_to(row, (size, size)), 0, 1, stride=1, stride_axis=0)


def diagonals(square):
    size = square.shape[0]
    row = lax.broadcasted_iota(jnp.int32, square.shape, 0)
    turned, step = square, 1
    while step < size:
        moved = pltpu.roll(turned, size - step, 1)
        turned = jnp.where((row & step) != 0, moved, turned)
        step *= 2
    return jnp.sum(turned, axis=0, keepdims=True)


def ordered(core, scratch, own, far):
    half = own.shape[0]
    scratch[pl.ds(pl.multiple_of(core * half, half), half), :] = own
    scratch[pl.ds(pl.multiple_of((1 - core) * half, half), half), :] = far
    return scratch[...]


def split_store(core, scratch, value, out):
    half = out.shape[1]
    scratch[...] = value
    out[0] = scratch[pl.ds(pl.multiple_of(core * half, half), half), :]
    out[1] = scratch[pl.ds(pl.multiple_of((1 - core) * half, half), half), :]


def self_scores(query, keys, bias, head, length):
    scores = nt(keys, one_head(query, head)) + bias
    key_at = lax.broadcasted_iota(jnp.int32, scores.shape, 0)
    query_at = lax.broadcasted_iota(jnp.int32, scores.shape, 1)
    return jnp.where((key_at <= query_at) & (key_at < length), scores, masked_score)


def heads_joined(first, second):
    return jnp.concatenate([first[:HEAD_DIM], second[HEAD_DIM:]], axis=0).T


def self_forward_kernel(info, rows, bias, out, scratch, out_scratch, bias_scratch):
    core = info[0]
    example = pl.program_id(1)
    length = info[1 + example]
    size = scratch.shape[0]

    @pl.when(example == 0)
    def _():
        for head in range(2):
            bias_scratch[head] = toeplitz(bias[0, head : head + 1, :], size)

    joined = ordered(core, scratch, rows[0], rows[1])
    query, keys, values = joined[:, :128], joined[:, 128:256], joined[:, 256:]
    mixed = []
    for head in range(2):
        probs = softmax_columns(self_scores(query, keys, bias_scratch[head], head, length))
        mixed.append(tn(values, probs.astype(jnp.bfloat16)))
    result = heads_joined(*mixed).astype(jnp.bfloat16)
    split_store(core, out_scratch, result, out)


def self_backward_kernel(
    info,
    rows,
    bias,
    grads,
    out,
    out_bias,
    scratch,
    grad_scratch,
    out_scratch,
    bias_scratch,
    sum_scratch,
):
    core = info[0]
    example = pl.program_id(1)
    length = info[1 + example]
    size = scratch.shape[0]

    @pl.when(example == 0)
    def _():
        for head in range(2):
            bias_scratch[head] = toeplitz(bias[0, head : head + 1, :], size)
        sum_scratch[...] = jnp.zeros_like(sum_scratch)

    joined = ordered(core, scratch, rows[0], rows[1])
    query, keys, values = joined[:, :128], joined[:, 128:256], joined[:, 256:]
    grad = ordered(core, grad_scratch, grads[0], grads[1])
    grad_query, grad_keys, grad_values, squares = [], [], [], []
    for head in range(2):
        probs = softmax_columns(self_scores(query, keys, bias_scratch[head], head, length))
        low = probs.astype(jnp.bfloat16)
        grad_head = one_head(grad, head)
        grad_probs = nt(values, grad_head)
        inner = jnp.sum(probs * grad_probs, axis=0, keepdims=True)
        grad_scores = (probs * (grad_probs - inner)).astype(jnp.bfloat16)
        grad_values.append(nn(low, grad_head))
        grad_keys.append(nn(grad_scores, one_head(query, head)))
        grad_query.append(tn(keys, grad_scores))
        squares.append(grad_scores.astype(jnp.float32))
    for head in range(2):
        sum_scratch[head] = sum_scratch[head] + squares[head]
    result = jnp.concatenate(
        [
            heads_joined(*grad_query),
            grad_keys[0] + grad_keys[1],
            grad_values[0] + grad_values[1],
        ],
        axis=1,
    ).astype(jnp.bfloat16)
    split_store(core, out_scratch, result, out)

    @pl.when(example == pl.num_programs(1) - 1)
    def _():
        for head in range(2):
            out_bias[0, head : head + 1, :] = diagonals(sum_scratch[head])


def cross_scores(query, keys, head, core, length):
    scores = nt(keys, one_head(query, head))
    size = scores.shape[0]
    key_at = lax.broadcasted_iota(jnp.int32, scores.shape, 0)
    key_at = (key_at + core * (size // 2)) & (size - 1)
    return jnp.where(key_at < length, scores, masked_score)


def cross_forward_kernel(info, queries, kv_own, kv_far, out):
    core = info[0]
    length = info[1 + pl.program_id(0)]
    query = queries[...].reshape(-1, 128)
    keys = jnp.concatenate([kv_own[:, :128], kv_far[:, :128]], axis=0)
    values = jnp.concatenate([kv_own[:, 128:], kv_far[:, 128:]], axis=0)
    mixed = []
    for head in range(2):
        probs = softmax_columns(cross_scores(query, keys, head, core, length))
        mixed.append(tn(values, probs.astype(jnp.bfloat16)))
    out[...] = heads_joined(*mixed).astype(jnp.bfloat16).reshape(out.shape)


def cross_backward_kernel(info, queries, kv_own, kv_far, grads, dq, dkv_own, dkv_far):
    core = info[0]
    length = info[1 + pl.program_id(0)]
    query = queries[...].reshape(-1, 128)
    grad = grads[...].reshape(-1, 128)
    keys = jnp.concatenate([kv_own[:, :128], kv_far[:, :128]], axis=0)
    values = jnp.concatenate([kv_own[:, 128:], kv_far[:, 128:]], axis=0)
    grad_query, grad_keys, grad_values = [], [], []
    for head in range(2):
        probs = softmax_columns(cross_scores(query, keys, head, core, length))
        low = probs.astype(jnp.bfloat16)
        grad_head = one_head(grad, head)
        grad_probs = nt(values, grad_head)
        inner = jnp.sum(probs * grad_probs, axis=0, keepdims=True)
        grad_scores = (probs * (grad_probs - inner)).astype(jnp.bfloat16)
        grad_values.append(nn(low, grad_head))
        grad_keys.append(nn(grad_scores, one_head(query, head)))
        grad_query.append(tn(keys, grad_scores))
    dq[...] = heads_joined(*grad_query).astype(jnp.bfloat16).reshape(dq.shape)
    result = jnp.concatenate(
        [grad_keys[0] + grad_keys[1], grad_values[0] + grad_values[1]], axis=1
    ).astype(jnp.bfloat16)
    half = dkv_own.shape[0]
    dkv_own[...] = result[:half]
    dkv_far[...] = result[half:]


MIB = 1024 * 1024


def cost(flops, moved, exps=0):
    return pl.CostEstimate(
        flops=int(flops), bytes_accessed=int(moved), transcendentals=int(exps)
    )


SMALL_VMEM = 12 * MIB
ATTEND_VMEM = 24 * MIB
FFN_VMEM = 44 * MIB
SETTLE_VMEM = 48 * MIB
MESH = pl.DeviceIdType.MESH
SMEM_SPEC = pl.BlockSpec(memory_space=pltpu.SMEM)


def self_forward(info, rows, bias, examples):
    _, count, width = rows.shape
    pairs, size = width // 384, count // examples
    return pl.pallas_call(
        self_forward_kernel,
        grid=(pairs, examples),
        in_specs=[
            SMEM_SPEC,
            pl.BlockSpec((2, size, 384), lambda h, e: (0, e, h)),
            pl.BlockSpec((1, 2, 2 * size), lambda h, e: (h, 0, 0)),
        ],
        out_specs=pl.BlockSpec((2, size, 128), lambda h, e: (0, e, h)),
        out_shape=jax.ShapeDtypeStruct((2, count, pairs * 128), jnp.bfloat16),
        scratch_shapes=[
            pltpu.VMEM((2 * size, 384), jnp.bfloat16),
            pltpu.VMEM((2 * size, 128), jnp.bfloat16),
            pltpu.VMEM((2, 2 * size, 2 * size), jnp.float32),
        ],
        cost_estimate=cost(2 * 2 * examples * 2 * pairs * (2 * size) ** 2 * 256 * 8, 8 * rows.size, examples * 2 * pairs * (2 * size) ** 2),
        compiler_params=pltpu.CompilerParams(vmem_limit_bytes=SMALL_VMEM),
    )(info, rows, bias)


def self_backward(info, rows, bias, grads, examples):
    _, count, width = rows.shape
    pairs, size = width // 384, count // examples
    row = pl.BlockSpec((1, 2, 2 * size), lambda h, e: (h, 0, 0))
    wide = pl.BlockSpec((2, size, 384), lambda h, e: (0, e, h))
    return pl.pallas_call(
        self_backward_kernel,
        grid=(pairs, examples),
        in_specs=[
            SMEM_SPEC,
            wide,
            row,
            pl.BlockSpec((2, size, 128), lambda h, e: (0, e, h)),
        ],
        out_specs=[wide, row],
        out_shape=[
            jax.ShapeDtypeStruct(rows.shape, jnp.bfloat16),
            jax.ShapeDtypeStruct((pairs, 2, 2 * size), jnp.float32),
        ],
        scratch_shapes=[
            pltpu.VMEM((2 * size, 384), jnp.bfloat16),
            pltpu.VMEM((2 * size, 128), jnp.bfloat16),
            pltpu.VMEM((2 * size, 384), jnp.bfloat16),
            pltpu.VMEM((2, 2 * size, 2 * size), jnp.float32),
            pltpu.VMEM((2, 2 * size, 2 * size), jnp.float32),
        ],
        cost_estimate=cost(5 * 2 * examples * 2 * pairs * (2 * size) ** 2 * 256 * 8, 12 * rows.size, examples * 2 * pairs * (2 * size) ** 2),
        compiler_params=pltpu.CompilerParams(vmem_limit_bytes=SMALL_VMEM),
    )(info, rows, bias, grads)


def cross_forward(info, queries, kv_own, kv_far, examples):
    _, count, width = queries.shape
    pairs, size, span = width // 128, count // examples, kv_own.shape[0] // examples
    thin = pl.BlockSpec((2, size, 128), lambda e, h: (0, e, h))
    wide = pl.BlockSpec((span, 256), lambda e, h: (e, h))
    return pl.pallas_call(
        cross_forward_kernel,
        grid=(examples, pairs),
        in_specs=[SMEM_SPEC, thin, wide, wide],
        out_specs=thin,
        out_shape=jax.ShapeDtypeStruct(queries.shape, jnp.bfloat16),
        cost_estimate=cost(2 * 2 * examples * 2 * pairs * 4 * size * span * 256 * 4, 8 * kv_own.size, examples * 2 * pairs * 4 * size * span),
        compiler_params=pltpu.CompilerParams(vmem_limit_bytes=ATTEND_VMEM),
    )(info, queries, kv_own, kv_far)


def cross_backward(info, queries, kv_own, kv_far, grads, examples):
    _, count, width = queries.shape
    pairs, size, span = width // 128, count // examples, kv_own.shape[0] // examples
    thin = pl.BlockSpec((2, size, 128), lambda e, h: (0, e, h))
    wide = pl.BlockSpec((span, 256), lambda e, h: (e, h))
    return pl.pallas_call(
        cross_backward_kernel,
        grid=(examples, pairs),
        in_specs=[SMEM_SPEC, thin, wide, wide, thin],
        out_specs=[thin, wide, wide],
        out_shape=[jax.ShapeDtypeStruct(queries.shape, jnp.bfloat16)]
        + [jax.ShapeDtypeStruct(kv_own.shape, jnp.bfloat16)] * 2,
        cost_estimate=cost(5 * 2 * examples * 2 * pairs * 4 * size * span * 256 * 2, 12 * kv_own.size, examples * 2 * pairs * 4 * size * span),
        compiler_params=pltpu.CompilerParams(vmem_limit_bytes=ATTEND_VMEM),
    )(info, queries, kv_own, kv_far, grads)


root = math.sqrt(2.0 / math.pi)
cubic = 0.044715


def ffn_kernel(
    n_own,
    n_far,
    g_own,
    g_far,
    into,
    outof,
    out_own,
    out_far,
    dn_own,
    dn_far,
    outof_grad,
    into_grad,
    turned,
    out_sum,
    dn_sum,
):
    step = pl.program_id(0)
    half = n_own.shape[0]

    @pl.when(step == 0)
    def _():
        turned[:, :half] = n_own[...].T
        turned[:, half:] = n_far[...].T
        out_own[...] = jnp.zeros_like(out_own)
        dn_own[...] = jnp.zeros_like(dn_own)
        out_sum[...] = jnp.zeros_like(out_sum)
        dn_sum[...] = jnp.zeros_like(dn_sum)

    grads, backs = [], []
    for normed, grad, out, back in (
        (n_own, g_own, out_own, dn_own),
        (n_far, g_far, out_sum, dn_sum),
    ):
        pre = nn(normed[...], into[...])
        grad_hidden = nt(grad[...], outof[...])
        bend = jnp.tanh(root * (pre + cubic * (pre * pre * pre)))
        hidden = (0.5 * pre * (1.0 + bend)).astype(jnp.bfloat16)
        slope = 0.5 * (1.0 + bend) + 0.5 * pre * (1.0 - bend * bend) * (
            root * (1.0 + 3.0 * cubic * (pre * pre))
        )
        grad_pre = (grad_hidden * slope).astype(jnp.bfloat16)
        out[...] += nn(hidden, outof[...])
        back[...] += nt(grad_pre, into[...])
        grads.append(tn(hidden, grad[...]))
        backs.append(nn(turned[:, : half] if normed is n_own else turned[:, half:], grad_pre))
    outof_grad[...] = (grads[0] + grads[1]).astype(jnp.bfloat16)
    into_grad[...] = (backs[0] + backs[1]).astype(jnp.bfloat16)

    @pl.when(step == pl.num_programs(0) - 1)
    def _():
        out_far[...] = out_sum[...].astype(jnp.bfloat16)
        dn_far[...] = dn_sum[...].astype(jnp.bfloat16)


def ffn(n_own, n_far, g_own, g_far, into, outof):
    rows, width = n_own.shape
    units = into.shape[1]
    tile = 256
    whole = pl.BlockSpec((rows, width), lambda i: (0, 0))
    tall = pl.BlockSpec((width, tile), lambda i: (0, i))
    flat = pl.BlockSpec((tile, width), lambda i: (i, 0))
    wide = jax.ShapeDtypeStruct((rows, width), jnp.float32)
    thin = jax.ShapeDtypeStruct((rows, width), jnp.bfloat16)
    return pl.pallas_call(
        ffn_kernel,
        grid=(units // tile,),
        in_specs=[whole, whole, whole, whole, tall, flat],
        out_specs=[whole, whole, whole, whole, flat, tall],
        out_shape=[
            wide,
            thin,
            wide,
            thin,
            jax.ShapeDtypeStruct(outof.shape, jnp.bfloat16),
            jax.ShapeDtypeStruct(into.shape, jnp.bfloat16),
        ],
        scratch_shapes=[
            pltpu.VMEM((width, 2 * rows), jnp.bfloat16),
            pltpu.VMEM((rows, width), jnp.float32),
            pltpu.VMEM((rows, width), jnp.float32),
        ],
        cost_estimate=cost(6 * 2 * 2 * rows * width * units, 24 * rows * width + 8 * width * units, 2 * rows * units),
        compiler_params=pltpu.CompilerParams(vmem_limit_bytes=FFN_VMEM),
    )(n_own, n_far, g_own, g_far, into, outof)


def assemble_kernel(count, moves, info, *refs):
    held, pair, far, targets = refs[:count], refs[count], refs[count + 1], refs[count + 2 :]
    part = pl.program_id(0) ^ info[0]

    @pl.when(info[1] == 1)
    def _():
        for source, column, _, _, target, at, columns in moves:
            targets[target][:, at : at + columns] = held[source][:, column : column + columns]

    def write(ref):
        for _, _, row, start, target, at, columns in moves:
            rows = targets[target].shape[0]
            targets[target][:, at : at + columns] = ref[
                0, row : row + rows, start : start + columns
            ]

    @pl.when((info[1] == 0) & ((part & 1) == 0))
    def _():
        write(pair)

    @pl.when((info[1] == 0) & ((part & 1) == 1))
    def _():
        write(far)


def bring(weights, pack, shapes, moves, place, net):
    mine = place["x"] * 2 + place["zl"]
    quarters = [
        lax.dynamic_slice_in_dim(w, mine * (w.shape[0] // 4), w.shape[0] // 4, 0)
        for w in weights
    ]
    first = permute(pack(*quarters)[None], net["turn"])
    pair = jnp.concatenate([first, permute(first, net["off_x"])], axis=0)
    far = permute(pair, net["off_zl"])
    info = jnp.stack([mine, place["settled"][0]])
    block = (1,) + first.shape[1:]

    def at(i, s):
        return ((i ^ s[0]) >> 1, 0, 0)

    return pl.pallas_call(
        functools.partial(assemble_kernel, len(weights), moves),
        grid_spec=pltpu.PrefetchScalarGridSpec(
            num_scalar_prefetch=1,
            grid=(4,),
            in_specs=[
                pl.BlockSpec((w.shape[0] // 4, w.shape[1]), lambda i, s: (i * s[1], 0))
                for w in weights
            ]
            + [pl.BlockSpec(block, at)] * 2,
            out_specs=[
                pl.BlockSpec((shape[0] // 4, shape[1]), lambda i, s: (i, 0)) for shape in shapes
            ],
        ),
        out_shape=[jax.ShapeDtypeStruct(shape, jnp.bfloat16) for shape in shapes],
        cost_estimate=cost(0, 4 * sum(w.size for w in weights)),
        compiler_params=pltpu.CompilerParams(vmem_limit_bytes=ATTEND_VMEM),
    )(info, *weights, pair, far)


def add_low(left, right):
    return (left.astype(jnp.float32) + right.astype(jnp.float32)).astype(jnp.bfloat16)


def pick(value, index):
    return lax.dynamic_index_in_dim(value, index, 0, keepdims=False)


def halve(total, name, place, net):
    view = total.reshape(2, total.shape[0] // 2, *total.shape[1:])
    sent = permute(pick(view, 1 - place[name]), net[name])
    return add_low(pick(view, place[name]), sent)


def spread_back(total, order, net):
    for name in reversed(order):
        total = jnp.concatenate([total, permute(total, net[name])], axis=0)
    return total, permute(total, net["core"])


def reduce_units(value, order, place, net):
    total = halve(value, "core", place, net)
    for name in order:
        total = halve(total, name, place, net)
    return spread_back(total, order, net)


def settle_kernel(groups, value, out, first, second, third, send, receive):
    index, y = lax.axis_index("dp"), lax.axis_index("mp")
    core, x, z = index % 2, (index // 2) % 2, index // 4
    deep = groups // 4
    chunks, rows = first.shape[0], first.shape[3]

    def at(c, yy, xx, zz):
        return (zz * 4 + xx * 2 + c, yy)

    def part(k):
        return pl.ds(pl.multiple_of(k * rows, rows), rows)

    partners = [at(1 - core, y, x, z), at(core, 1 - y, x, z), at(1 - core, 1 - y, x, z)]
    partners.append(at(core, y, 1 - x, z))
    for step in range(1, deep):
        partners.append(at(core, y, x, (z + step) % deep))
    barrier = pltpu.get_barrier_semaphore()
    for partner in partners:
        pl.semaphore_signal(barrier, inc=1, device_id=partner, device_id_type=MESH)
    pl.semaphore_wait(barrier, len(partners))

    def copy(source, target, slot, k, device):
        return pltpu.make_async_remote_copy(
            src_ref=source,
            dst_ref=target,
            send_sem=send.at[k, slot],
            recv_sem=receive.at[k, slot],
            device_id=device,
            device_id_type=MESH,
        )

    def quarter(k, q):
        return value.at[pl.ds(q * 8, 8), part(k)]

    def to_core(k):
        return copy(quarter(k, 1 - core), first.at[k, 0], 0, k, at(1 - core, core, x, z))

    def to_turned(k):
        return copy(quarter(k, 1 - core), first.at[k, 1], 1, k, at(1 - core, core, x, z))

    def to_same(k):
        return copy(quarter(k, core), first.at[k, 1], 2, k, at(core, core, x, z))

    def arrived(k, slot):
        return copy(quarter(k, core), first.at[k, 1 if slot else 0], slot, k, at(1 - core, y, x, z))

    def along_x(k):
        return copy(
            first.at[k, 1, pl.ds((1 - x) * 4, 4)], second.at[k], 3, k, at(core, y, 1 - x, z)
        )

    def along_z(k, step):
        far = (z + step) % deep
        return copy(
            second.at[k, far], third.at[k, step - 1], 3 + step, k, at(core, y, x, far)
        )

    def back_z(k, step):
        far = (z + step) % deep
        piece = core * 8 + x * 4 + z
        return copy(
            out.at[piece, part(k)], out.at[piece, part(k)], 6 + step, k, at(core, y, x, far)
        )

    def back_x(k):
        held = out.at[pl.ds(core * 8 + x * 4, 4), part(k)]
        return copy(held, held, 10, k, at(core, y, 1 - x, z))

    def back_core(k):
        held = out.at[pl.ds(core * 8, 8), part(k)]
        return copy(held, held, 11, k, at(1 - core, y, x, z))

    def start(k, carry):
        @pl.when(core == y)
        def _():
            to_core(k).start()

        @pl.when(core != y)
        def _():
            to_same(k).start()
            to_turned(k).start()

        return carry

    lax.fori_loop(0, chunks, start, 0)

    def total(left, right):
        return (left.astype(jnp.float32) + right.astype(jnp.float32)).astype(jnp.bfloat16)

    def tick(t, carry):
        @pl.when(t < chunks)
        def _():
            k = jnp.minimum(t, chunks - 1)

            @pl.when(core == y)
            def _():
                arrived(k, 2).wait_recv()

                def add(i, c):
                    first[k, 1, i] = total(value[core * 8 + i, part(k)], first[k, 1, i])
                    return c

                lax.fori_loop(0, 8, add, 0)

            @pl.when(core != y)
            def _():
                arrived(k, 0).wait_recv()
                arrived(k, 1).wait_recv()

                def add(i, c):
                    first[k, 1, i] = total(first[k, 0, i], first[k, 1, i])
                    return c

                lax.fori_loop(0, 8, add, 0)

            along_x(k).start()

        @pl.when((t >= 1) & (t < chunks + 1))
        def _():
            k = t - 1
            along_x(k).wait_recv()

            def add(i, c):
                second[k, i] = total(first[k, 1, x * 4 + i], second[k, i])
                return c

            lax.fori_loop(0, deep, add, 0)
            for step in range(1, deep):
                along_z(k, step).start()

        @pl.when((t >= 2) & (t < chunks + 2))
        def _():
            k = t - 2
            for step in range(1, deep):
                along_z(k, step).wait_recv()
            summed = second[k, z].astype(jnp.float32)
            for step in range(1, deep):
                summed = summed + third[k, step - 1].astype(jnp.float32)
            out[core * 8 + x * 4 + z, part(k)] = summed.astype(jnp.bfloat16)
            for step in range(1, deep):
                back_z(k, step).start()

        @pl.when((t >= 3) & (t < chunks + 3))
        def _():
            k = t - 3
            for step in range(1, deep):
                back_z(k, step).wait_recv()
            back_x(k).start()

        @pl.when((t >= 4) & (t < chunks + 4))
        def _():
            k = t - 4
            back_x(k).wait_recv()
            back_core(k).start()

        @pl.when(t >= 5)
        def _():
            back_core(t - 5).wait_recv()

        return carry

    lax.fori_loop(0, chunks + 5, tick, 0)

    def finish_sends(k, carry):
        @pl.when(core == y)
        def _():
            to_core(k).wait_send()

        @pl.when(core != y)
        def _():
            to_same(k).wait_send()
            to_turned(k).wait_send()

        along_x(k).wait_send()
        for step in range(1, deep):
            along_z(k, step).wait_send()
            back_z(k, step).wait_send()
        back_x(k).wait_send()
        back_core(k).wait_send()
        return carry

    lax.fori_loop(0, chunks, finish_sends, 0)


def settle(value, groups):
    count, rows, width = value.shape
    chunk = 32
    chunks = rows // chunk
    deep = groups // 4
    whole = pl.BlockSpec(memory_space=pltpu.VMEM)
    return pl.pallas_call(
        functools.partial(settle_kernel, groups),
        in_specs=[whole],
        out_specs=whole,
        out_shape=jax.ShapeDtypeStruct(value.shape, value.dtype),
        scratch_shapes=[
            pltpu.VMEM((chunks, 2, count // 2, chunk, width), value.dtype),
            pltpu.VMEM((chunks, deep, chunk, width), value.dtype),
            pltpu.VMEM((chunks, deep - 1, chunk, width), value.dtype),
            pltpu.SemaphoreType.DMA((chunks, 12)),
            pltpu.SemaphoreType.DMA((chunks, 12)),
        ],
        cost_estimate=cost(0, 60 * value.size),
        compiler_params=pltpu.CompilerParams(
            collective_id=0, has_side_effects=True, vmem_limit_bytes=SETTLE_VMEM
        ),
    )(value)


def unpack_kernel(pairs, source, key, val, cross_out, self_out, cross_q, *self_in):
    wide = key.shape[0] // 4
    thin = cross_out.shape[0] // 4

    def taken(row, rows):
        block = source[:, row : row + rows, :].astype(jnp.float32)
        return block.reshape(4 * rows, block.shape[2])

    kv = taken(0, wide)
    for i in range(pairs):
        key[:, 128 * i : 128 * i + 128] = kv[:, 256 * i : 256 * i + 128]
        val[:, 128 * i : 128 * i + 128] = kv[:, 256 * i + 128 : 256 * i + 256]
    cross_out[...] = taken(wide, thin)
    self_out[...] = taken(wide + thin, thin)
    cross_q[...] = taken(wide + 2 * thin, thin).T
    rest = taken(wide + 3 * thin, 3 * thin)
    for i in range(3):
        self_in[i][...] = rest[4 * thin * i : 4 * thin * (i + 1)].T


def unpack(value, inner):
    count, rows, width = value.shape
    tall = jax.ShapeDtypeStruct((width, inner), jnp.float32)
    flat = jax.ShapeDtypeStruct((inner, width), jnp.float32)
    by_row = pl.BlockSpec((width // 4, inner), lambda i: (i, 0))
    by_out = pl.BlockSpec((inner // 4, width), lambda i: (i, 0))
    by_column = pl.BlockSpec((width, inner // 4), lambda i: (0, i))
    return pl.pallas_call(
        functools.partial(unpack_kernel, inner // 128),
        grid=(4,),
        in_specs=[pl.BlockSpec((4, rows, width), lambda i: (i, 0, 0))],
        out_specs=[by_row, by_row, by_out, by_out] + [by_column] * 4,
        out_shape=[tall, tall, flat, flat] + [tall] * 4,
        cost_estimate=cost(0, 6 * value.size),
        compiler_params=pltpu.CompilerParams(vmem_limit_bytes=ATTEND_VMEM),
    )(value)


def finish_kernel(layout, info, own, other, *targets):
    mine = (pl.program_id(0) >> 3) == info[1]

    def write(source):
        for target, moves in zip(targets, layout):
            for row, rows, column, columns, at in moves:
                target[:, at : at + columns] = source[
                    0, row : row + rows, column : column + columns
                ].astype(jnp.float32)

    @pl.when(mine)
    def _():
        write(own)

    @pl.when(jnp.logical_not(mine))
    def _():
        write(other)


def finish(done, order, place, shapes, layout):
    own, other = done
    count, rows, width = own.shape
    mine = place[order[0]] * 4 + place[order[1]] * 2 + place[order[2]]
    info = jnp.stack([mine, place["core"]])

    def at(held):
        def index(i, s):
            used = ((i >> 3) == s[1]) == held
            return (jnp.where(used, (i & 7) ^ s[0], s[0]), 0, 0)

        return index

    return pl.pallas_call(
        functools.partial(finish_kernel, layout),
        grid_spec=pltpu.PrefetchScalarGridSpec(
            num_scalar_prefetch=1,
            grid=(2 * count,),
            in_specs=[
                pl.BlockSpec((1, rows, width), at(True)),
                pl.BlockSpec((1, rows, width), at(False)),
            ],
            out_specs=[
                pl.BlockSpec((shape[0] // (2 * count), shape[1]), lambda i, s: (i, 0))
                for shape in shapes
            ],
        ),
        out_shape=[jax.ShapeDtypeStruct(shape, jnp.float32) for shape in shapes],
        cost_estimate=cost(0, 4 * own.size * 6),
        compiler_params=pltpu.CompilerParams(vmem_limit_bytes=ATTEND_VMEM),
    )(info, own, other)


def pieces(*values):
    split = [v.reshape(16, v.shape[0] // 16, v.shape[1]) for v in values]
    return split[0] if len(split) == 1 else jnp.concatenate(split, axis=1)


def low(value):
    return value.astype(jnp.bfloat16)


def on_chip_group(
    tokens,
    memory,
    cotangent,
    target_lengths,
    memory_lengths,
    norm_self,
    query_self,
    key_self,
    value_self,
    out_self,
    bias_table,
    norm_cross,
    query_cross,
    key_cross,
    value_cross,
    out_cross,
    norm_ffn,
    ffn_in,
    ffn_out,
):
    examples = target_lengths.shape[0]
    groups = lax.axis_size("dp")
    net = links(groups)
    index = lax.axis_index("dp")
    place = {
        "y": lax.axis_index("mp"),
        "core": index & 1,
        "x": (index >> 1) & 1,
        "zl": (index >> 2) & 1,
        "zh": (index >> 3) & 1,
    }
    core = place["core"]
    settled = (core == place["y"]).astype(jnp.int32)
    place["settled"] = settled[None]
    rows, width = tokens.shape
    half_pos = rows // examples
    inner = query_self.shape[1]
    pairs = inner // 128

    def swap(value):
        return permute(value, net["core"])

    def both(value):
        return jnp.stack([value, swap(value)])

    def flat(value):
        return value.reshape(-1, value.shape[2])

    def turn(value):
        return permute(value, net["turn"])

    tok_raw = turn(tokens)
    qkv_moves = [
        (i, 128 * h, 0, inner * i + 128 * h, 0, 384 * h + 128 * i, 128)
        for h in range(pairs)
        for i in range(3)
    ]
    self_in, cross_q = bring(
        [query_self, key_self, value_self, query_cross],
        lambda *w: jnp.concatenate(w, axis=1),
        [(width, 3 * inner), (width, inner)],
        qkv_moves + [(3, 0, 0, 3 * inner, 1, 0, inner)],
        place,
        net,
    )
    kv_moves = [
        (i, 128 * h, 0, inner * i + 128 * h, 0, 256 * h + 128 * i, 128)
        for h in range(pairs)
        for i in range(2)
    ]
    quarter, thin = width // 4, inner // 4
    cross_kv, self_out, cross_out = bring(
        [key_cross, value_cross, out_self, out_cross],
        lambda k, v, a, b: jnp.concatenate([jnp.concatenate([k, v], axis=1), a, b], axis=0),
        [(width, 2 * inner), (inner, width), (inner, width)],
        kv_moves + [(2, 0, quarter, 0, 1, 0, width), (3, 0, quarter + thin, 0, 2, 0, width)],
        place,
        net,
    )
    mem_raw = turn(memory)
    cot_raw = turn(cotangent)
    facts = jnp.concatenate(
        [
            target_lengths.astype(jnp.float32),
            memory_lengths.astype(jnp.float32),
            bias_table.astype(jnp.float32).reshape(-1),
        ]
    )
    facts = jnp.where(settled == 1, facts, turn(facts))
    target_len = facts[:examples].astype(jnp.int32)
    memory_len = facts[examples : 2 * examples].astype(jnp.int32)
    table = facts[2 * examples :].reshape(bias_table.shape)
    group_count = jnp.sum(target_len).astype(jnp.float32)
    total_count = group_count.reshape(1, 1)
    for name in ("y", "x", "zl", "zh"):
        total_count = total_count + permute(total_count, net[name])
    token_scale = groups * group_count / total_count[0, 0]
    self_info = jnp.concatenate([core[None], target_len])
    cross_info = jnp.concatenate([core[None], memory_len])
    tok = reorder(False, tokens, tok_raw, place["settled"], examples)

    span = 2 * half_pos
    distance = jnp.arange(span, dtype=jnp.int32)
    level = jnp.sum(
        (distance[:, None] >= jnp.asarray(bucket_edges())[None, :]).astype(jnp.int32), axis=-1
    )
    level_hot = (level[:, None] == jnp.arange(BUCKETS, dtype=jnp.int32)[None, :]).astype(
        jnp.float32
    )
    bias = jnp.einsum("db,bh->hd", level_hot, table, precision=highest).reshape(-1, 2, span)

    tok_float = tok.astype(jnp.float32)
    n1 = both(low(rms_norm(tok_float, norm_self.astype(jnp.float32))))
    qkv = low(nn(flat(n1), self_in)).reshape(2, rows, -1)
    a1 = self_forward(self_info, qkv, bias, examples)
    r1 = tok_float + (nn(a1[0], self_out) + swap(nn(a1[1], self_out)))

    mem = reorder(False, memory, mem_raw, place["settled"], examples)
    mem_far = swap(mem)
    kv, kv_far = low(nn(mem, cross_kv)), low(nn(mem_far, cross_kv))
    n2 = both(low(rms_norm(r1, norm_cross.astype(jnp.float32))))
    q2 = low(nn(flat(n2), cross_q)).reshape(2, rows, -1)
    a2 = cross_forward(cross_info, q2, kv, kv_far, examples)
    r2 = r1 + (nn(a2[0], cross_out) + swap(nn(a2[1], cross_out)))

    cot = reorder(False, cotangent, cot_raw, place["settled"], examples)
    positions = core * half_pos + jnp.arange(half_pos, dtype=jnp.int32)
    live = (positions[None, :] < target_len[:, None]).astype(jnp.float32).reshape(rows, 1)
    dy = cot.astype(jnp.float32) * live * token_scale
    gy = low(dy)
    gy_far = permute(gy, net["y"])

    n3 = low(rms_norm(r2, norm_ffn.astype(jnp.float32)))
    n3_far = permute(n3, net["y"])
    out_own, out_far, dn_own, dn_far, ffn_out_part, ffn_in_part = ffn(
        n3, n3_far, gy, gy_far, ffn_in, ffn_out
    )
    dn3 = dn_own + permute(dn_far, net["y"]).astype(jnp.float32)
    back, gain_three = norm_backward(r2, norm_ffn, dn3)
    dr2 = dy + back
    block_out = low(r2 + (out_own + permute(out_far, net["y"]).astype(jnp.float32)))
    block_out = reorder(True, block_out, turn(block_out), place["settled"], examples)
    x_first, z_first = ("x", "zl", "zh"), ("zl", "zh", "x")
    ffn_out_done = reduce_units(pieces(ffn_out_part), x_first, place, net)
    ffn_in_done = reduce_units(pieces(ffn_in_part), z_first, place, net)

    g2 = both(low(dr2))
    da2 = low(nt(flat(g2), cross_out)).reshape(2, rows, -1)
    dq2, dkv, dkv_far = cross_backward(cross_info, q2, kv, kv_far, da2, examples)
    dn2 = nt(dq2[0], cross_q) + swap(nt(dq2[1], cross_q))
    back, gain_two = norm_backward(r1, norm_cross, dn2)
    dr1 = dr2 + back
    cross_out_part = low(tn(flat(a2), flat(g2)))
    cross_q_part = low(tn(flat(dq2), flat(n2)))
    cross_kv_part = low(tn(mem, dkv) + tn(mem_far, dkv_far))
    memory_grad = low(
        nt(dkv, cross_kv) + swap(low(nt(dkv_far, cross_kv))).astype(jnp.float32)
    )
    memory_grad = reorder(True, memory_grad, turn(memory_grad), place["settled"], examples)

    g1 = both(low(dr1))
    self_out_part = low(tn(flat(a1), flat(g1)))
    da1 = low(nt(flat(g1), self_out)).reshape(2, rows, -1)
    dqkv, by_distance = self_backward(self_info, qkv, bias, da1, examples)
    self_in_part = low(tn(flat(dqkv), flat(n1)))
    heads_done = settle(
        pieces(cross_kv_part, cross_out_part, self_out_part, cross_q_part, self_in_part), groups
    )
    dn1 = nt(dqkv[0], self_in) + swap(nt(dqkv[1], self_in))
    back, gain_one = norm_backward(tok_float, norm_self, dn1)
    tokens_grad = low(dr1 + back)
    tokens_grad = reorder(True, tokens_grad, turn(tokens_grad), place["settled"], examples)

    bias_part = jnp.einsum(
        "hd,db->bh", by_distance.reshape(-1, span), level_hot, precision=highest
    )
    bias_row = jnp.pad(bias_part.reshape(1, -1), ((0, 0), (0, width - bias_part.size)))
    small = jnp.concatenate(
        [gain_one[None], gain_two[None], gain_three[None], bias_row], axis=0
    )
    for name in ("y", "x", "zl", "zh"):
        small = small + permute(small, net[name])
    small_far = swap(small)
    gains = small[:3] + small_far[:3]
    bias_sum = jnp.where(settled == 1, small[3], small_far[3])
    bias_grad = bias_sum[: bias_part.size].reshape(bias_part.shape)

    (ffn_out_grad,) = finish(
        ffn_out_done,
        x_first,
        place,
        [ffn_out.shape],
        [[(0, ffn_out.shape[0] // 16, 0, width, 0)]],
    )
    (ffn_in_grad,) = finish(
        ffn_in_done,
        z_first,
        place,
        [ffn_in.shape],
        [[(0, width // 16, 0, ffn_in.shape[1], 0)]],
    )
    (
        key_cross_grad,
        value_cross_grad,
        out_cross_grad,
        out_self_grad,
        query_cross_grad,
        query_self_grad,
        key_self_grad,
        value_self_grad,
    ) = unpack(heads_done, inner)
    return (
        block_out,
        tokens_grad,
        memory_grad,
        gains[0],
        query_self_grad,
        key_self_grad,
        value_self_grad,
        out_self_grad,
        bias_grad,
        gains[1],
        query_cross_grad,
        key_cross_grad,
        value_cross_grad,
        out_cross_grad,
        gains[2],
        ffn_in_grad,
        ffn_out_grad,
    )


def solution(mesh):
    placed = (
        P(("dp", "mp"), None),
        P(("dp", "mp"), None),
        P(("dp", "mp"), None),
        P("dp"),
        P("dp"),
        P(),
        P(None, "mp"),
        P(None, "mp"),
        P(None, "mp"),
        P("mp", None),
        P(None, "mp"),
        P(),
        P(None, "mp"),
        P(None, "mp"),
        P(None, "mp"),
        P("mp", None),
        P(),
        P(None, "mp"),
        P("mp", None),
    )
    near = mesh.shape["mp"] == 2 and mesh.shape["dp"] == 16
    return jax.shard_map(
        on_chip_group if near else on_device,
        mesh=mesh,
        in_specs=placed,
        out_specs=(
            P(("dp", "mp"), None),
            P(("dp", "mp"), None),
            P(("dp", "mp"), None),
            P(),
            P(None, "mp"),
            P(None, "mp"),
            P(None, "mp"),
            P("mp", None),
            P(None, "mp"),
            P(),
            P(None, "mp"),
            P(None, "mp"),
            P(None, "mp"),
            P("mp", None),
            P(),
            P(None, "mp"),
            P("mp", None),
        ),
        check_vma=False,
    )
```

profile of v0, /device:TPU:6, one launch (start us, length us, event | category | flops | bytes accessed | tf_op | source)
XLA Modules:
  0.0 796.3 jit_solution(2501939779079623449)
XLA Ops:
  11.0 8.4 %collective-permute-done.6 = bf16[1,512,1024]{2,1,0:T(8,128)(2,1)} collective-permute-done((bf16[1,512,1024]{2,1,0:T(8,128)(2,1)S(1)}, bf16[1,512,1024]{2,1,0:T(8,128)(2,1)}, u32[]{:S(2)}, u32[]{:S(2)}) %collective-permute-start.6) | collective-permute-done | bytes 1048608 | tf_op jit(solution)/shard_map/ppermute | solution.py:313
  21.8 8.8 %collective-permute-done.3 = bf16[1,256,2048]{2,1,0:T(8,128)(2,1)} collective-permute-done((bf16[1,256,2048]{2,1,0:T(8,128)(2,1)S(1)}, bf16[1,256,2048]{2,1,0:T(8,128)(2,1)}, u32[]{:S(2)}, u32[]{:S(2)}) %collective-permute-start.3) | collective-permute-done | bytes 1048608 | tf_op jit(solution)/shard_map/ppermute | solution.py:313
  63.3 11.6 %collective-permute-done.8.refs_5_ = bf16[2,512,1024]{2,1,0:T(8,128)(2,1)} collective-permute-done((bf16[2,512,1024]{2,1,0:T(8,128)(2,1)}, bf16[2,512,1024]{2,1,0:T(8,128)(2,1)}, u32[]{:S(2)}, u32[]{:S(2)}) %collective-permute-start.8) | collective-permute-done | bytes 2097184 | tf_op jit(solution)/shard_map/ppermute | solution.py:313
  79.1 18.3 %collective-permute-done.5.refs_5_ = bf16[2,256,2048]{2,1,0:T(8,128)(2,1)} collective-permute-done((bf16[2,256,2048]{2,1,0:T(8,128)(2,1)S(1)}, bf16[2,256,2048]{2,1,0:T(8,128)(2,1)}, u32[]{:S(2)}, u32[]{:S(2)}) %collective-permute-start.5) | collective-permute-done | bytes 2097184 | tf_op jit(solution)/shard_map/ppermute | solution.py:313
  104.7 16.2 %shard_map.325 = bf16[2,512,512]{2,1,0:T(8,128)(2,1)S(1)} custom-call(s32[5]{0:T(128)S(1)} %pad_add_fusion.info, bf16[2,512,1536]{2,1,0:T(8,128)(2,1)S(1)} %bitcast.206, f32[4,2,256]{2,1,0:T(2,128)S(1)} %fusion.38.bias), custom_call_target="tpu_custom_call" | custom-call | flops 17179869184 | bytes 12582912 | tf_op jit(solution)/shard_map/pallas_call | solution.py:590
  121.8 6.1 shard_map.327
  129.9 4.7 convolution_convert_fusion.3.kv_own
  138.9 4.7 convolution_convert_fusion.2.kv_far
  143.7 33.0 %shard_map.328 = bf16[2,512,512]{2,1,0:T(8,128)(2,1)S(1)} custom-call(s32[5]{0:T(128)S(1)} %pad_add_fusion.2.info, bf16[2,512,512]{2,1,0:T(8,128)(2,1)S(1)} %bitcast.208, bf16[2048,1024]{1,0:T(8,128)(2,1)S(1)} %convolution_convert_fusion.3.kv_own, bf16[2048,1024]{1,0:T(8,128)(2,1)S(1)} %convolution_convert_fusion.2.kv_far), custom_call_target="tpu_custom_call" | custom-call | flops 34359738368 | bytes 16777216 | tf_op jit(solution)/shard_map/pallas_call | solution.py:646
  182.8 11.0 %collective-permute-start.16 = (f32[1,1]{1,0:T(1,128)}, f32[1,1]{1,0:T(1,128)}, u32[]{:S(2)}, u32[]{:S(2)}) collective-permute-start(f32[1,1]{1,0:T(1,128)} %bitcast.25), channel_id=1, source_target_pairs={{0,1},{1,0},{2,3},{3,2},{4,5},{5,4},{6,7},{7,6},{8,9},{9,8},{10,11... | collective-permute-start | bytes 20 | tf_op jit(solution)/shard_map/ppermute | solution.py:313
  215.8 21.2 %collective-permute-done.20.g_far = bf16[512,1024]{1,0:T(8,128)(2,1)S(1)} collective-permute-done((bf16[512,1024]{1,0:T(8,128)(2,1)S(1)}, bf16[512,1024]{1,0:T(8,128)(2,1)S(1)}, u32[]{:S(2)}, u32[]{:S(2)}) %collective-permute-start.20) | collective-permute-done | bytes 1048608 | tf_op jit(solution)/shard_map/ppermute | solution.py:313
  237.1 18.5 %collective-permute-done.14.n_far = bf16[512,1024]{1,0:T(8,128)(2,1)S(1)} collective-permute-done((bf16[512,1024]{1,0:T(8,128)(2,1)S(1)}, bf16[512,1024]{1,0:T(8,128)(2,1)S(1)}, u32[]{:S(2)}, u32[]{:S(2)}) %collective-permute-start.14) | collective-permute-done | bytes 1048608 | tf_op jit(solution)/shard_map/ppermute | solution.py:313
  255.6 36.4 %shard_map.330 = (f32[512,1024]{1,0:T(8,128)S(1)}, bf16[512,1024]{1,0:T(8,128)(2,1)S(1)}, f32[512,1024]{1,0:T(8,128)}, bf16[512,1024]{1,0:T(8,128)(2,1)S(1)}, bf...) custom-call(bf16[512,1024]{1,0:T(8,128)(2,1)S(1)} %multiply_convert_fusion.n_own, ...), custom_call_target="tpu_custom_call" | custom-call | flops 25769803776 | bytes 29360128 | tf_op jit(solution)/shard_map/pallas_call | solution.py:742
  294.0 24.1 %collective-permute-done.23 = bf16[512,1024]{1,0:T(8,128)(2,1)S(1)} collective-permute-done((bf16[512,1024]{1,0:T(8,128)(2,1)S(1)}, bf16[512,1024]{1,0:T(8,128)(2,1)S(1)}, u32[]{:S(2)}, u32[]{:S(2)}) %collective-permute-start.23) | collective-permute-done | bytes 1048608 | tf_op jit(solution)/shard_map/ppermute | solution.py:313
  321.0 14.6 %collective-permute-done.21 = bf16[512,1024]{1,0:T(8,128)(2,1)S(1)} collective-permute-done((bf16[512,1024]{1,0:T(8,128)(2,1)S(1)}, bf16[512,1024]{1,0:T(8,128)(2,1)S(1)}, u32[]{:S(2)}, u32[]{:S(2)}) %collective-permute-start.21) | collective-permute-done | bytes 1048608 | tf_op jit(solution)/shard_map/ppermute | solution.py:313
  350.7 41.7 %shard_map.332 = (bf16[2,512,512]{2,1,0:T(8,128)(2,1)S(1)}, bf16[2048,1024]{1,0:T(8,128)(2,1)S(1)}, bf16[2048,1024]{1,0:T(8,128)(2,1)S(1)}) custom-call(s32[5]{0:T(128)S(1)} %pad_add_fusion.2.info, bf16[2,512,512]{2,1,0:T(8,128)(2,1)S(1)} %bitcast.209, bf16[2048,1024]{1,0:T(8,128)(2,1)S(1)} %copy-done.45, bf16[2048,1024]{1,0:T(8,128)(2,1)S(1)} %copy-done.47, ...), custom_call_target="tpu_custom_call" | custom-call | flops 42949672960 | bytes 25165824 | tf_op jit(solution)/shard_map/pallas_call | solution.py:662
  399.3 8.4 %fusion.52 = f32[1024,1024]{1,0:T(8,128)} fusion(bf16[2048,1024]{1,0:T(8,128)(2,1)} %copy-done.98, bf16[2048,1024]{1,0:T(8,128)(2,1)S(1)} %get-tuple-element.53), kind=kOutput, calls=%fused_computation.157 | convolution fusion | flops 4294967296 | bytes 12582912 | tf_op jit(solution)/shard_map/dot_general | solution.py:384
  407.7 6.5 add_convert_fusion.1
  414.3 6.4 convolution_convert_fusion.1
  430.2 17.1 %collective-permute-done.46 = bf16[2,128,1024]{2,1,0:T(8,128)(2,1)S(1)} collective-permute-done((bf16[2,128,1024]{2,1,0:T(8,128)(2,1)S(1)}, bf16[2,128,1024]{2,1,0:T(8,128)(2,1)S(1)}, u32[]{:S(2)}, u32[]{:S(2)}) %collective-permute-start.46) | collective-permute-done | bytes 524320 | tf_op jit(solution)/shard_map/ppermute | solution.py:313
  447.6 9.7 %collective-permute-done.38 = bf16[2,64,2048]{2,1,0:T(8,128)(2,1)S(1)} collective-permute-done((bf16[2,64,2048]{2,1,0:T(8,128)(2,1)S(1)}, bf16[2,64,2048]{2,1,0:T(8,128)(2,1)S(1)}, u32[]{:S(2)}, u32[]{:S(2)}) %collective-permute-start.38) | collective-permute-done | bytes 524320 | tf_op jit(solution)/shard_map/ppermute | solution.py:313
  469.1 7.4 collective-permute-done.48
  483.9 16.2 %collective-permute-done.49 = bf16[2,128,1024]{2,1,0:T(8,128)(2,1)S(1)} collective-permute-done((bf16[2,128,1024]{2,1,0:T(8,128)(2,1)S(1)}, bf16[2,128,1024]{2,1,0:T(8,128)(2,1)S(1)}, u32[]{:S(2)}, u32[]{:S(2)}) %collective-permute-start.49) | collective-permute-done | bytes 524320 | tf_op jit(solution)/shard_map/ppermute | solution.py:313
  507.5 23.4 %shard_map.333 = (bf16[2,512,1536]{2,1,0:T(8,128)(2,1)S(1)}, f32[4,2,256]{2,1,0:T(2,128)S(1)}) custom-call(s32[5]{0:T(128)S(1)} %copy-done.36, bf16[2,512,1536]{2,1,0:T(8,128)(2,1)S(1)} %bitcast.207, f32[4,2,256]{2,1,0:T(2,128)S(1)} %copy-done.38, bf16[2,512,512]{2,1,0:T(8,128)(2,1)S(1)} %bitcast.211), custom_call_target="tpu_custom_call" | custom-call | flops 42949672960 | bytes 18874368 | tf_op jit(solution)/shard_map/pallas_call | solution.py:615
  539.7 8.1 %add_convert_fusion = bf16[2048,1024]{1,0:T(8,128)(2,1)} fusion(bf16[2048,1024]{1,0:T(8,128)(2,1)} %collective-permute-done.29, bf16[2048,1024]{1,0:T(8,128)(2,1)S(1)} %copy-done.40, bf16[1024,1024]{1,0:T(8,128)(2,1)S(1)} %copy-done.30), kind=kOutput, calls=%fused_computation | convolution fusion | flops 4301258752 | bytes 14680064 | tf_op jit(solution)/shard_map/dot_general | solution.py:378
  551.4 5.4 bitcast_convert_fusion
  567.1 30.6 %collective-permute-done.31 = f32[4,1024]{1,0:T(4,128)S(1)} collective-permute-done((f32[4,1024]{1,0:T(4,128)S(1)}, f32[4,1024]{1,0:T(4,128)S(1)}, u32[]{:S(2)}, u32[]{:S(2)}) %collective-permute-start.31) | collective-permute-done | bytes 16416 | tf_op jit(solution)/shard_map/ppermute | solution.py:313
  613.9 139.1 %shard_map.336.source = bf16[16,256,1024]{2,1,0:T(8,128)(2,1)} custom-call(bf16[16,256,1024]{2,1,0:T(8,128)(2,1)} %copy-done.52), custom_call_target="tpu_custom_call" | custom-call | bytes 251658240 | tf_op jit(solution)/shard_map/pallas_call | solution.py:1042
  756.4 6.0 shard_map.337
  763.8 11.4 %shard_map.338 = f32[1024,2048]{1,0:T(8,128)} custom-call(s32[2]{0:T(128)S(1)} %get-tuple-element.121.info, bf16[8,64,2048]{2,1,0:T(8,128)(2,1)} %pad_maximum_fusion.4.own, bf16[8,64,2048]{2,1,0:T(8,128)(2,1)} %collective-permute-done.43.other), custom_call_target="tpu_custom_call" | custom-call | bytes 25165824 | tf_op jit(solution)/shard_map/pallas_call | solution.py:1131
  775.3 10.3 %shard_map.339 = f32[2048,1024]{1,0:T(8,128)} custom-call(s32[2]{0:T(128)S(1)} %get-tuple-element.122.info, bf16[8,128,1024]{2,1,0:T(8,128)(2,1)S(1)} %pad_maximum_fusion.5.own, bf16[8,128,1024]{2,1,0:T(8,128)(2,1)} %collective-permute-done.51.other), custom_call_target="tpu_custom_call" | custom-call | bytes 25165824 | tf_op jit(solution)/shard_map/pallas_call | solution.py:1131
  788.1 7.7 shard_map.335
  (416 shorter events, 197.3 us)
Async XLA Ops:
  19.3 25.1 %collective-permute-start.7 = (bf16[1,512,1024]{2,1,0:T(8,128)(2,1)}, bf16[1,512,1024]{2,1,0:T(8,128)(2,1)}, u32[]{:S(2)}, u32[]{:S(2)}) collective-permute-start(bf16[1,512,1024]{2,1,0:T(8,128)(2,1)} %collective-permute-done.6), channel_id=1, source_target_pairs={{1,5},{2,6},{5,1},{6,2},{9,13},{10,14},{13,9},{14,10},{17,21},{18,... | collective-permute-start | bytes 3145736 | tf_op jit(solution)/shard_map/ppermute | solution.py:313
  35.2 23.4 %collective-permute-start.1 = (f32[264]{0:T(512)S(1)}, f32[264]{0:T(512)S(1)}, u32[]{:S(2)}, u32[]{:S(2)}) collective-permute-start(f32[264]{0:T(512)S(1)} %pad_maximum_fusion.10), channel_id=1, source_target_pairs={{1,2},{2,1},{5,6},{6,5},{9,10},{10,9},{13,14},{14,13},{17,18},{18,... | collective-permute-start | bytes 3176 | tf_op jit(solution)/shard_map/ppermute | solution.py:313
  38.9 82.9 %collective-permute-start.11 = (bf16[2048,1024]{1,0:T(8,128)(2,1)}, bf16[2048,1024]{1,0:T(8,128)(2,1)}, u32[]{:S(2)}, u32[]{:S(2)}) collective-permute-start(bf16[2048,1024]{1,0:T(8,128)(2,1)} %held.4), channel_id=1, source_target_pairs={{1,2},{2,1},{5,6},{6,5},{9,10},{10,9},{13,14},{14,13},{17,18},{18,... | collective-permute-start | bytes 12582920 | tf_op jit(solution)/shard_map/ppermute | solution.py:313
  46.7 28.2 %collective-permute-start.8 = (bf16[2,512,1024]{2,1,0:T(8,128)(2,1)}, bf16[2,512,1024]{2,1,0:T(8,128)(2,1)}, u32[]{:S(2)}, u32[]{:S(2)}) collective-permute-start(bf16[2,512,1024]{2,1,0:T(8,128)(2,1)} %constant_dynamic-update-slice_fusion.2.refs_4_), channel_id=1, source_target_pairs={{1,9},{2,10},{5,13},{6,14},{9,1},{10,2},{13,5},{14,6},{17,25},{18,... | collective-permute-start | bytes 6291464 | tf_op jit(solution)/shard_map/ppermute | solution.py:313
  51.5 45.9 %collective-permute-start.5 = (bf16[2,256,2048]{2,1,0:T(8,128)(2,1)S(1)}, bf16[2,256,2048]{2,1,0:T(8,128)(2,1)}, u32[]{:S(2)}, u32[]{:S(2)}) collective-permute-start(bf16[2,256,2048]{2,1,0:T(8,128)(2,1)S(1)} %constant_dynamic-update-slice_fusion.refs_4_), channel_id=1, source_target_pairs={{1,9},{2,10},{5,13},{6,14},{9,1},{10,2},{13,5},{14,6},{17,25},{18,... | collective-permute-start | bytes 6291464 | tf_op jit(solution)/shard_map/ppermute | solution.py:313
  178.8 34.2 %collective-permute-start.13 = (f32[512,1024]{1,0:T(8,128)}, f32[512,1024]{1,0:T(8,128)}, u32[]{:S(2)}, u32[]{:S(2)}) collective-permute-start(f32[512,1024]{1,0:T(8,128)} %fusion.29), channel_id=1, source_target_pairs={{0,2},{1,3},{2,0},{3,1},{4,6},{5,7},{6,4},{7,5},{8,10},{9,11},{10,... | collective-permute-start | bytes 6291464 | tf_op jit(solution)/shard_map/ppermute | solution.py:313
  178.9 29.3 %collective-permute-start.15 = (bf16[512,1024]{1,0:T(8,128)(2,1)S(1)}, bf16[512,1024]{1,0:T(8,128)(2,1)}, u32[]{:S(2)}, u32[]{:S(2)}) collective-permute-start(bf16[512,1024]{1,0:T(8,128)(2,1)S(1)} %copy-done.24), channel_id=1, source_target_pairs={{1,2},{2,1},{5,6},{6,5},{9,10},{10,9},{13,14},{14,13},{17,18},{18,... | collective-permute-start | bytes 3145736 | tf_op jit(solution)/shard_map/ppermute | solution.py:313
  210.5 26.6 %collective-permute-start.20 = (bf16[512,1024]{1,0:T(8,128)(2,1)S(1)}, bf16[512,1024]{1,0:T(8,128)(2,1)S(1)}, u32[]{:S(2)}, u32[]{:S(2)}) collective-permute-start(bf16[512,1024]{1,0:T(8,128)(2,1)S(1)} %fusion.9.g_own), channel_id=1, source_target_pairs={{0,1},{1,0},{2,3},{3,2},{4,5},{5,4},{6,7},{7,6},{8,9},{9,8},{10,11... | collective-permute-start | bytes 3145736 | tf_op jit(solution)/shard_map/ppermute | solution.py:313
  215.8 39.8 %collective-permute-start.14 = (bf16[512,1024]{1,0:T(8,128)(2,1)S(1)}, bf16[512,1024]{1,0:T(8,128)(2,1)S(1)}, u32[]{:S(2)}, u32[]{:S(2)}) collective-permute-start(bf16[512,1024]{1,0:T(8,128)(2,1)S(1)} %multiply_convert_fusion.n_own), channel_id=1, source_target_pairs={{0,1},{1,0},{2,3},{3,2},{4,5},{5,4},{6,7},{7,6},{8,9},{9,8},{10,11... | collective-permute-start | bytes 3145736 | tf_op jit(solution)/shard_map/ppermute | solution.py:313
  291.9 26.1 %collective-permute-start.23 = (bf16[512,1024]{1,0:T(8,128)(2,1)S(1)}, bf16[512,1024]{1,0:T(8,128)(2,1)S(1)}, u32[]{:S(2)}, u32[]{:S(2)}) collective-permute-start(bf16[512,1024]{1,0:T(8,128)(2,1)S(1)} %get-tuple-element.49), channel_id=1, source_target_pairs={{0,1},{1,0},{2,3},{3,2},{4,5},{5,4},{6,7},{7,6},{8,9},{9,8},{10,11... | collective-permute-start | bytes 3145736 | tf_op jit(solution)/shard_map/ppermute | solution.py:313
  292.2 43.4 %collective-permute-start.21 = (bf16[512,1024]{1,0:T(8,128)(2,1)S(1)}, bf16[512,1024]{1,0:T(8,128)(2,1)S(1)}, u32[]{:S(2)}, u32[]{:S(2)}) collective-permute-start(bf16[512,1024]{1,0:T(8,128)(2,1)S(1)} %get-tuple-element.47), channel_id=1, source_target_pairs={{0,1},{1,0},{2,3},{3,2},{4,5},{5,4},{6,7},{7,6},{8,9},{9,8},{10,11... | collective-permute-start | bytes 3145736 | tf_op jit(solution)/shard_map/ppermute | solution.py:313
  340.4 52.0 %collective-permute-start.44 = (bf16[8,128,1024]{2,1,0:T(8,128)(2,1)S(1)}, bf16[8,128,1024]{2,1,0:T(8,128)(2,1)S(1)}, u32[]{:S(2)}, u32[]{:S(2)}) collective-permute-start(bf16[8,128,1024]{2,1,0:T(8,128)(2,1)S(1)} %dynamic-slice_bitcast_fusion), channel_id=1, source_target_pairs={{0,2},{1,3},{2,0},{3,1},{4,6},{5,7},{6,4},{7,5},{8,10},{9,11},{10,... | collective-permute-start | bytes 6291464 | tf_op jit(solution)/shard_map/ppermute | solution.py:313
  342.8 53.1 %collective-permute-start.36 = (bf16[8,64,2048]{2,1,0:T(8,128)(2,1)}, bf16[8,64,2048]{2,1,0:T(8,128)(2,1)S(1)}, u32[]{:S(2)}, u32[]{:S(2)}) collective-permute-start(bf16[8,64,2048]{2,1,0:T(8,128)(2,1)} %dynamic-slice_bitcast_fusion.1), channel_id=1, source_target_pairs={{0,2},{1,3},{2,0},{3,1},{4,6},{5,7},{6,4},{7,5},{8,10},{9,11},{10,... | collective-permute-start | bytes 6291464 | tf_op jit(solution)/shard_map/ppermute | solution.py:313
  343.3 135.3 %collective-permute-start.22 = (bf16[512,1024]{1,0:T(8,128)(2,1)S(1)}, bf16[512,1024]{1,0:T(8,128)(2,1)S(1)}, u32[]{:S(2)}, u32[]{:S(2)}) collective-permute-start(bf16[512,1024]{1,0:T(8,128)(2,1)S(1)} %get-tuple-element.109), channel_id=1, source_target_pairs={{1,2},{2,1},{5,6},{6,5},{9,10},{10,9},{13,14},{14,13},{17,18},{18,... | collective-permute-start | bytes 3145736 | tf_op jit(solution)/shard_map/ppermute | solution.py:313
  393.6 27.1 %collective-permute-start.45 = (bf16[4,128,1024]{2,1,0:T(8,128)(2,1)S(1)}, bf16[4,128,1024]{2,1,0:T(8,128)(2,1)}, u32[]{:S(2)}, u32[]{:S(2)}) collective-permute-start(bf16[4,128,1024]{2,1,0:T(8,128)(2,1)S(1)} %dynamic-slice_bitcast_fusion.2), channel_id=1, source_target_pairs={{0,4},{1,5},{2,6},{3,7},{4,0},{5,1},{6,2},{7,3},{8,12},{9,13},{10,... | collective-permute-start | bytes 3145736 | tf_op jit(solution)/shard_map/ppermute | solution.py:313
  397.7 25.2 %collective-permute-start.37 = (bf16[4,64,2048]{2,1,0:T(8,128)(2,1)}, bf16[4,64,2048]{2,1,0:T(8,128)(2,1)}, u32[]{:S(2)}, u32[]{:S(2)}) collective-permute-start(bf16[4,64,2048]{2,1,0:T(8,128)(2,1)} %dynamic-slice_bitcast_fusion.3), channel_id=1, source_target_pairs={{0,8},{1,9},{2,10},{3,11},{4,12},{5,13},{6,14},{7,15},{8,0},{9,1},... | collective-permute-start | bytes 3145736 | tf_op jit(solution)/shard_map/ppermute | solution.py:313
  399.3 66.8 %collective-permute-start.25 = (f32[512,1024]{1,0:T(8,128)S(1)}, f32[512,1024]{1,0:T(8,128)S(1)}, u32[]{:S(2)}, u32[]{:S(2)}) collective-permute-start(f32[512,1024]{1,0:T(8,128)S(1)} %fusion.31), channel_id=1, source_target_pairs={{0,2},{1,3},{2,0},{3,1},{4,6},{5,7},{6,4},{7,5},{8,10},{9,11},{10,... | collective-permute-start | bytes 6291464 | tf_op jit(solution)/shard_map/ppermute | solution.py:313
  422.4 24.9 %collective-permute-start.46 = (bf16[2,128,1024]{2,1,0:T(8,128)(2,1)S(1)}, bf16[2,128,1024]{2,1,0:T(8,128)(2,1)S(1)}, u32[]{:S(2)}, u32[]{:S(2)}) collective-permute-start(bf16[2,128,1024]{2,1,0:T(8,128)(2,1)S(1)} %dynamic-slice_bitcast_fusion.4), channel_id=1, source_target_pairs={{0,8},{1,9},{2,10},{3,11},{4,12},{5,13},{6,14},{7,15},{8,0},{9,1},... | collective-permute-start | bytes 1572872 | tf_op jit(solution)/shard_map/ppermute | solution.py:313
  424.7 32.6 %collective-permute-start.38 = (bf16[2,64,2048]{2,1,0:T(8,128)(2,1)S(1)}, bf16[2,64,2048]{2,1,0:T(8,128)(2,1)S(1)}, u32[]{:S(2)}, u32[]{:S(2)}) collective-permute-start(bf16[2,64,2048]{2,1,0:T(8,128)(2,1)S(1)} %dynamic-slice_bitcast_fusion.5), channel_id=1, source_target_pairs={{0,16},{1,17},{2,18},{3,19},{4,20},{5,21},{6,22},{7,23},{8,24},{9,... | collective-permute-start | bytes 1572872 | tf_op jit(solution)/shard_map/ppermute | solution.py:313
  430.1 109.5 %collective-permute-start.29 = (bf16[2048,1024]{1,0:T(8,128)(2,1)}, bf16[2048,1024]{1,0:T(8,128)(2,1)}, u32[]{:S(2)}, u32[]{:S(2)}) collective-permute-start(bf16[2048,1024]{1,0:T(8,128)(2,1)} %convolution_convert_fusion.1), channel_id=1, source_target_pairs={{0,2},{1,3},{2,0},{3,1},{4,6},{5,7},{6,4},{7,5},{8,10},{9,11},{10,... | collective-permute-start | bytes 12582920 | tf_op jit(solution)/shard_map/ppermute | solution.py:313
  469.1 34.9 %collective-permute-start.26 = (bf16[512,1024]{1,0:T(8,128)(2,1)S(1)}, bf16[512,1024]{1,0:T(8,128)(2,1)S(1)}, u32[]{:S(2)}, u32[]{:S(2)}) collective-permute-start(bf16[512,1024]{1,0:T(8,128)(2,1)S(1)} %get-tuple-element.105), channel_id=1, source_target_pairs={{0,2},{1,3},{2,0},{3,1},{4,6},{5,7},{6,4},{7,5},{8,10},{9,11},{10,... | collective-permute-start | bytes 3145736 | tf_op jit(solution)/shard_map/ppermute | solution.py:313
  476.5 23.6 %collective-permute-start.49 = (bf16[2,128,1024]{2,1,0:T(8,128)(2,1)S(1)}, bf16[2,128,1024]{2,1,0:T(8,128)(2,1)S(1)}, u32[]{:S(2)}, u32[]{:S(2)}) collective-permute-start(bf16[2,128,1024]{2,1,0:T(8,128)(2,1)S(1)} %pad_maximum_fusion.9), channel_id=1, source_target_pairs={{0,8},{1,9},{2,10},{3,11},{4,12},{5,13},{6,14},{7,15},{8,0},{9,1},... | collective-permute-start | bytes 1572872 | tf_op jit(solution)/shard_map/ppermute | solution.py:313
  476.7 26.1 %collective-permute-start.41 = (bf16[2,64,2048]{2,1,0:T(8,128)(2,1)S(1)}, bf16[2,64,2048]{2,1,0:T(8,128)(2,1)S(1)}, u32[]{:S(2)}, u32[]{:S(2)}) collective-permute-start(bf16[2,64,2048]{2,1,0:T(8,128)(2,1)S(1)} %pad_maximum_fusion.8), channel_id=1, source_target_pairs={{0,16},{1,17},{2,18},{3,19},{4,20},{5,21},{6,22},{7,23},{8,24},{9,... | collective-permute-start | bytes 1572872 | tf_op jit(solution)/shard_map/ppermute | solution.py:313
  501.3 55.6 %collective-permute-start.50 = (bf16[4,128,1024]{2,1,0:T(8,128)(2,1)}, bf16[4,128,1024]{2,1,0:T(8,128)(2,1)}, u32[]{:S(2)}, u32[]{:S(2)}) collective-permute-start(bf16[4,128,1024]{2,1,0:T(8,128)(2,1)} %pad_maximum_fusion.7), channel_id=1, source_target_pairs={{0,4},{1,5},{2,6},{3,7},{4,0},{5,1},{6,2},{7,3},{8,12},{9,13},{10,... | collective-permute-start | bytes 3145736 | tf_op jit(solution)/shard_map/ppermute | solution.py:313
  503.9 54.7 %collective-permute-start.42 = (bf16[4,64,2048]{2,1,0:T(8,128)(2,1)}, bf16[4,64,2048]{2,1,0:T(8,128)(2,1)}, u32[]{:S(2)}, u32[]{:S(2)}) collective-permute-start(bf16[4,64,2048]{2,1,0:T(8,128)(2,1)} %pad_maximum_fusion.6), channel_id=1, source_target_pairs={{0,8},{1,9},{2,10},{3,11},{4,12},{5,13},{6,14},{7,15},{8,0},{9,1},... | collective-permute-start | bytes 3145736 | tf_op jit(solution)/shard_map/ppermute | solution.py:313
  537.3 24.9 %collective-permute-start.27 = (f32[512,1024]{1,0:T(8,128)}, f32[512,1024]{1,0:T(8,128)}, u32[]{:S(2)}, u32[]{:S(2)}) collective-permute-start(f32[512,1024]{1,0:T(8,128)} %fusion.18), channel_id=1, source_target_pairs={{0,2},{1,3},{2,0},{3,1},{4,6},{5,7},{6,4},{7,5},{8,10},{9,11},{10,... | collective-permute-start | bytes 6291464 | tf_op jit(solution)/shard_map/ppermute | solution.py:313
  547.8 240.3 %collective-permute-start.30 = (bf16[2048,1024]{1,0:T(8,128)(2,1)}, bf16[2048,1024]{1,0:T(8,128)(2,1)}, u32[]{:S(2)}, u32[]{:S(2)}) collective-permute-start(bf16[2048,1024]{1,0:T(8,128)(2,1)} %add_convert_fusion), channel_id=1, source_target_pairs={{1,2},{2,1},{5,6},{6,5},{9,10},{10,9},{13,14},{14,13},{17,18},{18,... | collective-permute-start | bytes 12582920 | tf_op jit(solution)/shard_map/ppermute | solution.py:313
  558.5 216.8 %collective-permute-start.51 = (bf16[8,128,1024]{2,1,0:T(8,128)(2,1)S(1)}, bf16[8,128,1024]{2,1,0:T(8,128)(2,1)}, u32[]{:S(2)}, u32[]{:S(2)}) collective-permute-start(bf16[8,128,1024]{2,1,0:T(8,128)(2,1)S(1)} %pad_maximum_fusion.5.own), channel_id=1, source_target_pairs={{0,2},{1,3},{2,0},{3,1},{4,6},{5,7},{6,4},{7,5},{8,10},{9,11},{10,... | collective-permute-start | bytes 6291464 | tf_op jit(solution)/shard_map/ppermute | solution.py:313
  561.5 202.3 %collective-permute-start.43 = (bf16[8,64,2048]{2,1,0:T(8,128)(2,1)}, bf16[8,64,2048]{2,1,0:T(8,128)(2,1)}, u32[]{:S(2)}, u32[]{:S(2)}) collective-permute-start(bf16[8,64,2048]{2,1,0:T(8,128)(2,1)} %pad_maximum_fusion.4.own), channel_id=1, source_target_pairs={{0,2},{1,3},{2,0},{3,1},{4,6},{5,7},{6,4},{7,5},{8,10},{9,11},{10,... | collective-permute-start | bytes 6291464 | tf_op jit(solution)/shard_map/ppermute | solution.py:313
  566.4 31.3 %collective-permute-start.31 = (f32[4,1024]{1,0:T(4,128)S(1)}, f32[4,1024]{1,0:T(4,128)S(1)}, u32[]{:S(2)}, u32[]{:S(2)}) collective-permute-start(f32[4,1024]{1,0:T(4,128)S(1)} %select_maximum_fusion), channel_id=1, source_target_pairs={{0,1},{1,0},{2,3},{3,2},{4,5},{5,4},{6,7},{7,6},{8,9},{9,8},{10,11... | collective-permute-start | bytes 49160 | tf_op jit(solution)/shard_map/ppermute | solution.py:313
  599.4 186.1 %collective-permute-start.28 = (bf16[512,1024]{1,0:T(8,128)(2,1)S(1)}, bf16[512,1024]{1,0:T(8,128)(2,1)}, u32[]{:S(2)}, u32[]{:S(2)}) collective-permute-start(bf16[512,1024]{1,0:T(8,128)(2,1)S(1)} %fusion.5), channel_id=1, source_target_pairs={{1,2},{2,1},{5,6},{6,5},{9,10},{10,9},{13,14},{14,13},{17,18},{18,... | collective-permute-start | bytes 3145736 | tf_op jit(solution)/shard_map/ppermute | solution.py:313
  610.0 152.4 %collective-permute-start.35 = (f32[4,1024]{1,0:T(4,128)S(1)}, f32[4,1024]{1,0:T(4,128)S(1)}, u32[]{:S(2)}, u32[]{:S(2)}) collective-permute-start(f32[4,1024]{1,0:T(4,128)S(1)} %add.242), channel_id=1, source_target_pairs={{0,2},{1,3},{2,0},{3,1},{4,6},{5,7},{6,4},{7,5},{8,10},{9,11},{10,... | collective-permute-start | bytes 49160 | tf_op jit(solution)/shard_map/ppermute | solution.py:313
  (124 other events, 1664.8 us)
where the time goes:
time: 809 us; the launch traced here: 796 us
  Pallas kernels  347 us (43%)
  waiting for transfers between devices  221 us (27%)
  starting transfers between devices  81.3 us (10%)
  matrix products  76.1 us (9%)
  local copies, waits for them, and re-layouts  36 us (4%)
  other arithmetic  29.1 us (4%)
    ppermute x52, waiting for transfers between devices, permute(): return lax.ppermute(value, ('dp', 'mp'), pairs)  221 us
    pallas_call x1, Pallas kernels, settle(): pl.pallas_call(functools.partial(settle_kernel, groups), in_specs=[whole]...  139 us
    ppermute x52, starting transfers between devices, permute(): return lax.ppermute(value, ('dp', 'mp'), pairs)  81.3 us
    pallas_call x1, Pallas kernels, cross_backward(): pl.pallas_call(cross_backward_kernel, grid=(examples, pairs), in_specs=[S...  41.7 us
    pallas_call x1, Pallas kernels, ffn(): pl.pallas_call(ffn_kernel, grid=(units // tile,), in_specs=[whole, whole,...  36.4 us
    pallas_call x1, Pallas kernels, cross_forward(): pl.pallas_call(cross_forward_kernel, grid=(examples, pairs), in_specs=[SM...  33 us
    dot_general x8, matrix products, nt(): lax.dot_general(left, right, (((1,), (1,)), ((), ())), preferred_element_...  27.7 us
    dot_general x6, matrix products, tn(): lax.dot_general(left, right, (((0,), (0,)), ((), ())), preferred_element_...  27.6 us
  transfers between devices with their start and end apart: 52, of which 22 were waited for; matrix products, arithmetic and copies ran while one was open for 14% of the time, Pallas kernels for 34%

commit v1 on v0

--- a/solution.py
+++ b/solution.py
@@ -762,64 +762,188 @@
     )(n_own, n_far, g_own, g_far, into, outof)
 
 
-def assemble_kernel(count, moves, info, *refs):
-    held, pair, far, targets = refs[:count], refs[count], refs[count + 1], refs[count + 2 :]
-    part = pl.program_id(0) ^ info[0]
-
-    @pl.when(info[1] == 1)
+def gather_kernel(groups, examples, tokens, facts, counts, *refs):
+    weights, refs = refs[:8], refs[8:]
+    tok_out, facts_out, counts_out, self_in, cross_q, cross_kv, self_out, cross_out = refs[:8]
+    raw, landed, round_in, near_send, near_get, send, get = refs[8:]
+    index, y = lax.axis_index("dp"), lax.axis_index("mp")
+    core, x, z = index % 2, (index // 2) % 2, index // 4
+    deep = groups // 4
+
+    def at(c, yy, xx, zz):
+        return (zz * 4 + xx * 2 + c, yy)
+
+    z_near = z + 1 - 2 * (z % 2)
+    x_side, z_side = at(core, y, 1 - x, z), at(core, y, x, z_near)
+    turned = at(1 - core, 1 - y, x, z)
+    rounds = [at(1 - core, y, x, z), x_side, z_side]
+    step = 2
+    while step < deep:
+        rounds.append(at(core, y, x, z + step - 2 * step * ((z // step) % 2)))
+        step *= 2
+    barrier = pltpu.get_barrier_semaphore()
+    for partner in rounds:
+        pl.semaphore_signal(barrier, inc=1, device_id=partner, device_id_type=MESH)
+
+    @pl.when(core != y)
     def _():
-        for source, column, _, _, target, at, columns in moves:
-            targets[target][:, at : at + columns] = held[source][:, column : column + columns]
-
-    def write(ref):
-        for _, _, row, start, target, at, columns in moves:
-            rows = targets[target].shape[0]
-            targets[target][:, at : at + columns] = ref[
-                0, row : row + rows, start : start + columns
+        pl.semaphore_signal(barrier, inc=1, device_id=turned, device_id_type=MESH)
+        pl.semaphore_wait(barrier, len(rounds) + 1)
+
+    @pl.when(core == y)
+    def _():
+        pl.semaphore_wait(barrier, len(rounds))
+
+    homes = [raw.at[0], raw.at[1], raw.at[2], cross_q, raw.at[3], raw.at[4], self_out, cross_out]
+
+    def remote(source, target, sems, slot, device):
+        return pltpu.make_async_remote_copy(
+            src_ref=source,
+            dst_ref=target,
+            send_sem=sems[0].at[slot],
+            recv_sem=sems[1].at[slot],
+            device_id=device,
+            device_id_type=MESH,
+        )
+
+    mine = x * 2 + z % 2
+
+    def quarter(w, which, first=0, parts=1):
+        rows = homes[w].shape[0] // 4
+        size = rows // parts
+        return homes[w].at[pl.ds(pl.multiple_of(which * rows + first * size, size), size)]
+
+    def along_y(w):
+        rows = homes[w].shape[0] // 4
+        sent = mine * rows
+        return remote(
+            weights[w].at[pl.ds(pl.multiple_of(sent, rows), rows)],
+            quarter(w, mine),
+            (send, get),
+            w,
+            turned,
+        )
+
+    def direct(w, which):
+        piece = quarter(w, mine)
+        return remote(piece, piece, (send, get), 8 + 2 * w + which, (x_side, z_side)[which])
+
+    def passed(w, which):
+        other = mine + (2 - 4 * x if which == 0 else 1 - 2 * (z % 2))
+        piece = quarter(w, other, which, 2)
+        return remote(piece, piece, (send, get), 24 + 2 * w + which, (z_side, x_side)[which])
+
+    token_copy = remote(tokens, landed, (send, get), 40, turned)
+    facts_copy = remote(facts, facts_out, (send, get), 41, turned)
+
+    @pl.when(core != y)
+    def _():
+        facts_copy.start()
+        for w in range(8):
+            along_y(w).start()
+        token_copy.start()
+
+    @pl.when(core == y)
+    def _():
+        pltpu.make_async_copy(tokens, landed, near_get.at[0]).start()
+        pltpu.make_async_copy(facts, facts_out, near_get.at[1]).start()
+        for w in range(8):
+            pltpu.make_async_copy(weights[w], homes[w], near_get.at[2 + w]).start()
+
+    counts_out[...] = counts[...]
+    for i, partner in enumerate(rounds):
+        swap = remote(counts_out, round_in.at[i], (near_send, get), 42 + i, partner)
+        swap.start()
+        swap.wait()
+        counts_out[...] += round_in[i]
+
+    @pl.when(core == y)
+    def _():
+        pltpu.make_async_copy(tokens, landed, near_get.at[0]).wait()
+        pltpu.make_async_copy(facts, facts_out, near_get.at[1]).wait()
+        for w in range(8):
+            pltpu.make_async_copy(weights[w], homes[w], near_get.at[2 + w]).wait()
+
+    @pl.when(core != y)
+    def _():
+        facts_copy.wait()
+        for w in range(9):
+            if w < 8:
+                along_y(w).wait()
+                for which in range(2):
+                    direct(w, which).start()
+            if w > 0:
+                for which in range(2):
+                    direct(w - 1, which).wait()
+                for which in range(2):
+                    passed(w - 1, which).start()
+        token_copy.wait()
+
+    rows = landed.shape[0]
+    block = 256
+    chunk = block // examples
+    high = lax.broadcasted_iota(jnp.int32, (block, block), 0)
+    low = lax.broadcasted_iota(jnp.int32, (block, block), 1)
+    hot = (low == (high % chunk) * examples + high // chunk).astype(jnp.bfloat16)
+    for i in range(rows // block):
+        moved = nn(hot, landed[pl.ds(i * block, block), :]).astype(jnp.bfloat16)
+        tok_out[:, pl.ds(i * chunk, chunk), :] = moved.reshape(examples, chunk, moved.shape[1])
+
+    @pl.when(core != y)
+    def _():
+        for w in range(8):
+            for which in range(2):
+                passed(w, which).wait()
+
+    for h in range(raw.shape[2] // 128):
+        for i in range(3):
+            self_in[:, 384 * h + 128 * i : 384 * h + 128 * i + 128] = raw[
+                i, :, 128 * h : 128 * h + 128
             ]
-
-    @pl.when((info[1] == 0) & ((part & 1) == 0))
-    def _():
-        write(pair)
-
-    @pl.when((info[1] == 0) & ((part & 1) == 1))
-    def _():
-        write(far)
-
-
-def bring(weights, pack, shapes, moves, place, net):
-    mine = place["x"] * 2 + place["zl"]
-    quarters = [
-        lax.dynamic_slice_in_dim(w, mine * (w.shape[0] // 4), w.shape[0] // 4, 0)
-        for w in weights
-    ]
-    first = permute(pack(*quarters)[None], net["turn"])
-    pair = jnp.concatenate([first, permute(first, net["off_x"])], axis=0)
-    far = permute(pair, net["off_zl"])
-    info = jnp.stack([mine, place["settled"][0]])
-    block = (1,) + first.shape[1:]
-
-    def at(i, s):
-        return ((i ^ s[0]) >> 1, 0, 0)
+        for i in range(2):
+            cross_kv[:, 256 * h + 128 * i : 256 * h + 128 * i + 128] = raw[
+                3 + i, :, 128 * h : 128 * h + 128
+            ]
+
+
+def gather(tokens, facts, counts, weights, groups, examples):
+    rows, width = tokens.shape
+    inner = weights[0].shape[1]
+    rounds = 2 + (groups // 4).bit_length() - 1
+    anywhere = pl.BlockSpec(memory_space=pl.ANY)
+    whole = pl.BlockSpec(memory_space=pltpu.VMEM)
+
+    def half(*shape):
+        return jax.ShapeDtypeStruct(shape, jnp.bfloat16)
 
     return pl.pallas_call(
-        functools.partial(assemble_kernel, len(weights), moves),
-        grid_spec=pltpu.PrefetchScalarGridSpec(
-            num_scalar_prefetch=1,
-            grid=(4,),
-            in_specs=[
-                pl.BlockSpec((w.shape[0] // 4, w.shape[1]), lambda i, s: (i * s[1], 0))
-                for w in weights
-            ]
-            + [pl.BlockSpec(block, at)] * 2,
-            out_specs=[
-                pl.BlockSpec((shape[0] // 4, shape[1]), lambda i, s: (i, 0)) for shape in shapes
-            ],
+        functools.partial(gather_kernel, groups, examples),
+        in_specs=[anywhere, whole, whole] + [anywhere] * 8,
+        out_specs=[whole] * 8,
+        out_shape=[
+            half(examples, rows // examples, width),
+            jax.ShapeDtypeStruct(facts.shape, facts.dtype),
+            jax.ShapeDtypeStruct(counts.shape, counts.dtype),
+            half(width, 3 * inner),
+            half(width, inner),
+            half(width, 2 * inner),
+            half(inner, width),
+            half(inner, width),
+        ],
+        scratch_shapes=[
+            pltpu.VMEM((5, width, inner), jnp.bfloat16),
+            pltpu.VMEM((rows, width), jnp.bfloat16),
+            pltpu.VMEM((rounds,) + counts.shape, counts.dtype),
+            pltpu.SemaphoreType.DMA((42 + rounds,)),
+            pltpu.SemaphoreType.DMA((10,)),
+            pltpu.SemaphoreType.DMA((42,)),
+            pltpu.SemaphoreType.DMA((42 + rounds,)),
+        ],
+        cost_estimate=cost(0, 150 * MIB),
+        compiler_params=pltpu.CompilerParams(
+            collective_id=1, has_side_effects=True, vmem_limit_bytes=SETTLE_VMEM
         ),
-        out_shape=[jax.ShapeDtypeStruct(shape, jnp.bfloat16) for shape in shapes],
-        cost_estimate=cost(0, 4 * sum(w.size for w in weights)),
-        compiler_params=pltpu.CompilerParams(vmem_limit_bytes=ATTEND_VMEM),
-    )(info, *weights, pair, far)
+    )(tokens, facts, counts, *weights)
 
 
 def add_low(left, right):
@@ -830,26 +954,29 @@
     return lax.dynamic_index_in_dim(value, index, 0, keepdims=False)
 
 
+def part_out(total, name, place, net):
+    view = total.reshape(2, total.shape[0] // 2, *total.shape[1:])
+    return permute(pick(view, 1 - place[name]), net[name])
+
+
+def part_in(total, arrived, name, place):
+    view = total.reshape(2, total.shape[0] // 2, *total.shape[1:])
+    return add_low(pick(view, place[name]), arrived)
+
+
 def halve(total, name, place, net):
-    view = total.reshape(2, total.shape[0] // 2, *total.shape[1:])
-    sent = permute(pick(view, 1 - place[name]), net[name])
-    return add_low(pick(view, place[name]), sent)
-
-
-def spread_back(total, order, net):
-    for name in reversed(order):
-        total = jnp.concatenate([total, permute(total, net[name])], axis=0)
-    return total, permute(total, net["core"])
-
-
-def reduce_units(value, order, place, net):
-    total = halve(value, "core", place, net)
-    for name in order:
-        total = halve(total, name, place, net)
-    return spread_back(total, order, net)
-
-
-def settle_kernel(groups, value, out, first, second, third, send, receive):
+    return part_in(total, part_out(total, name, place, net), name, place)
+
+
+def beside(own, arrived):
+    return jnp.concatenate([own, arrived], axis=0)
+
+
+def tie(*values):
+    return lax.optimization_barrier(values)
+
+
+def settle_kernel(groups, value, small, out, small_out, first, second, third, small_in, send, receive, small_send, small_get):
     index, y = lax.axis_index("dp"), lax.axis_index("mp")
     core, x, z = index % 2, (index // 2) % 2, index // 4
     deep = groups // 4
@@ -921,6 +1048,32 @@
         held = out.at[pl.ds(core * 8, 8), part(k)]
         return copy(held, held, 11, k, at(1 - core, y, x, z))
 
+    rounds = [at(core, 1 - y, x, z), at(core, y, 1 - x, z)]
+    step = 1
+    while step < deep:
+        rounds.append(at(core, y, x, z + step - 2 * step * ((z // step) % 2)))
+        step *= 2
+    rounds.append(at(1 - core, y, x, z))
+    small_out[0] = small[...]
+
+    def small_round(i):
+        swap = pltpu.make_async_remote_copy(
+            src_ref=small_out.at[0],
+            dst_ref=small_in.at[i],
+            send_sem=small_send.at[i],
+            recv_sem=small_get.at[i],
+            device_id=rounds[i],
+            device_id_type=MESH,
+        )
+        swap.start()
+        swap.wait()
+        if i < len(rounds) - 1:
+            small_out[0] = small_out[0] + small_in[i]
+        else:
+            small_out[1] = small_in[i]
+
+    small_round(0)
+
     def start(k, carry):
         @pl.when(core == y)
         def _():
@@ -934,6 +1087,8 @@
         return carry
 
     lax.fori_loop(0, chunks, start, 0)
+    for i in range(1, len(rounds)):
+        small_round(i)
 
     def total(left, right):
         return (left.astype(jnp.float32) + right.astype(jnp.float32)).astype(jnp.bfloat16)
@@ -1033,29 +1188,36 @@
     lax.fori_loop(0, chunks, finish_sends, 0)
 
 
-def settle(value, groups):
+def settle(value, small, groups):
     count, rows, width = value.shape
     chunk = 32
     chunks = rows // chunk
     deep = groups // 4
+    rounds = 3 + deep.bit_length() - 1
     whole = pl.BlockSpec(memory_space=pltpu.VMEM)
     return pl.pallas_call(
         functools.partial(settle_kernel, groups),
-        in_specs=[whole],
-        out_specs=whole,
-        out_shape=jax.ShapeDtypeStruct(value.shape, value.dtype),
+        in_specs=[whole, whole],
+        out_specs=[whole, whole],
+        out_shape=[
+            jax.ShapeDtypeStruct(value.shape, value.dtype),
+            jax.ShapeDtypeStruct((2,) + small.shape, small.dtype),
+        ],
         scratch_shapes=[
             pltpu.VMEM((chunks, 2, count // 2, chunk, width), value.dtype),
             pltpu.VMEM((chunks, deep, chunk, width), value.dtype),
             pltpu.VMEM((chunks, deep - 1, chunk, width), value.dtype),
+            pltpu.VMEM((rounds,) + small.shape, small.dtype),
             pltpu.SemaphoreType.DMA((chunks, 12)),
             pltpu.SemaphoreType.DMA((chunks, 12)),
+            pltpu.SemaphoreType.DMA((rounds,)),
+            pltpu.SemaphoreType.DMA((rounds,)),
         ],
         cost_estimate=cost(0, 60 * value.size),
         compiler_params=pltpu.CompilerParams(
             collective_id=0, has_side_effects=True, vmem_limit_bytes=SETTLE_VMEM
         ),
-    )(value)
+    )(value, small)
 
 
 def unpack_kernel(pairs, source, key, val, cross_out, self_out, cross_q, *self_in):
@@ -1096,56 +1258,37 @@
     )(value)
 
 
-def finish_kernel(layout, info, own, other, *targets):
-    mine = (pl.program_id(0) >> 3) == info[1]
-
-    def write(source):
-        for target, moves in zip(targets, layout):
-            for row, rows, column, columns, at in moves:
-                target[:, at : at + columns] = source[
-                    0, row : row + rows, column : column + columns
-                ].astype(jnp.float32)
-
-    @pl.when(mine)
-    def _():
-        write(own)
-
-    @pl.when(jnp.logical_not(mine))
-    def _():
-        write(other)
-
-
-def finish(done, order, place, shapes, layout):
-    own, other = done
-    count, rows, width = own.shape
-    mine = place[order[0]] * 4 + place[order[1]] * 2 + place[order[2]]
+def finish_kernel(info, *refs):
+    target = refs[4]
+    rows = refs[0].shape[1]
+    which = 2 * ((pl.program_id(0) >> 1) ^ info[1]) + ((pl.program_id(0) & 1) ^ (info[0] >> 2))
+
+    for held in range(4):
+
+        @pl.when(which == held)
+        def _():
+            for i in range(4):
+                target[rows * i : rows * (i + 1), :] = refs[held][i ^ (info[0] & 3)].astype(
+                    jnp.float32
+                )
+
+
+def finish(done, order, place, shape):
+    count, rows, width = done[0].shape
+    mine = place[order[0]] * 4 + place[order[1]] * 2
     info = jnp.stack([mine, place["core"]])
-
-    def at(held):
-        def index(i, s):
-            used = ((i >> 3) == s[1]) == held
-            return (jnp.where(used, (i & 7) ^ s[0], s[0]), 0, 0)
-
-        return index
-
     return pl.pallas_call(
-        functools.partial(finish_kernel, layout),
+        finish_kernel,
         grid_spec=pltpu.PrefetchScalarGridSpec(
             num_scalar_prefetch=1,
-            grid=(2 * count,),
-            in_specs=[
-                pl.BlockSpec((1, rows, width), at(True)),
-                pl.BlockSpec((1, rows, width), at(False)),
-            ],
-            out_specs=[
-                pl.BlockSpec((shape[0] // (2 * count), shape[1]), lambda i, s: (i, 0))
-                for shape in shapes
-            ],
+            grid=(4,),
+            in_specs=[pl.BlockSpec((4, rows, width), lambda i, s: (0, 0, 0))] * 4,
+            out_specs=pl.BlockSpec((shape[0] // 4, shape[1]), lambda i, s: (i, 0)),
         ),
-        out_shape=[jax.ShapeDtypeStruct(shape, jnp.float32) for shape in shapes],
-        cost_estimate=cost(0, 4 * own.size * 6),
+        out_shape=jax.ShapeDtypeStruct(shape, jnp.float32),
+        cost_estimate=cost(0, 4 * done[0].size * 12),
         compiler_params=pltpu.CompilerParams(vmem_limit_bytes=ATTEND_VMEM),
-    )(info, own, other)
+    )(info, *done)
 
 
 def pieces(*values):
@@ -1209,55 +1352,31 @@
     def turn(value):
         return permute(value, net["turn"])
 
-    tok_raw = turn(tokens)
-    qkv_moves = [
-        (i, 128 * h, 0, inner * i + 128 * h, 0, 384 * h + 128 * i, 128)
-        for h in range(pairs)
-        for i in range(3)
-    ]
-    self_in, cross_q = bring(
-        [query_self, key_self, value_self, query_cross],
-        lambda *w: jnp.concatenate(w, axis=1),
-        [(width, 3 * inner), (width, inner)],
-        qkv_moves + [(3, 0, 0, 3 * inner, 1, 0, inner)],
-        place,
-        net,
-    )
-    kv_moves = [
-        (i, 128 * h, 0, inner * i + 128 * h, 0, 256 * h + 128 * i, 128)
-        for h in range(pairs)
-        for i in range(2)
-    ]
-    quarter, thin = width // 4, inner // 4
-    cross_kv, self_out, cross_out = bring(
-        [key_cross, value_cross, out_self, out_cross],
-        lambda k, v, a, b: jnp.concatenate([jnp.concatenate([k, v], axis=1), a, b], axis=0),
-        [(width, 2 * inner), (inner, width), (inner, width)],
-        kv_moves + [(2, 0, quarter, 0, 1, 0, width), (3, 0, quarter + thin, 0, 2, 0, width)],
-        place,
-        net,
-    )
-    mem_raw = turn(memory)
-    cot_raw = turn(cotangent)
+    lengths = jnp.concatenate([target_lengths, memory_lengths]).astype(jnp.float32)
+    table_rows = bias_table.astype(jnp.float32).reshape(-1, 128)
     facts = jnp.concatenate(
-        [
-            target_lengths.astype(jnp.float32),
-            memory_lengths.astype(jnp.float32),
-            bias_table.astype(jnp.float32).reshape(-1),
-        ]
-    )
-    facts = jnp.where(settled == 1, facts, turn(facts))
-    target_len = facts[:examples].astype(jnp.int32)
-    memory_len = facts[examples : 2 * examples].astype(jnp.int32)
-    table = facts[2 * examples :].reshape(bias_table.shape)
+        [jnp.pad(lengths, (0, 128 - lengths.size))[None], table_rows], axis=0
+    )
+    facts = jnp.pad(facts, ((0, 8 - facts.shape[0]), (0, 0)))
+    counts = jnp.broadcast_to(jnp.sum(target_lengths).astype(jnp.float32), (8, 128))
+    tok, facts, counts, self_in, cross_q, cross_kv, self_out, cross_out = gather(
+        tokens,
+        facts,
+        counts,
+        [query_self, key_self, value_self, query_cross, key_cross, value_cross, out_self, out_cross],
+        groups,
+        examples,
+    )
+    tok = tok.reshape(rows, width)
+    target_len = facts[0, :examples].astype(jnp.int32)
+    memory_len = facts[0, examples : 2 * examples].astype(jnp.int32)
+    table = facts[1 : 1 + table_rows.shape[0]].reshape(bias_table.shape)
     group_count = jnp.sum(target_len).astype(jnp.float32)
-    total_count = group_count.reshape(1, 1)
-    for name in ("y", "x", "zl", "zh"):
-        total_count = total_count + permute(total_count, net[name])
-    token_scale = groups * group_count / total_count[0, 0]
+    token_scale = groups * group_count / counts[0, 0]
     self_info = jnp.concatenate([core[None], target_len])
     cross_info = jnp.concatenate([core[None], memory_len])
-    tok = reorder(False, tokens, tok_raw, place["settled"], examples)
+    memory_after, tok = tie(memory, tok)
+    mem_raw = turn(memory_after)
 
     span = 2 * half_pos
     distance = jnp.arange(span, dtype=jnp.int32)
@@ -1272,6 +1391,8 @@
     tok_float = tok.astype(jnp.float32)
     n1 = both(low(rms_norm(tok_float, norm_self.astype(jnp.float32))))
     qkv = low(nn(flat(n1), self_in)).reshape(2, rows, -1)
+    cot_after, qkv = tie(cotangent, qkv)
+    cot_raw = turn(cot_after)
     a1 = self_forward(self_info, qkv, bias, examples)
     r1 = tok_float + (nn(a1[0], self_out) + swap(nn(a1[1], self_out)))
 
@@ -1280,85 +1401,100 @@
     kv, kv_far = low(nn(mem, cross_kv)), low(nn(mem_far, cross_kv))
     n2 = both(low(rms_norm(r1, norm_cross.astype(jnp.float32))))
     q2 = low(nn(flat(n2), cross_q)).reshape(2, rows, -1)
-    a2 = cross_forward(cross_info, q2, kv, kv_far, examples)
-    r2 = r1 + (nn(a2[0], cross_out) + swap(nn(a2[1], cross_out)))
 
     cot = reorder(False, cotangent, cot_raw, place["settled"], examples)
     positions = core * half_pos + jnp.arange(half_pos, dtype=jnp.int32)
     live = (positions[None, :] < target_len[:, None]).astype(jnp.float32).reshape(rows, 1)
     dy = cot.astype(jnp.float32) * live * token_scale
-    gy = low(dy)
+    gy, q2 = tie(low(dy), q2)
     gy_far = permute(gy, net["y"])
+
+    a2 = cross_forward(cross_info, q2, kv, kv_far, examples)
+    a2, gy_far = tie(a2, gy_far)
+    r2 = r1 + (nn(a2[0], cross_out) + swap(nn(a2[1], cross_out)))
 
     n3 = low(rms_norm(r2, norm_ffn.astype(jnp.float32)))
     n3_far = permute(n3, net["y"])
     out_own, out_far, dn_own, dn_far, ffn_out_part, ffn_in_part = ffn(
         n3, n3_far, gy, gy_far, ffn_in, ffn_out
     )
-    dn3 = dn_own + permute(dn_far, net["y"]).astype(jnp.float32)
+    dn_far = permute(dn_far, net["y"])
+    first = pieces(ffn_out_part)
+    second = pieces(ffn_in_part)
+    first, second = halve(first, "core", place, net), halve(second, "core", place, net)
+    first_in, second_in = part_out(first, "x", place, net), part_out(second, "zl", place, net)
+    dn3 = dn_own + dn_far.astype(jnp.float32)
     back, gain_three = norm_backward(r2, norm_ffn, dn3)
     dr2 = dy + back
-    block_out = low(r2 + (out_own + permute(out_far, net["y"]).astype(jnp.float32)))
-    block_out = reorder(True, block_out, turn(block_out), place["settled"], examples)
-    x_first, z_first = ("x", "zl", "zh"), ("zl", "zh", "x")
-    ffn_out_done = reduce_units(pieces(ffn_out_part), x_first, place, net)
-    ffn_in_done = reduce_units(pieces(ffn_in_part), z_first, place, net)
 
     g2 = both(low(dr2))
     da2 = low(nt(flat(g2), cross_out)).reshape(2, rows, -1)
+    out_far = permute(out_far, net["y"])
     dq2, dkv, dkv_far = cross_backward(cross_info, q2, kv, kv_far, da2, examples)
+    dq2, first_in, second_in, out_far = tie(dq2, first_in, second_in, out_far)
+    first = part_in(first, first_in, "x", place)
+    second = part_in(second, second_in, "zl", place)
+    first_in, second_in = part_out(first, "zl", place, net), part_out(second, "zh", place, net)
+    block_out = low(r2 + (out_own + out_far.astype(jnp.float32)))
+    block_back = turn(block_out)
+    memory_grad = low(
+        nt(dkv, cross_kv) + swap(low(nt(dkv_far, cross_kv))).astype(jnp.float32)
+    )
+    memory_back = turn(memory_grad)
     dn2 = nt(dq2[0], cross_q) + swap(nt(dq2[1], cross_q))
     back, gain_two = norm_backward(r1, norm_cross, dn2)
     dr1 = dr2 + back
+    cross_kv_part = low(tn(mem, dkv) + tn(mem_far, dkv_far))
     cross_out_part = low(tn(flat(a2), flat(g2)))
     cross_q_part = low(tn(flat(dq2), flat(n2)))
-    cross_kv_part = low(tn(mem, dkv) + tn(mem_far, dkv_far))
-    memory_grad = low(
-        nt(dkv, cross_kv) + swap(low(nt(dkv_far, cross_kv))).astype(jnp.float32)
-    )
-    memory_grad = reorder(True, memory_grad, turn(memory_grad), place["settled"], examples)
 
     g1 = both(low(dr1))
     self_out_part = low(tn(flat(a1), flat(g1)))
     da1 = low(nt(flat(g1), self_out)).reshape(2, rows, -1)
+    head_parts = pieces(cross_kv_part, cross_out_part, self_out_part, cross_q_part)
+    da1, first_in, second_in, head_parts, memory_grad = tie(
+        da1, first_in, second_in, head_parts, memory_grad
+    )
+    first = part_in(first, first_in, "zl", place)
+    second = part_in(second, second_in, "zh", place)
+    first_in, second_in = permute(first, net["zh"]), permute(second, net["x"])
     dqkv, by_distance = self_backward(self_info, qkv, bias, da1, examples)
+    dqkv, first_in, second_in = tie(dqkv, first_in, second_in)
+    first, second = add_low(first, first_in), add_low(second, second_in)
+    first_in, second_in = permute(first, net["zl"]), permute(second, net["zh"])
     self_in_part = low(tn(flat(dqkv), flat(n1)))
-    heads_done = settle(
-        pieces(cross_kv_part, cross_out_part, self_out_part, cross_q_part, self_in_part), groups
-    )
     dn1 = nt(dqkv[0], self_in) + swap(nt(dqkv[1], self_in))
     back, gain_one = norm_backward(tok_float, norm_self, dn1)
     tokens_grad = low(dr1 + back)
-    tokens_grad = reorder(True, tokens_grad, turn(tokens_grad), place["settled"], examples)
+    tokens_back = turn(tokens_grad)
 
     bias_part = jnp.einsum(
         "hd,db->bh", by_distance.reshape(-1, span), level_hot, precision=highest
     )
     bias_row = jnp.pad(bias_part.reshape(1, -1), ((0, 0), (0, width - bias_part.size)))
     small = jnp.concatenate(
-        [gain_one[None], gain_two[None], gain_three[None], bias_row], axis=0
-    )
-    for name in ("y", "x", "zl", "zh"):
-        small = small + permute(small, net[name])
-    small_far = swap(small)
-    gains = small[:3] + small_far[:3]
-    bias_sum = jnp.where(settled == 1, small[3], small_far[3])
+        [gain_one[None], gain_two[None], gain_three[None], bias_row, jnp.zeros((4, width))], axis=0
+    )
+    head_parts = jnp.concatenate([head_parts, pieces(self_in_part)], axis=1)
+    head_parts, small, first_in, second_in = tie(head_parts, small, first_in, second_in)
+    first, second = beside(first, first_in), beside(second, second_in)
+    first_in, second_in = permute(first, net["x"]), permute(second, net["zl"])
+    first_far, second_far = swap(first), swap(second)
+    heads_done, small = settle(head_parts, small, groups)
+    small, first_in, second_in, first_far, second_far = tie(
+        small, first_in, second_in, first_far, second_far
+    )
+    first = (first, first_in, first_far, swap(first_in))
+    second = (second, second_in, second_far, swap(second_in))
+    gains = small[0, :3] + small[1, :3]
+    bias_sum = jnp.where(settled == 1, small[0, 3], small[1, 3])
     bias_grad = bias_sum[: bias_part.size].reshape(bias_part.shape)
-
-    (ffn_out_grad,) = finish(
-        ffn_out_done,
-        x_first,
-        place,
-        [ffn_out.shape],
-        [[(0, ffn_out.shape[0] // 16, 0, width, 0)]],
-    )
-    (ffn_in_grad,) = finish(
-        ffn_in_done,
-        z_first,
-        place,
-        [ffn_in.shape],
-        [[(0, width // 16, 0, ffn_in.shape[1], 0)]],
-    )
+    block_out = reorder(True, block_out, block_back, place["settled"], examples)
+    tokens_grad = reorder(True, tokens_grad, tokens_back, place["settled"], examples)
+    memory_grad = reorder(True, memory_grad, memory_back, place["settled"], examples)
+
+    ffn_out_grad = finish(first, ("x", "zl"), place, ffn_out.shape)
+    ffn_in_grad = finish(second, ("zl", "zh"), place, ffn_in.shape)
     (
         key_cross_grad,
         value_cross_grad,

time: 809 us -> 706 us (0.87)
  waiting for transfers between devices: 221 us -> 113 us
  starting transfers between devices: 81.3 us -> 29.5 us
  Pallas kernels: 347 us -> 386 us
  other arithmetic: 29.1 us -> 53.5 us
  local copies, waits for them, and re-layouts: 36 us -> 24.3 us
  matrix products: 76.1 us -> 85.4 us
    ppermute x52 -> x35, waiting for transfers between devices: 221 us -> 113 us  [permute(): return lax.ppermute(value, ('dp', 'mp'), pairs)]
    ppermute x52 -> x35, starting transfers between devices: 81.3 us -> 29.5 us  [permute(): return lax.ppermute(value, ('dp', 'mp'), pairs)]
    pallas_call x5 -> x4, Pallas kernels: 169 us -> 208 us  [the longest x1 142 us: settle(): pl.pallas_call(functools.partial(settle_kernel, groups), in_specs=[whole,...]
    concatenate x8 -> x5, other arithmetic: 7 us -> 17.9 us  [the longest x1 8.26 us: on_chip_group(): head_parts = jnp.concatenate([head_parts, pieces(self_in_part)], axis=1)]
    unnamed x215 -> x149, local copies, waits for them, and re-layouts: 21.9 us -> 16.6 us
    pallas_call x6 -> x5, Pallas kernels: 21.6 us -> 21.3 us  [reorder(): pl.pallas_call(functools.partial(reorder_kernel, inverse, examples), grid...]
  transfers between devices with their start and end apart: 52 -> 35, of which waited for: 22 -> 12; matrix products, arithmetic and copies ran while one was open for 14% -> 20% of each run, Pallas kernels for 34% -> 42%
where the time goes in v1:
time: 706 us; the launch traced here: 696 us
  Pallas kernels  386 us (55%)
  waiting for transfers between devices  113 us (16%)
  matrix products  85.4 us (12%)
  other arithmetic  53.5 us (8%)
  starting transfers between devices  29.5 us (4%)
  local copies, waits for them, and re-layouts  24.3 us (3%)
    pallas_call x1, Pallas kernels, settle(): pl.pallas_call(functools.partial(settle_kernel, groups), in_specs=[whole,...  142 us
    ppermute x35, waiting for transfers between devices, permute(): return lax.ppermute(value, ('dp', 'mp'), pairs)  113 us
    pallas_call x1, Pallas kernels, gather(): pl.pallas_call(functools.partial(gather_kernel, groups, examples), in_spe...  53.9 us
    pallas_call x1, Pallas kernels, cross_backward(): pl.pallas_call(cross_backward_kernel, grid=(examples, pairs), in_specs=[S...  41.7 us
    pallas_call x1, Pallas kernels, ffn(): pl.pallas_call(ffn_kernel, grid=(units // tile,), in_specs=[whole, whole,...  37.4 us
    pallas_call x1, Pallas kernels, cross_forward(): pl.pallas_call(cross_forward_kernel, grid=(examples, pairs), in_specs=[SM...  32.6 us
    dot_general x8, matrix products, nt(): lax.dot_general(left, right, (((1,), (1,)), ((), ())), preferred_element_...  31 us
    ppermute x35, starting transfers between devices, permute(): return lax.ppermute(value, ('dp', 'mp'), pairs)  29.5 us
  transfers between devices with their start and end apart: 35, of which 12 were waited for; matrix products, arithmetic and copies ran while one was open for 20% of the time, Pallas kernels for 42%

profile of v1, /device:TPU:6, one launch (start us, length us, event | category | flops | bytes accessed | tf_op | source)
XLA Modules:
  0.0 696.2 jit_solution(7310558553311175017)
XLA Ops:
  6.1 53.9 %shard_map.323 = (bf16[4,128,1024]{2,1,0:T(8,128)(2,1)S(1)}, f32[8,128]{1,0:T(8,128)S(1)}, f32[8,128]{1,0:T(8,128)S(1)}, bf16[1024,1536]{1,0:T(8,128)(2,1)}, bf1...) custom-call(bf16[512,1024]{1,0:T(8,128)(2,1)S(1)} %copy-done.17, ...), custom_call_target="tpu_custom_call" | custom-call | bytes 157286400 | tf_op jit(solution)/shard_map/pallas_call | solution.py:919
  72.1 16.2 %shard_map.324 = bf16[2,512,512]{2,1,0:T(8,128)(2,1)S(1)} custom-call(s32[5]{0:T(128)S(1)} %pad_add_fusion.info, bf16[2,512,1536]{2,1,0:T(8,128)(2,1)S(1)} %bitcast.178, f32[4,2,256]{2,1,0:T(2,128)S(1)} %fusion.40.bias), custom_call_target="tpu_custom_call" | custom-call | flops 17179869184 | bytes 12582912 | tf_op jit(solution)/shard_map/pallas_call | solution.py:590
  92.6 20.6 %collective-permute-done.4.arrived = bf16[2048,1024]{1,0:T(8,128)(2,1)} collective-permute-done((bf16[2048,1024]{1,0:T(8,128)(2,1)}, bf16[2048,1024]{1,0:T(8,128)(2,1)}, u32[]{:S(2)}, u32[]{:S(2)}) %collective-permute-start.4) | collective-permute-done | bytes 4194336 | tf_op jit(solution)/shard_map/ppermute | solution.py:313
  113.2 7.6 %shard_map.326 = bf16[4,512,1024]{2,1,0:T(8,128)(2,1)} custom-call(s32[1]{0:T(128)} %bitcast.info, bf16[2048,1024]{1,0:T(8,128)(2,1)} %held.3, bf16[2048,1024]{1,0:T(8,128)(2,1)} %collective-permute-done.4.arrived), custom_call_target="tpu_custom_call" | custom-call | flops 1073741824 | bytes 8388608 | tf_op jit(solution)/shard_map/pallas_call | solution.py:363
  128.8 10.8 %collective-permute-done.2.arrived = bf16[512,1024]{1,0:T(8,128)(2,1)S(1)} collective-permute-done((bf16[512,1024]{1,0:T(8,128)(2,1)}, bf16[512,1024]{1,0:T(8,128)(2,1)S(1)}, u32[]{:S(2)}, u32[]{:S(2)}) %collective-permute-start.2) | collective-permute-done | bytes 1048608 | tf_op jit(solution)/shard_map/ppermute | solution.py:313
  144.0 7.0 %convolution_convert_fusion.3.kv_own = bf16[2048,1024]{1,0:T(8,128)(2,1)S(1)} fusion(bf16[2048,1024]{1,0:T(8,128)(2,1)} %bitcast.22, bf16[1024,1024]{1,0:T(8,128)(2,1)S(1)} %copy-done.70), kind=kOutput, calls=%fused_computation.17 | convolution fusion | flops 4297064448 | bytes 10485760 | tf_op jit(solution)/shard_map/dot_general | solution.py:390
  151.0 8.5 %convolution_convert_fusion.2.kv_far = bf16[2048,1024]{1,0:T(8,128)(2,1)S(1)} fusion(bf16[2048,1024]{1,0:T(8,128)(2,1)} %collective-permute-done.5, bf16[1024,1024]{1,0:T(8,128)(2,1)S(1)} %copy-done.70), kind=kOutput, calls=%fused_computation.16 | convolution fusion | flops 4297064448 | bytes 10485760 | tf_op jit(solution)/shard_map/dot_general | solution.py:390
  159.5 32.6 %shard_map.327 = bf16[2,512,512]{2,1,0:T(8,128)(2,1)S(1)} custom-call(s32[5]{0:T(128)S(1)} %pad_add_fusion.1.info, bf16[2,512,512]{2,1,0:T(8,128)(2,1)S(1)} %bitcast.180, bf16[2048,1024]{1,0:T(8,128)(2,1)S(1)} %convolution_convert_fusion.3.kv_own, bf16[2048,1024]{1,0:T(8,128)(2,1)S(1)} %convolution_convert_fusion.2.kv_far), custom_call_target="tpu_custom_call" | custom-call | flops 34359738368 | bytes 16777216 | tf_op jit(solution)/shard_map/pallas_call | solution.py:646
  193.0 4.1 collective-permute-done.7
  200.2 23.5 %collective-permute-done.8.n_far = bf16[512,1024]{1,0:T(8,128)(2,1)S(1)} collective-permute-done((bf16[512,1024]{1,0:T(8,128)(2,1)S(1)}, bf16[512,1024]{1,0:T(8,128)(2,1)S(1)}, u32[]{:S(2)}, u32[]{:S(2)}) %collective-permute-start.8) | collective-permute-done | bytes 1048608 | tf_op jit(solution)/shard_map/ppermute | solution.py:313
  223.6 37.4 %shard_map.328 = (f32[512,1024]{1,0:T(8,128)S(1)}, bf16[512,1024]{1,0:T(8,128)(2,1)S(1)}, f32[512,1024]{1,0:T(8,128)}, bf16[512,1024]{1,0:T(8,128)(2,1)}, bf16[2...) custom-call(bf16[512,1024]{1,0:T(8,128)(2,1)S(1)} %multiply_convert_fusion.n_own, ...), custom_call_target="tpu_custom_call" | custom-call | flops 25769803776 | bytes 29360128 | tf_op jit(solution)/shard_map/pallas_call | solution.py:742
  268.3 19.6 %collective-permute-done.9 = bf16[512,1024]{1,0:T(8,128)(2,1)} collective-permute-done((bf16[512,1024]{1,0:T(8,128)(2,1)}, bf16[512,1024]{1,0:T(8,128)(2,1)}, u32[]{:S(2)}, u32[]{:S(2)}) %collective-permute-start.9) | collective-permute-done | bytes 1048608 | tf_op jit(solution)/shard_map/ppermute | solution.py:313
  290.6 3.8 fusion.50
  306.2 41.7 %shard_map.329 = (bf16[2,512,512]{2,1,0:T(8,128)(2,1)S(1)}, bf16[2048,1024]{1,0:T(8,128)(2,1)S(1)}, bf16[2048,1024]{1,0:T(8,128)(2,1)S(1)}) custom-call(s32[5]{0:T(128)S(1)} %pad_add_fusion.1.info, bf16[2,512,512]{2,1,0:T(8,128)(2,1)S(1)} %bitcast.181, bf16[2048,1024]{1,0:T(8,128)(2,1)S(1)} %copy-done.29, bf16[2048,1024]{1,0:T(8,128)(2,1)S(1)} %copy-done.31, ...), custom_call_target="tpu_custom_call" | custom-call | flops 42949672960 | bytes 25165824 | tf_op jit(solution)/shard_map/pallas_call | solution.py:662
  350.6 6.2 convolution_convert_fusion.1
  359.7 14.8 %collective-permute-done.12 = bf16[4,128,1024]{2,1,0:T(8,128)(2,1)S(1)} collective-permute-done((bf16[4,128,1024]{2,1,0:T(8,128)(2,1)S(1)}, bf16[4,128,1024]{2,1,0:T(8,128)(2,1)S(1)}, u32[]{:S(2)}, u32[]{:S(2)}) %collective-permute-start.12) | collective-permute-done | bytes 1048608 | tf_op jit(solution)/shard_map/ppermute | solution.py:313
  375.3 8.3 %fusion.54 = f32[1024,1024]{1,0:T(8,128)} fusion(bf16[2048,1024]{1,0:T(8,128)(2,1)} %collective-permute-done.5, bf16[2048,1024]{1,0:T(8,128)(2,1)S(1)} %get-tuple-element.103), kind=kOutput, calls=%fused_computation.131 | convolution fusion | flops 4294967296 | bytes 12582912 | tf_op jit(solution)/shard_map/dot_general | solution.py:384
  383.6 8.0 %add_convert_fusion.1 = bf16[1024,1024]{1,0:T(8,128)(2,1)S(1)} fusion(f32[1024,1024]{1,0:T(8,128)} %fusion.54, bf16[2048,1024]{1,0:T(8,128)(2,1)} %bitcast.22, bf16[2048,1024]{1,0:T(8,128)(2,1)S(1)} %get-tuple-element.102), kind=kOutput, calls=%fused_computation.8 | convolution fusion | flops 4297064448 | bytes 14680064 | tf_op jit(solution)/shard_map/dot_general | solution.py:384
  403.7 7.8 %add_convert_fusion = bf16[2048,1024]{1,0:T(8,128)(2,1)} fusion(bf16[2048,1024]{1,0:T(8,128)(2,1)} %collective-permute-done.21, bf16[2048,1024]{1,0:T(8,128)(2,1)S(1)} %get-tuple-element.102, bf16[1024,1024]{1,0:T(8,128)(2,1)S(1)} %copy-done.72), kind=kOutput, calls=%fused_computation.1 | convolution fusion | flops 4301258752 | bytes 14680064 | tf_op jit(solution)/shard_map/dot_general | solution.py:378
  414.8 6.9 pad_maximum_fusion.1
  426.1 23.1 %shard_map.331 = (bf16[2,512,1536]{2,1,0:T(8,128)(2,1)S(1)}, f32[4,2,256]{2,1,0:T(2,128)S(1)}) custom-call(s32[5]{0:T(128)S(1)} %copy-done.24, bf16[2,512,1536]{2,1,0:T(8,128)(2,1)S(1)} %bitcast.179, f32[4,2,256]{2,1,0:T(2,128)S(1)} %copy-done.26, bf16[2,512,512]{2,1,0:T(8,128)(2,1)S(1)} %bitcast.182), custom_call_target="tpu_custom_call" | custom-call | flops 42949672960 | bytes 18874368 | tf_op jit(solution)/shard_map/pallas_call | solution.py:615
  449.3 6.1 fusion.16
  463.0 6.1 bitcast_convert_fusion
  469.1 8.3 %pad_maximum_fusion.value = bf16[16,256,1024]{2,1,0:T(8,128)(2,1)} fusion(bf16[16,96,1024]{2,1,0:T(8,128)(2,1)} %bitcast.198, bf16[16,160,1024]{2,1,0:T(8,128)(2,1)} %pad_maximum_fusion.1), kind=kLoop, calls=%fused_computation | loop fusion | flops 16777216 | bytes 16777216 | tf_op jit(solution)/shard_map/concatenate | solution.py:1478
  477.4 6.4 fusion.5
  488.4 4.0 add_convert_fusion.2
  498.8 15.0 %collective-permute-done.30.refs_1_ = bf16[4,64,2048]{2,1,0:T(8,128)(2,1)S(1)} collective-permute-done((bf16[4,64,2048]{2,1,0:T(8,128)(2,1)S(1)}, bf16[4,64,2048]{2,1,0:T(8,128)(2,1)S(1)}, u32[]{:S(2)}, u32[]{:S(2)}) %collective-permute-start.30) | collective-permute-done | bytes 1048608 | tf_op jit(solution)/shard_map/ppermute | solution.py:313
  517.2 142.5 %shard_map.334 = (bf16[16,256,1024]{2,1,0:T(8,128)(2,1)}, f32[2,8,1024]{2,1,0:T(8,128)S(1)}) custom-call(bf16[16,256,1024]{2,1,0:T(8,128)(2,1)} %pad_maximum_fusion.value, f32[8,1024]{1,0:T(8,128)S(1)} %concatenate.33.small), custom_call_target="tpu_custom_call" | custom-call | bytes 251658240 | tf_op jit(solution)/shard_map/pallas_call | solution.py:1198
  666.5 6.0 shard_map.335
  676.6 7.7 %shard_map.333 = bf16[2048,1024]{1,0:T(8,128)(2,1)} custom-call(s32[1]{0:T(128)} %bitcast.info, bf16[4,512,1024]{2,1,0:T(8,128)(2,1)} %bitcast.66.held, bf16[4,512,1024]{2,1,0:T(8,128)(2,1)} %bitcast.67.arrived), custom_call_target="tpu_custom_call" | custom-call | flops 1073741824 | bytes 8388608 | tf_op jit(solution)/shard_map/pallas_call | solution.py:363
  684.2 6.0 shard_map.337
  690.3 5.4 shard_map.336
  (298 shorter events, 115.7 us)
Async XLA Ops:
  63.1 50.1 %collective-permute-start.4 = (bf16[2048,1024]{1,0:T(8,128)(2,1)}, bf16[2048,1024]{1,0:T(8,128)(2,1)}, u32[]{:S(2)}, u32[]{:S(2)}) collective-permute-start(bf16[2048,1024]{1,0:T(8,128)(2,1)} %held.3), channel_id=1, source_target_pairs={{1,2},{2,1},{5,6},{6,5},{9,10},{10,9},{13,14},{14,13},{17,18},{18,... | collective-permute-start | bytes 12582920 | tf_op jit(solution)/shard_map/ppermute | solution.py:313
  91.3 34.2 %collective-permute-start.1 = (f32[512,1024]{1,0:T(8,128)}, f32[512,1024]{1,0:T(8,128)}, u32[]{:S(2)}, u32[]{:S(2)}) collective-permute-start(f32[512,1024]{1,0:T(8,128)} %fusion.27), channel_id=1, source_target_pairs={{0,2},{1,3},{2,0},{3,1},{4,6},{5,7},{6,4},{7,5},{8,10},{9,11},{10,... | collective-permute-start | bytes 6291464 | tf_op jit(solution)/shard_map/ppermute | solution.py:313
  120.8 30.2 %collective-permute-start.5 = (bf16[2048,1024]{1,0:T(8,128)(2,1)}, bf16[2048,1024]{1,0:T(8,128)(2,1)}, u32[]{:S(2)}, u32[]{:S(2)}) collective-permute-start(bf16[2048,1024]{1,0:T(8,128)(2,1)} %bitcast.22), channel_id=1, source_target_pairs={{0,2},{1,3},{2,0},{3,1},{4,6},{5,7},{6,4},{7,5},{8,10},{9,11},{10,... | collective-permute-start | bytes 12582920 | tf_op jit(solution)/shard_map/ppermute | solution.py:313
  123.4 16.3 %collective-permute-start.2 = (bf16[512,1024]{1,0:T(8,128)(2,1)}, bf16[512,1024]{1,0:T(8,128)(2,1)S(1)}, u32[]{:S(2)}, u32[]{:S(2)}) collective-permute-start(bf16[512,1024]{1,0:T(8,128)(2,1)} %held.2), channel_id=1, source_target_pairs={{1,2},{2,1},{5,6},{6,5},{9,10},{10,9},{13,14},{14,13},{17,18},{18,... | collective-permute-start | bytes 3145736 | tf_op jit(solution)/shard_map/ppermute | solution.py:313
  128.5 12.5 %collective-permute-start.3 = (bf16[512,1024]{1,0:T(8,128)(2,1)S(1)}, bf16[512,1024]{1,0:T(8,128)(2,1)S(1)}, u32[]{:S(2)}, u32[]{:S(2)}) collective-permute-start(bf16[512,1024]{1,0:T(8,128)(2,1)S(1)} %multiply_convert_fusion.1), channel_id=1, source_target_pairs={{0,2},{1,3},{2,0},{3,1},{4,6},{5,7},{6,4},{7,5},{8,10},{9,11},{10,... | collective-permute-start | bytes 3145736 | tf_op jit(solution)/shard_map/ppermute | solution.py:313
  143.7 48.5 %collective-permute-start.6 = (bf16[512,1024]{1,0:T(8,128)(2,1)S(1)}, bf16[512,1024]{1,0:T(8,128)(2,1)S(1)}, u32[]{:S(2)}, u32[]{:S(2)}) collective-permute-start(bf16[512,1024]{1,0:T(8,128)(2,1)S(1)} %fusion.15.g_own), channel_id=1, source_target_pairs={{0,1},{1,0},{2,3},{3,2},{4,5},{5,4},{6,7},{7,6},{8,9},{9,8},{10,11... | collective-permute-start | bytes 3145736 | tf_op jit(solution)/shard_map/ppermute | solution.py:313
  198.4 25.3 %collective-permute-start.8 = (bf16[512,1024]{1,0:T(8,128)(2,1)S(1)}, bf16[512,1024]{1,0:T(8,128)(2,1)S(1)}, u32[]{:S(2)}, u32[]{:S(2)}) collective-permute-start(bf16[512,1024]{1,0:T(8,128)(2,1)S(1)} %multiply_convert_fusion.n_own), channel_id=1, source_target_pairs={{0,1},{1,0},{2,3},{3,2},{4,5},{5,4},{6,7},{7,6},{8,9},{9,8},{10,11... | collective-permute-start | bytes 3145736 | tf_op jit(solution)/shard_map/ppermute | solution.py:313
  263.3 24.7 %collective-permute-start.9 = (bf16[512,1024]{1,0:T(8,128)(2,1)}, bf16[512,1024]{1,0:T(8,128)(2,1)}, u32[]{:S(2)}, u32[]{:S(2)}) collective-permute-start(bf16[512,1024]{1,0:T(8,128)(2,1)} %get-tuple-element.93), channel_id=1, source_target_pairs={{0,1},{1,0},{2,3},{3,2},{4,5},{5,4},{6,7},{7,6},{8,9},{9,8},{10,11... | collective-permute-start | bytes 3145736 | tf_op jit(solution)/shard_map/ppermute | solution.py:313
  268.3 32.9 %collective-permute-start.13 = (bf16[8,64,2048]{2,1,0:T(8,128)(2,1)}, bf16[8,64,2048]{2,1,0:T(8,128)(2,1)}, u32[]{:S(2)}, u32[]{:S(2)}) collective-permute-start(bf16[8,64,2048]{2,1,0:T(8,128)(2,1)} %dynamic-slice_bitcast_fusion), channel_id=1, source_target_pairs={{0,2},{1,3},{2,0},{3,1},{4,6},{5,7},{6,4},{7,5},{8,10},{9,11},{10,... | collective-permute-start | bytes 6291464 | tf_op jit(solution)/shard_map/ppermute | solution.py:313
  294.4 65.3 %collective-permute-start.15 = (bf16[512,1024]{1,0:T(8,128)(2,1)}, bf16[512,1024]{1,0:T(8,128)(2,1)S(1)}, u32[]{:S(2)}, u32[]{:S(2)}) collective-permute-start(bf16[512,1024]{1,0:T(8,128)(2,1)} %copy-done.18), channel_id=1, source_target_pairs={{0,1},{1,0},{2,3},{3,2},{4,5},{5,4},{6,7},{7,6},{8,9},{9,8},{10,11... | collective-permute-start | bytes 3145736 | tf_op jit(solution)/shard_map/ppermute | solution.py:313
  297.8 50.1 %collective-permute-start.11 = (bf16[8,128,1024]{2,1,0:T(8,128)(2,1)S(1)}, bf16[8,128,1024]{2,1,0:T(8,128)(2,1)S(1)}, u32[]{:S(2)}, u32[]{:S(2)}) collective-permute-start(bf16[8,128,1024]{2,1,0:T(8,128)(2,1)S(1)} %dynamic-slice_bitcast_fusion.1), channel_id=1, source_target_pairs={{0,2},{1,3},{2,0},{3,1},{4,6},{5,7},{6,4},{7,5},{8,10},{9,11},{10,... | collective-permute-start | bytes 6291464 | tf_op jit(solution)/shard_map/ppermute | solution.py:313
  304.9 54.8 %collective-permute-start.14 = (bf16[4,64,2048]{2,1,0:T(8,128)(2,1)S(1)}, bf16[4,64,2048]{2,1,0:T(8,128)(2,1)S(1)}, u32[]{:S(2)}, u32[]{:S(2)}) collective-permute-start(bf16[4,64,2048]{2,1,0:T(8,128)(2,1)S(1)} %dynamic-slice_bitcast_fusion.2), channel_id=1, source_target_pairs={{0,8},{1,9},{2,10},{3,11},{4,12},{5,13},{6,14},{7,15},{8,0},{9,1},... | collective-permute-start | bytes 3145736 | tf_op jit(solution)/shard_map/ppermute | solution.py:313
  349.1 25.4 %collective-permute-start.12 = (bf16[4,128,1024]{2,1,0:T(8,128)(2,1)S(1)}, bf16[4,128,1024]{2,1,0:T(8,128)(2,1)S(1)}, u32[]{:S(2)}, u32[]{:S(2)}) collective-permute-start(bf16[4,128,1024]{2,1,0:T(8,128)(2,1)S(1)} %dynamic-slice_bitcast_fusion.3), channel_id=1, source_target_pairs={{0,4},{1,5},{2,6},{3,7},{4,0},{5,1},{6,2},{7,3},{8,12},{9,13},{10,... | collective-permute-start | bytes 3145736 | tf_op jit(solution)/shard_map/ppermute | solution.py:313
  356.8 46.6 %collective-permute-start.21 = (bf16[2048,1024]{1,0:T(8,128)(2,1)}, bf16[2048,1024]{1,0:T(8,128)(2,1)}, u32[]{:S(2)}, u32[]{:S(2)}) collective-permute-start(bf16[2048,1024]{1,0:T(8,128)(2,1)} %convolution_convert_fusion.1), channel_id=1, source_target_pairs={{0,2},{1,3},{2,0},{3,1},{4,6},{5,7},{6,4},{7,5},{8,10},{9,11},{10,... | collective-permute-start | bytes 12582920 | tf_op jit(solution)/shard_map/ppermute | solution.py:313
  375.2 16.4 %collective-permute-start.17 = (f32[512,1024]{1,0:T(8,128)S(1)}, f32[512,1024]{1,0:T(8,128)S(1)}, u32[]{:S(2)}, u32[]{:S(2)}) collective-permute-start(f32[512,1024]{1,0:T(8,128)S(1)} %fusion.28), channel_id=1, source_target_pairs={{0,2},{1,3},{2,0},{3,1},{4,6},{5,7},{6,4},{7,5},{8,10},{9,11},{10,... | collective-permute-start | bytes 6291464 | tf_op jit(solution)/shard_map/ppermute | solution.py:313
  395.1 5.8 collective-permute-start.18
  396.0 26.2 %collective-permute-start.20 = (bf16[2,64,2048]{2,1,0:T(8,128)(2,1)S(1)}, bf16[2,64,2048]{2,1,0:T(8,128)(2,1)S(1)}, u32[]{:S(2)}, u32[]{:S(2)}) collective-permute-start(bf16[2,64,2048]{2,1,0:T(8,128)(2,1)S(1)} %dynamic-slice_bitcast_fusion.4), channel_id=1, source_target_pairs={{0,16},{1,17},{2,18},{3,19},{4,20},{5,21},{6,22},{7,23},{8,24},{9,... | collective-permute-start | bytes 1572872 | tf_op jit(solution)/shard_map/ppermute | solution.py:313
  398.2 24.6 %collective-permute-start.19 = (bf16[2,128,1024]{2,1,0:T(8,128)(2,1)S(1)}, bf16[2,128,1024]{2,1,0:T(8,128)(2,1)S(1)}, u32[]{:S(2)}, u32[]{:S(2)}) collective-permute-start(bf16[2,128,1024]{2,1,0:T(8,128)(2,1)S(1)} %dynamic-slice_bitcast_fusion.5), channel_id=1, source_target_pairs={{0,8},{1,9},{2,10},{3,11},{4,12},{5,13},{6,14},{7,15},{8,0},{9,1},... | collective-permute-start | bytes 1572872 | tf_op jit(solution)/shard_map/ppermute | solution.py:313
  412.8 263.7 %collective-permute-start.26 = (bf16[2048,1024]{1,0:T(8,128)(2,1)}, bf16[2048,1024]{1,0:T(8,128)(2,1)}, u32[]{:S(2)}, u32[]{:S(2)}) collective-permute-start(bf16[2048,1024]{1,0:T(8,128)(2,1)} %add_convert_fusion), channel_id=1, source_target_pairs={{1,2},{2,1},{5,6},{6,5},{9,10},{10,9},{13,14},{14,13},{17,18},{18,... | collective-permute-start | bytes 12582920 | tf_op jit(solution)/shard_map/ppermute | solution.py:313
  423.8 25.4 %collective-permute-start.22 = (bf16[2,128,1024]{2,1,0:T(8,128)(2,1)}, bf16[2,128,1024]{2,1,0:T(8,128)(2,1)}, u32[]{:S(2)}, u32[]{:S(2)}) collective-permute-start(bf16[2,128,1024]{2,1,0:T(8,128)(2,1)} %fusion.26), channel_id=1, source_target_pairs={{0,16},{1,17},{2,18},{3,19},{4,20},{5,21},{6,22},{7,23},{8,24},{9,... | collective-permute-start | bytes 1572872 | tf_op jit(solution)/shard_map/ppermute | solution.py:313
  424.8 24.4 %collective-permute-start.23 = (bf16[2,64,2048]{2,1,0:T(8,128)(2,1)}, bf16[2,64,2048]{2,1,0:T(8,128)(2,1)}, u32[]{:S(2)}, u32[]{:S(2)}) collective-permute-start(bf16[2,64,2048]{2,1,0:T(8,128)(2,1)} %fusion.25), channel_id=1, source_target_pairs={{0,4},{1,5},{2,6},{3,7},{4,0},{5,1},{6,2},{7,3},{8,12},{9,13},{10,... | collective-permute-start | bytes 1572872 | tf_op jit(solution)/shard_map/ppermute | solution.py:313
  455.4 21.9 %collective-permute-start.24 = (f32[512,1024]{1,0:T(8,128)}, f32[512,1024]{1,0:T(8,128)}, u32[]{:S(2)}, u32[]{:S(2)}) collective-permute-start(f32[512,1024]{1,0:T(8,128)} %fusion.16), channel_id=1, source_target_pairs={{0,2},{1,3},{2,0},{3,1},{4,6},{5,7},{6,4},{7,5},{8,10},{9,11},{10,... | collective-permute-start | bytes 6291464 | tf_op jit(solution)/shard_map/ppermute | solution.py:313
  457.9 26.9 %collective-permute-start.28 = (bf16[2,64,2048]{2,1,0:T(8,128)(2,1)}, bf16[2,64,2048]{2,1,0:T(8,128)(2,1)}, u32[]{:S(2)}, u32[]{:S(2)}) collective-permute-start(bf16[2,64,2048]{2,1,0:T(8,128)(2,1)} %add_convert_fusion.3), channel_id=1, source_target_pairs={{0,16},{1,17},{2,18},{3,19},{4,20},{5,21},{6,22},{7,23},{8,24},{9,... | collective-permute-start | bytes 1572872 | tf_op jit(solution)/shard_map/ppermute | solution.py:313
  462.4 24.5 %collective-permute-start.27 = (bf16[2,128,1024]{2,1,0:T(8,128)(2,1)}, bf16[2,128,1024]{2,1,0:T(8,128)(2,1)}, u32[]{:S(2)}, u32[]{:S(2)}) collective-permute-start(bf16[2,128,1024]{2,1,0:T(8,128)(2,1)} %add_convert_fusion.4), channel_id=1, source_target_pairs={{0,8},{1,9},{2,10},{3,11},{4,12},{5,13},{6,14},{7,15},{8,0},{9,1},... | collective-permute-start | bytes 1572872 | tf_op jit(solution)/shard_map/ppermute | solution.py:313
  488.2 7.0 %collective-permute-start.32 = (bf16[4,64,2048]{2,1,0:T(8,128)(2,1)S(1)}, bf16[4,64,2048]{2,1,0:T(8,128)(2,1)S(1)}, u32[]{:S(2)}, u32[]{:S(2)}) collective-permute-start(bf16[4,64,2048]{2,1,0:T(8,128)(2,1)S(1)} %pad_maximum_fusion.7.refs_0_), channel_id=1, source_target_pairs={{0,2},{1,3},{2,0},{3,1},{4,6},{5,7},{6,4},{7,5},{8,10},{9,11},{10,... | collective-permute-start | bytes 3145736 | tf_op jit(solution)/shard_map/ppermute | solution.py:313
  488.2 25.6 %collective-permute-start.30 = (bf16[4,64,2048]{2,1,0:T(8,128)(2,1)S(1)}, bf16[4,64,2048]{2,1,0:T(8,128)(2,1)S(1)}, u32[]{:S(2)}, u32[]{:S(2)}) collective-permute-start(bf16[4,64,2048]{2,1,0:T(8,128)(2,1)S(1)} %pad_maximum_fusion.7.refs_0_), channel_id=1, source_target_pairs={{0,8},{1,9},{2,10},{3,11},{4,12},{5,13},{6,14},{7,15},{8,0},{9,1},... | collective-permute-start | bytes 3145736 | tf_op jit(solution)/shard_map/ppermute | solution.py:313
  493.8 165.9 %collective-permute-start.31 = (bf16[4,128,1024]{2,1,0:T(8,128)(2,1)S(1)}, bf16[4,128,1024]{2,1,0:T(8,128)(2,1)}, u32[]{:S(2)}, u32[]{:S(2)}) collective-permute-start(bf16[4,128,1024]{2,1,0:T(8,128)(2,1)S(1)} %pad_maximum_fusion.6.refs_0_), channel_id=1, source_target_pairs={{0,2},{1,3},{2,0},{3,1},{4,6},{5,7},{6,4},{7,5},{8,10},{9,11},{10,... | collective-permute-start | bytes 3145736 | tf_op jit(solution)/shard_map/ppermute | solution.py:313
  494.2 165.5 %collective-permute-start.29 = (bf16[4,128,1024]{2,1,0:T(8,128)(2,1)S(1)}, bf16[4,128,1024]{2,1,0:T(8,128)(2,1)}, u32[]{:S(2)}, u32[]{:S(2)}) collective-permute-start(bf16[4,128,1024]{2,1,0:T(8,128)(2,1)S(1)} %pad_maximum_fusion.6.refs_0_), channel_id=1, source_target_pairs={{0,4},{1,5},{2,6},{3,7},{4,0},{5,1},{6,2},{7,3},{8,12},{9,13},{10,... | collective-permute-start | bytes 3145736 | tf_op jit(solution)/shard_map/ppermute | solution.py:313
  495.2 165.3 %collective-permute-start.16 = (bf16[512,1024]{1,0:T(8,128)(2,1)}, bf16[512,1024]{1,0:T(8,128)(2,1)}, u32[]{:S(2)}, u32[]{:S(2)}) collective-permute-start(bf16[512,1024]{1,0:T(8,128)(2,1)} %add_convert_fusion.2), channel_id=1, source_target_pairs={{1,2},{2,1},{5,6},{6,5},{9,10},{10,9},{13,14},{14,13},{17,18},{18,... | collective-permute-start | bytes 3145736 | tf_op jit(solution)/shard_map/ppermute | solution.py:313
  514.8 158.5 %collective-permute-start.25 = (bf16[512,1024]{1,0:T(8,128)(2,1)}, bf16[512,1024]{1,0:T(8,128)(2,1)}, u32[]{:S(2)}, u32[]{:S(2)}) collective-permute-start(bf16[512,1024]{1,0:T(8,128)(2,1)} %fusion.9), channel_id=1, source_target_pairs={{1,2},{2,1},{5,6},{6,5},{9,10},{10,9},{13,14},{14,13},{17,18},{18,... | collective-permute-start | bytes 3145736 | tf_op jit(solution)/shard_map/ppermute | solution.py:313
  659.7 30.6 %collective-permute-start.33 = (bf16[4,64,2048]{2,1,0:T(8,128)(2,1)S(1)}, bf16[4,64,2048]{2,1,0:T(8,128)(2,1)}, u32[]{:S(2)}, u32[]{:S(2)}) collective-permute-start(bf16[4,64,2048]{2,1,0:T(8,128)(2,1)S(1)} %copy-done.15), channel_id=1, source_target_pairs={{0,2},{1,3},{2,0},{3,1},{4,6},{5,7},{6,4},{7,5},{8,10},{9,11},{10,... | collective-permute-start | bytes 3145736 | tf_op jit(solution)/shard_map/ppermute | solution.py:313
  660.3 23.9 %collective-permute-start.34 = (bf16[4,128,1024]{2,1,0:T(8,128)(2,1)}, bf16[4,128,1024]{2,1,0:T(8,128)(2,1)}, u32[]{:S(2)}, u32[]{:S(2)}) collective-permute-start(bf16[4,128,1024]{2,1,0:T(8,128)(2,1)} %collective-permute-done.29.refs_1_), channel_id=1, source_target_pairs={{0,2},{1,3},{2,0},{3,1},{4,6},{5,7},{6,4},{7,5},{8,10},{9,11},{10,... | collective-permute-start | bytes 3145736 | tf_op jit(solution)/shard_map/ppermute | solution.py:313
  (77 other events, 1072.1 us)

commit v2 on v1

--- a/solution.py
+++ b/solution.py
@@ -287,25 +287,18 @@
     def swap(bit):
         return [(at, at ^ bit) for at in range(total)]
 
-    def off_swap(bit):
-        return [(at, at ^ bit) for at in range(total) if (at & 1) != ((at >> 1) & 1)]
-
     def turned(at):
         return (at & ~3) | ((at & 1) << 1) | ((at >> 1) & 1)
 
-    def crossed(at):
-        return (at & ~3) | ((1 - (at & 1)) << 1) | ((at >> 1) & 1)
-
     return {
         "turn": [(at, turned(at)) for at in range(total) if at != turned(at)],
-        "cross": [(at, crossed(at)) for at in range(total)],
+        "give": [(at, at ^ 2) for at in range(total) if (at & 1) == ((at >> 1) & 1)],
+        "take": [(at, at ^ 2) for at in range(total) if (at & 1) != ((at >> 1) & 1)],
         "y": swap(1),
         "core": swap(2),
         "x": swap(4),
         "zl": swap(8),
         "zh": swap(16),
-        "off_x": off_swap(4),
-        "off_zl": off_swap(8),
     }
 
 
@@ -374,6 +367,72 @@
     )(settled, held, arrived).reshape(flat_shape)
 
 
+def memory_kernel(examples, info, *refs):
+    sources, weight, rows_out, kv_out = refs[:6], refs[6], refs[7], refs[8]
+    block = 256
+    chunk = block // examples
+    high = lax.broadcasted_iota(jnp.int32, (block, block), 0)
+    low = lax.broadcasted_iota(jnp.int32, (block, block), 1)
+    hot = (low == (high % chunk) * examples + high // chunk).astype(jnp.bfloat16)
+
+    def write(source):
+        parts = []
+        for start in range(0, source.shape[0], block):
+            moved = nn(hot, source[start : start + block, :]).astype(jnp.bfloat16)
+            parts.append(moved.reshape(examples, chunk, moved.shape[1]))
+        moved = jnp.concatenate(parts, axis=1)
+        rows_out[...] = moved.reshape(rows_out.shape)
+        moved = nn(moved.reshape(source.shape), weight[...]).astype(jnp.bfloat16)
+        kv_out[...] = moved.reshape(kv_out.shape)
+
+    late = pl.program_id(1) >= 1
+    kind = jnp.where(pl.program_id(0) == 0, 0, jnp.where(late, 4, 2)) + info[1]
+    for i in range(6):
+        pl.when(kind == i)(functools.partial(write, sources[i]))
+
+
+def memory_rows(y_half, settled, sources, weight, examples):
+    rows, width = sources[0].shape
+    block = 512
+    blocks = rows // block
+    shape = (2, examples, rows // examples, width)
+    kv_shape = shape[:3] + (weight.shape[1],)
+
+    def source(which):
+        half, part = (0, 0) if which < 2 else (1, which // 2 - 1)
+        start = part
+        last = (blocks if half == 0 else 1 if part == 0 else blocks - 1) - 1
+
+        def index(p, i, s):
+            held = jnp.clip(i - start, 0, last)
+            return (jnp.where((p == half) & (s[1] == which % 2), held, 0), 0)
+
+        return pl.BlockSpec((block, width), index)
+
+    def out(columns):
+        return pl.BlockSpec(
+            (1, examples, block // examples, columns),
+            lambda p, i, s: ((p + s[0]) & 1, 0, i, 0),
+        )
+
+    return pl.pallas_call(
+        functools.partial(memory_kernel, examples),
+        grid_spec=pltpu.PrefetchScalarGridSpec(
+            num_scalar_prefetch=1,
+            grid=(2, blocks),
+            in_specs=[source(i) for i in range(6)]
+            + [pl.BlockSpec(weight.shape, lambda p, i, s: (0, 0))],
+            out_specs=[out(width), out(weight.shape[1])],
+        ),
+        out_shape=[
+            jax.ShapeDtypeStruct(shape, weight.dtype),
+            jax.ShapeDtypeStruct(kv_shape, weight.dtype),
+        ],
+        cost_estimate=cost(4 * rows * width * (weight.shape[1] + 256), 12 * rows * width),
+        compiler_params=pltpu.CompilerParams(vmem_limit_bytes=ATTEND_VMEM),
+    )(jnp.stack([y_half, settled]), *sources, weight)
+
+
 def nt(left, right):
     return lax.dot_general(
         left, right, (((1,), (1,)), ((), ())), preferred_element_type=jnp.float32
@@ -393,12 +452,6 @@
 def one_head(value, head):
     lane = lax.broadcasted_iota(jnp.int32, value.shape, 1)
     return jnp.where(lane // HEAD_DIM == head, value, jnp.zeros_like(value))
-
-
-def softmax_columns(scores):
-    top = jnp.max(scores, axis=0, keepdims=True)
-    weights = jnp.exp(scores - top)
-    return weights * (1.0 / jnp.sum(weights, axis=0, keepdims=True))
 
 
 def toeplitz(row, size):
@@ -416,155 +469,196 @@
     return jnp.sum(turned, axis=0, keepdims=True)
 
 
-def ordered(core, scratch, own, far):
-    half = own.shape[0]
-    scratch[pl.ds(pl.multiple_of(core * half, half), half), :] = own
-    scratch[pl.ds(pl.multiple_of((1 - core) * half, half), half), :] = far
-    return scratch[...]
-
-
-def split_store(core, scratch, value, out):
-    half = out.shape[1]
-    scratch[...] = value
-    out[0] = scratch[pl.ds(pl.multiple_of(core * half, half), half), :]
-    out[1] = scratch[pl.ds(pl.multiple_of((1 - core) * half, half), half), :]
-
-
-def self_scores(query, keys, bias, head, length):
-    scores = nt(keys, one_head(query, head)) + bias
-    key_at = lax.broadcasted_iota(jnp.int32, scores.shape, 0)
-    query_at = lax.broadcasted_iota(jnp.int32, scores.shape, 1)
-    return jnp.where((key_at <= query_at) & (key_at < length), scores, masked_score)
-
-
 def heads_joined(first, second):
-    return jnp.concatenate([first[:HEAD_DIM], second[HEAD_DIM:]], axis=0).T
-
-
-def self_forward_kernel(info, rows, bias, out, scratch, out_scratch, bias_scratch):
+    return jnp.concatenate([first, second], axis=0).T
+
+
+def head_rows(value, head):
+    return value[HEAD_DIM * head : HEAD_DIM * (head + 1)]
+
+
+def self_heads(core, rows, scratch, example):
+    half = scratch.shape[1] // 2
+    at = pl.ds(example * half, half)
+    scratch[example, pl.ds(pl.multiple_of(core * half, half), half), :] = rows[0, at, :]
+    scratch[example, pl.ds(pl.multiple_of((1 - core) * half, half), half), :] = rows[1, at, :]
+    return scratch[example]
+
+
+def self_store(core, value, scratch, out, example):
+    half = scratch.shape[1] // 2
+    at = pl.ds(example * half, half)
+    scratch[example] = value
+    out[0, at, :] = scratch[example, pl.ds(pl.multiple_of(core * half, half), half), :]
+    out[1, at, :] = scratch[example, pl.ds(pl.multiple_of((1 - core) * half, half), half), :]
+
+
+def self_masks(size, length):
+    key_at = lax.broadcasted_iota(jnp.int32, (size, size), 0)
+    query_at = lax.broadcasted_iota(jnp.int32, (size, size), 1)
+    return jnp.where((key_at <= query_at) & (key_at < length), 0.0, masked_score)
+
+
+def side_by_side(value):
+    return jnp.concatenate([one_head(value, head) for head in range(2)], axis=0)
+
+
+def own_blocks(value, size):
+    return value[:HEAD_DIM, :size], value[HEAD_DIM:, size:]
+
+
+def self_forward_kernel(examples, info, rows, bias, out, mixed, level, scratch, out_scratch):
     core = info[0]
-    example = pl.program_id(1)
-    length = info[1 + example]
-    size = scratch.shape[0]
-
-    @pl.when(example == 0)
-    def _():
+    size = scratch.shape[1]
+    slopes = jnp.concatenate(
+        [toeplitz(bias[0, head : head + 1, :], size) for head in range(2)], axis=1
+    )
+    for example in range(examples):
+        joined = self_heads(core, rows, scratch, example)
+        query, keys = joined[:, :128], joined[:, 128:256]
+        mask = self_masks(size, info[1 + example])
+        scores = nt(keys, side_by_side(query)) + slopes + jnp.concatenate([mask, mask], axis=1)
+        top = jnp.max(scores, axis=0, keepdims=True)
+        weights = jnp.exp(scores - top)
+        total = jnp.sum(weights, axis=0, keepdims=True)
+        probs = (weights * (1.0 / total)).astype(jnp.bfloat16)
+        sums = nn(joined[:, 256:].T, probs)
+        parts = own_blocks(sums, size)
+        levels = top + jnp.log(total)
         for head in range(2):
-            bias_scratch[head] = toeplitz(bias[0, head : head + 1, :], size)
-
-    joined = ordered(core, scratch, rows[0], rows[1])
-    query, keys, values = joined[:, :128], joined[:, 128:256], joined[:, 256:]
-    mixed = []
-    for head in range(2):
-        probs = softmax_columns(self_scores(query, keys, bias_scratch[head], head, length))
-        mixed.append(tn(values, probs.astype(jnp.bfloat16)))
-    result = heads_joined(*mixed).astype(jnp.bfloat16)
-    split_store(core, out_scratch, result, out)
+            level[0, example, head : head + 1, :] = levels[:, size * head : size * (head + 1)]
+            mixed[0, example, HEAD_DIM * head : HEAD_DIM * (head + 1), :] = parts[head]
+        result = heads_joined(*parts).astype(jnp.bfloat16)
+        self_store(core, result, out_scratch, out, example)
 
 
 def self_backward_kernel(
+    examples,
     info,
     rows,
     bias,
     grads,
+    mixed,
+    level,
     out,
     out_bias,
     scratch,
     grad_scratch,
     out_scratch,
-    bias_scratch,
-    sum_scratch,
 ):
     core = info[0]
-    example = pl.program_id(1)
-    length = info[1 + example]
-    size = scratch.shape[0]
-
-    @pl.when(example == 0)
-    def _():
+    size = scratch.shape[1]
+    slopes = jnp.concatenate(
+        [toeplitz(bias[0, head : head + 1, :], size) for head in range(2)], axis=1
+    )
+    sums = None
+    for example in range(examples):
+        joined = self_heads(core, rows, scratch, example)
+        query, keys, values = joined[:, :128], joined[:, 128:256], joined[:, 256:]
+        grad = self_heads(core, grads, grad_scratch, example)
+        products = grad.astype(jnp.float32).T * mixed[0, example]
+        inner = jnp.concatenate(
+            [jnp.sum(head_rows(products, head), axis=0, keepdims=True) for head in range(2)],
+            axis=1,
+        )
+        levels = jnp.concatenate([level[0, example, 0:1, :], level[0, example, 1:2, :]], axis=1)
+        mask = self_masks(size, info[1 + example])
+        heads, grad_heads = side_by_side(query), side_by_side(grad)
+        scores = nt(keys, heads) + slopes + jnp.concatenate([mask, mask], axis=1)
+        probs = jnp.exp(scores - levels)
+        grad_scores = (probs * (nt(values, grad_heads) - inner)).astype(jnp.bfloat16)
+        square = grad_scores.astype(jnp.float32)
+        sums = square if sums is None else sums + square
+        result = jnp.concatenate(
+            [
+                heads_joined(*own_blocks(nn(keys.T, grad_scores), size)),
+                nn(grad_scores, heads),
+                nn(probs.astype(jnp.bfloat16), grad_heads),
+            ],
+            axis=1,
+        ).astype(jnp.bfloat16)
+        self_store(core, result, out_scratch, out, example)
+    for head in range(2):
+        out_bias[0, head : head + 1, :] = diagonals(sums[:, size * head : size * (head + 1)])
+
+
+def by_length(length, span, body):
+    quarter = span // 4
+    for part in range(1, 5):
+        keys = part * quarter
+        inside = length > keys - quarter
+        if part < 4:
+            inside = inside & (length <= keys)
+
+        @pl.when(inside)
+        def _():
+            body(keys)
+
+
+def masked_tail(scores, length, quarter):
+    keys, count = scores.shape
+    key_at = keys - quarter + lax.broadcasted_iota(jnp.int32, (quarter, count), 0)
+    tail = scores[keys - quarter :] + jnp.where(key_at < length, 0.0, masked_score)
+    if keys == quarter:
+        return tail
+    return jnp.concatenate([scores[: keys - quarter], tail], axis=0)
+
+
+def cross_forward_kernel(info, queries, kv, out, mixed, level):
+    length = info[pl.program_id(0)]
+    query = queries[...].reshape(-1, 128)
+    count = query.shape[0]
+    span = 2 * kv.shape[1]
+    heads = side_by_side(query)
+
+    def body(keys):
+        joined = kv[...].reshape(span, 256)[:keys]
+        scores = masked_tail(nt(joined[:, :128], heads), length, span // 4)
+        top = jnp.max(scores, axis=0, keepdims=True)
+        weights = jnp.exp(scores - top)
+        total = jnp.sum(weights, axis=0, keepdims=True)
+        probs = (weights * (1.0 / total)).astype(jnp.bfloat16)
+        sums = nn(joined[:, 128:].T, probs)
+        parts = own_blocks(sums, count)
+        levels = top + jnp.log(total)
         for head in range(2):
-            bias_scratch[head] = toeplitz(bias[0, head : head + 1, :], size)
-        sum_scratch[...] = jnp.zeros_like(sum_scratch)
-
-    joined = ordered(core, scratch, rows[0], rows[1])
-    query, keys, values = joined[:, :128], joined[:, 128:256], joined[:, 256:]
-    grad = ordered(core, grad_scratch, grads[0], grads[1])
-    grad_query, grad_keys, grad_values, squares = [], [], [], []
-    for head in range(2):
-        probs = softmax_columns(self_scores(query, keys, bias_scratch[head], head, length))
-        low = probs.astype(jnp.bfloat16)
-        grad_head = one_head(grad, head)
-        grad_probs = nt(values, grad_head)
-        inner = jnp.sum(probs * grad_probs, axis=0, keepdims=True)
-        grad_scores = (probs * (grad_probs - inner)).astype(jnp.bfloat16)
-        grad_values.append(nn(low, grad_head))
-        grad_keys.append(nn(grad_scores, one_head(query, head)))
-        grad_query.append(tn(keys, grad_scores))
-        squares.append(grad_scores.astype(jnp.float32))
-    for head in range(2):
-        sum_scratch[head] = sum_scratch[head] + squares[head]
-    result = jnp.concatenate(
-        [
-            heads_joined(*grad_query),
-            grad_keys[0] + grad_keys[1],
-            grad_values[0] + grad_values[1],
-        ],
-        axis=1,
-    ).astype(jnp.bfloat16)
-    split_store(core, out_scratch, result, out)
-
-    @pl.when(example == pl.num_programs(1) - 1)
-    def _():
-        for head in range(2):
-            out_bias[0, head : head + 1, :] = diagonals(sum_scratch[head])
-
-
-def cross_scores(query, keys, head, core, length):
-    scores = nt(keys, one_head(query, head))
-    size = scores.shape[0]
-    key_at = lax.broadcasted_iota(jnp.int32, scores.shape, 0)
-    key_at = (key_at + core * (size // 2)) & (size - 1)
-    return jnp.where(key_at < length, scores, masked_score)
-
-
-def cross_forward_kernel(info, queries, kv_own, kv_far, out):
-    core = info[0]
-    length = info[1 + pl.program_id(0)]
+            mixed[0, 0, HEAD_DIM * head : HEAD_DIM * (head + 1), :] = parts[head]
+            level[0, 0, head : head + 1, :] = levels[:, count * head : count * (head + 1)]
+        out[...] = heads_joined(*parts).astype(jnp.bfloat16).reshape(out.shape)
+
+    by_length(length, span, body)
+
+
+def cross_backward_kernel(info, queries, kv, grads, mixed, level, dq, dkv):
+    length = info[pl.program_id(0)]
     query = queries[...].reshape(-1, 128)
-    keys = jnp.concatenate([kv_own[:, :128], kv_far[:, :128]], axis=0)
-    values = jnp.concatenate([kv_own[:, 128:], kv_far[:, 128:]], axis=0)
-    mixed = []
-    for head in range(2):
-        probs = softmax_columns(cross_scores(query, keys, head, core, length))
-        mixed.append(tn(values, probs.astype(jnp.bfloat16)))
-    out[...] = heads_joined(*mixed).astype(jnp.bfloat16).reshape(out.shape)
-
-
-def cross_backward_kernel(info, queries, kv_own, kv_far, grads, dq, dkv_own, dkv_far):
-    core = info[0]
-    length = info[1 + pl.program_id(0)]
-    query = queries[...].reshape(-1, 128)
+    count = query.shape[0]
     grad = grads[...].reshape(-1, 128)
-    keys = jnp.concatenate([kv_own[:, :128], kv_far[:, :128]], axis=0)
-    values = jnp.concatenate([kv_own[:, 128:], kv_far[:, 128:]], axis=0)
-    grad_query, grad_keys, grad_values = [], [], []
-    for head in range(2):
-        probs = softmax_columns(cross_scores(query, keys, head, core, length))
-        low = probs.astype(jnp.bfloat16)
-        grad_head = one_head(grad, head)
-        grad_probs = nt(values, grad_head)
-        inner = jnp.sum(probs * grad_probs, axis=0, keepdims=True)
-        grad_scores = (probs * (grad_probs - inner)).astype(jnp.bfloat16)
-        grad_values.append(nn(low, grad_head))
-        grad_keys.append(nn(grad_scores, one_head(query, head)))
-        grad_query.append(tn(keys, grad_scores))
-    dq[...] = heads_joined(*grad_query).astype(jnp.bfloat16).reshape(dq.shape)
-    result = jnp.concatenate(
-        [grad_keys[0] + grad_keys[1], grad_values[0] + grad_values[1]], axis=1
-    ).astype(jnp.bfloat16)
-    half = dkv_own.shape[0]
-    dkv_own[...] = result[:half]
-    dkv_far[...] = result[half:]
+    span = 2 * kv.shape[1]
+    heads, grad_heads = side_by_side(query), side_by_side(grad)
+    products = grad.astype(jnp.float32).T * mixed[0, 0]
+    inner = jnp.concatenate(
+        [jnp.sum(head_rows(products, head), axis=0, keepdims=True) for head in range(2)], axis=1
+    )
+    levels = jnp.concatenate([level[0, 0, 0:1, :], level[0, 0, 1:2, :]], axis=1)
+
+    def body(keys):
+        joined = kv[...].reshape(span, 256)[:keys]
+        scores = masked_tail(nt(joined[:, :128], heads), length, span // 4)
+        probs = jnp.exp(scores - levels)
+        grad_scores = (probs * (nt(joined[:, 128:], grad_heads) - inner)).astype(jnp.bfloat16)
+        result = jnp.concatenate(
+            [nn(grad_scores, heads), nn(probs.astype(jnp.bfloat16), grad_heads)], axis=1
+        ).astype(jnp.bfloat16)
+        if keys < span:
+            result = jnp.concatenate(
+                [result, jnp.zeros((span - keys, 256), jnp.bfloat16)], axis=0
+            )
+        dkv[...] = result.reshape(dkv.shape)
+        sums = nn(joined[:, :128].T, grad_scores)
+        dq[...] = heads_joined(*own_blocks(sums, count)).astype(jnp.bfloat16).reshape(dq.shape)
+
+    by_length(length, span, body)
 
 
 MIB = 1024 * 1024
@@ -588,38 +682,51 @@
     _, count, width = rows.shape
     pairs, size = width // 384, count // examples
     return pl.pallas_call(
-        self_forward_kernel,
-        grid=(pairs, examples),
+        functools.partial(self_forward_kernel, examples),
+        grid=(pairs,),
         in_specs=[
             SMEM_SPEC,
-            pl.BlockSpec((2, size, 384), lambda h, e: (0, e, h)),
-            pl.BlockSpec((1, 2, 2 * size), lambda h, e: (h, 0, 0)),
-        ],
-        out_specs=pl.BlockSpec((2, size, 128), lambda h, e: (0, e, h)),
-        out_shape=jax.ShapeDtypeStruct((2, count, pairs * 128), jnp.bfloat16),
+            pl.BlockSpec((2, count, 384), lambda h: (0, 0, h)),
+            pl.BlockSpec((1, 2, 2 * size), lambda h: (h, 0, 0)),
+        ],
+        out_specs=[
+            pl.BlockSpec((2, count, 128), lambda h: (0, 0, h)),
+            pl.BlockSpec((1, examples, 128, 2 * size), lambda h: (h, 0, 0, 0)),
+            pl.BlockSpec((1, examples, 2, 2 * size), lambda h: (h, 0, 0, 0)),
+        ],
+        out_shape=[
+            jax.ShapeDtypeStruct((2, count, pairs * 128), jnp.bfloat16),
+            jax.ShapeDtypeStruct((pairs, examples, 128, 2 * size), jnp.float32),
+            jax.ShapeDtypeStruct((pairs, examples, 2, 2 * size), jnp.float32),
+        ],
         scratch_shapes=[
-            pltpu.VMEM((2 * size, 384), jnp.bfloat16),
-            pltpu.VMEM((2 * size, 128), jnp.bfloat16),
-            pltpu.VMEM((2, 2 * size, 2 * size), jnp.float32),
-        ],
-        cost_estimate=cost(2 * 2 * examples * 2 * pairs * (2 * size) ** 2 * 256 * 8, 8 * rows.size, examples * 2 * pairs * (2 * size) ** 2),
-        compiler_params=pltpu.CompilerParams(vmem_limit_bytes=SMALL_VMEM),
+            pltpu.VMEM((examples, 2 * size, 384), jnp.bfloat16),
+            pltpu.VMEM((examples, 2 * size, 128), jnp.bfloat16),
+        ],
+        cost_estimate=cost(
+            2 * 2 * examples * 2 * pairs * (2 * size) ** 2 * 256 * 2,
+            8 * rows.size,
+            examples * 2 * pairs * (2 * size) ** 2,
+        ),
+        compiler_params=pltpu.CompilerParams(vmem_limit_bytes=ATTEND_VMEM),
     )(info, rows, bias)
 
 
-def self_backward(info, rows, bias, grads, examples):
+def self_backward(info, rows, bias, grads, mixed, level, examples):
     _, count, width = rows.shape
     pairs, size = width // 384, count // examples
-    row = pl.BlockSpec((1, 2, 2 * size), lambda h, e: (h, 0, 0))
-    wide = pl.BlockSpec((2, size, 384), lambda h, e: (0, e, h))
+    row = pl.BlockSpec((1, 2, 2 * size), lambda h: (h, 0, 0))
+    wide = pl.BlockSpec((2, count, 384), lambda h: (0, 0, h))
     return pl.pallas_call(
-        self_backward_kernel,
-        grid=(pairs, examples),
+        functools.partial(self_backward_kernel, examples),
+        grid=(pairs,),
         in_specs=[
             SMEM_SPEC,
             wide,
             row,
-            pl.BlockSpec((2, size, 128), lambda h, e: (0, e, h)),
+            pl.BlockSpec((2, count, 128), lambda h: (0, 0, h)),
+            pl.BlockSpec((1, examples, 128, 2 * size), lambda h: (h, 0, 0, 0)),
+            pl.BlockSpec((1, examples, 2, 2 * size), lambda h: (h, 0, 0, 0)),
         ],
         out_specs=[wide, row],
         out_shape=[
@@ -627,145 +734,180 @@
             jax.ShapeDtypeStruct((pairs, 2, 2 * size), jnp.float32),
         ],
         scratch_shapes=[
-            pltpu.VMEM((2 * size, 384), jnp.bfloat16),
-            pltpu.VMEM((2 * size, 128), jnp.bfloat16),
-            pltpu.VMEM((2 * size, 384), jnp.bfloat16),
-            pltpu.VMEM((2, 2 * size, 2 * size), jnp.float32),
-            pltpu.VMEM((2, 2 * size, 2 * size), jnp.float32),
-        ],
-        cost_estimate=cost(5 * 2 * examples * 2 * pairs * (2 * size) ** 2 * 256 * 8, 12 * rows.size, examples * 2 * pairs * (2 * size) ** 2),
-        compiler_params=pltpu.CompilerParams(vmem_limit_bytes=SMALL_VMEM),
-    )(info, rows, bias, grads)
-
-
-def cross_forward(info, queries, kv_own, kv_far, examples):
+            pltpu.VMEM((examples, 2 * size, 384), jnp.bfloat16),
+            pltpu.VMEM((examples, 2 * size, 128), jnp.bfloat16),
+            pltpu.VMEM((examples, 2 * size, 384), jnp.bfloat16),
+        ],
+        cost_estimate=cost(
+            5 * 2 * examples * 2 * pairs * (2 * size) ** 2 * 256 * 2,
+            12 * rows.size,
+            examples * 2 * pairs * (2 * size) ** 2,
+        ),
+        compiler_params=pltpu.CompilerParams(vmem_limit_bytes=ATTEND_VMEM),
+    )(info, rows, bias, grads, mixed, level)
+
+
+def cross_forward(info, queries, kv, examples):
     _, count, width = queries.shape
-    pairs, size, span = width // 128, count // examples, kv_own.shape[0] // examples
+    pairs, size, span = width // 128, count // examples, kv.shape[1] // examples
     thin = pl.BlockSpec((2, size, 128), lambda e, h: (0, e, h))
-    wide = pl.BlockSpec((span, 256), lambda e, h: (e, h))
+    wide = pl.BlockSpec((2, span, 256), lambda e, h: (0, e, h))
     return pl.pallas_call(
         cross_forward_kernel,
         grid=(examples, pairs),
-        in_specs=[SMEM_SPEC, thin, wide, wide],
-        out_specs=thin,
-        out_shape=jax.ShapeDtypeStruct(queries.shape, jnp.bfloat16),
-        cost_estimate=cost(2 * 2 * examples * 2 * pairs * 4 * size * span * 256 * 4, 8 * kv_own.size, examples * 2 * pairs * 4 * size * span),
+        in_specs=[SMEM_SPEC, thin, wide],
+        out_specs=[
+            thin,
+            pl.BlockSpec((1, 1, 128, 2 * size), lambda e, h: (e, h, 0, 0)),
+            pl.BlockSpec((1, 1, 2, 2 * size), lambda e, h: (e, h, 0, 0)),
+        ],
+        out_shape=[
+            jax.ShapeDtypeStruct(queries.shape, jnp.bfloat16),
+            jax.ShapeDtypeStruct((examples, pairs, 128, 2 * size), jnp.float32),
+            jax.ShapeDtypeStruct((examples, pairs, 2, 2 * size), jnp.float32),
+        ],
+        cost_estimate=cost(
+            2 * 2 * examples * 2 * pairs * 4 * size * span * 256,
+            4 * kv.size,
+            examples * 2 * pairs * 4 * size * span,
+        ),
         compiler_params=pltpu.CompilerParams(vmem_limit_bytes=ATTEND_VMEM),
-    )(info, queries, kv_own, kv_far)
-
-
-def cross_backward(info, queries, kv_own, kv_far, grads, examples):
+    )(info, queries, kv)
+
+
+def cross_backward(info, queries, kv, grads, mixed, level, examples):
     _, count, width = queries.shape
-    pairs, size, span = width // 128, count // examples, kv_own.shape[0] // examples
+    pairs, size, span = width // 128, count // examples, kv.shape[1] // examples
     thin = pl.BlockSpec((2, size, 128), lambda e, h: (0, e, h))
-    wide = pl.BlockSpec((span, 256), lambda e, h: (e, h))
+    wide = pl.BlockSpec((2, span, 256), lambda e, h: (0, e, h))
     return pl.pallas_call(
         cross_backward_kernel,
         grid=(examples, pairs),
-        in_specs=[SMEM_SPEC, thin, wide, wide, thin],
-        out_specs=[thin, wide, wide],
-        out_shape=[jax.ShapeDtypeStruct(queries.shape, jnp.bfloat16)]
-        + [jax.ShapeDtypeStruct(kv_own.shape, jnp.bfloat16)] * 2,
-        cost_estimate=cost(5 * 2 * examples * 2 * pairs * 4 * size * span * 256 * 2, 12 * kv_own.size, examples * 2 * pairs * 4 * size * span),
+        in_specs=[
+            SMEM_SPEC,
+            thin,
+            wide,
+            thin,
+            pl.BlockSpec((1, 1, 128, 2 * size), lambda e, h: (e, h, 0, 0)),
+            pl.BlockSpec((1, 1, 2, 2 * size), lambda e, h: (e, h, 0, 0)),
+        ],
+        out_specs=[thin, wide],
+        out_shape=[
+            jax.ShapeDtypeStruct(queries.shape, jnp.bfloat16),
+            jax.ShapeDtypeStruct(kv.shape, jnp.bfloat16),
+        ],
+        cost_estimate=cost(
+            5 * 2 * examples * 2 * pairs * 4 * size * span * 256,
+            6 * kv.size,
+            examples * 2 * pairs * 4 * size * span,
+        ),
         compiler_params=pltpu.CompilerParams(vmem_limit_bytes=ATTEND_VMEM),
-    )(info, queries, kv_own, kv_far, grads)
+    )(info, queries, kv, grads, mixed, level)
 
 
 root = math.sqrt(2.0 / math.pi)
 cubic = 0.044715
 
 
-def ffn_kernel(
-    n_own,
-    n_far,
-    g_own,
-    g_far,
-    into,
-    outof,
-    out_own,
-    out_far,
-    dn_own,
-    dn_far,
-    outof_grad,
-    into_grad,
-    turned,
-    out_sum,
-    dn_sum,
+def ffn_rows_kernel(normed, grad, into, outof, out, back, hidden_out, pre_out, out_sum, back_sum):
+    step = pl.program_id(0)
+
+    @pl.when(step == 0)
+    def _():
+        out_sum[...] = jnp.zeros_like(out_sum)
+        back_sum[...] = jnp.zeros_like(back_sum)
+
+    pre = nn(normed[...], into[...])
+    grad_hidden = nt(grad[...], outof[...])
+    bend = jnp.tanh(root * (pre + cubic * (pre * pre * pre)))
+    hidden = (0.5 * pre * (1.0 + bend)).astype(jnp.bfloat16)
+    slope = 0.5 * (1.0 + bend) + 0.5 * pre * (1.0 - bend * bend) * (
+        root * (1.0 + 3.0 * cubic * (pre * pre))
+    )
+    grad_pre = (grad_hidden * slope).astype(jnp.bfloat16)
+    hidden_out[...] = hidden
+    pre_out[...] = grad_pre
+    out_sum[...] += nn(hidden, outof[...])
+    back_sum[...] += nt(grad_pre, into[...])
+
+    @pl.when(step == pl.num_programs(0) - 1)
+    def _():
+        out[...] = out_sum[...].astype(out.dtype)
+        back[...] = back_sum[...].astype(back.dtype)
+
+
+def ffn_rows(normed, grad, into, outof, kind):
+    rows, width = normed.shape
+    units = into.shape[1]
+    tile = 512
+    whole = pl.BlockSpec((rows, width), lambda i: (0, 0))
+    tall = pl.BlockSpec((width, tile), lambda i: (0, i))
+    flat = pl.BlockSpec((tile, width), lambda i: (i, 0))
+    thin = pl.BlockSpec((rows, tile), lambda i: (0, i))
+    return pl.pallas_call(
+        ffn_rows_kernel,
+        grid=(units // tile,),
+        in_specs=[whole, whole, tall, flat],
+        out_specs=[whole, whole, thin, thin],
+        out_shape=[jax.ShapeDtypeStruct((rows, width), kind)] * 2
+        + [jax.ShapeDtypeStruct((rows, units), jnp.bfloat16)] * 2,
+        scratch_shapes=[pltpu.VMEM((rows, width), jnp.float32)] * 2,
+        cost_estimate=cost(
+            4 * 2 * rows * width * units, 12 * rows * width + 4 * width * units, rows * units
+        ),
+        compiler_params=pltpu.CompilerParams(vmem_limit_bytes=ATTEND_VMEM),
+    )(normed, grad, into, outof)
+
+
+def ffn_weights_kernel(
+    n_own, n_far, g_own, g_far, h_own, h_far, p_own, p_far, outof_grad, into_grad, turned
 ):
-    step = pl.program_id(0)
     half = n_own.shape[0]
 
-    @pl.when(step == 0)
+    @pl.when(pl.program_id(0) == 0)
     def _():
         turned[:, :half] = n_own[...].T
         turned[:, half:] = n_far[...].T
-        out_own[...] = jnp.zeros_like(out_own)
-        dn_own[...] = jnp.zeros_like(dn_own)
-        out_sum[...] = jnp.zeros_like(out_sum)
-        dn_sum[...] = jnp.zeros_like(dn_sum)
-
-    grads, backs = [], []
-    for normed, grad, out, back in (
-        (n_own, g_own, out_own, dn_own),
-        (n_far, g_far, out_sum, dn_sum),
-    ):
-        pre = nn(normed[...], into[...])
-        grad_hidden = nt(grad[...], outof[...])
-        bend = jnp.tanh(root * (pre + cubic * (pre * pre * pre)))
-        hidden = (0.5 * pre * (1.0 + bend)).astype(jnp.bfloat16)
-        slope = 0.5 * (1.0 + bend) + 0.5 * pre * (1.0 - bend * bend) * (
-            root * (1.0 + 3.0 * cubic * (pre * pre))
-        )
-        grad_pre = (grad_hidden * slope).astype(jnp.bfloat16)
-        out[...] += nn(hidden, outof[...])
-        back[...] += nt(grad_pre, into[...])
-        grads.append(tn(hidden, grad[...]))
-        backs.append(nn(turned[:, : half] if normed is n_own else turned[:, half:], grad_pre))
-    outof_grad[...] = (grads[0] + grads[1]).astype(jnp.bfloat16)
-    into_grad[...] = (backs[0] + backs[1]).astype(jnp.bfloat16)
-
-    @pl.when(step == pl.num_programs(0) - 1)
-    def _():
-        out_far[...] = out_sum[...].astype(jnp.bfloat16)
-        dn_far[...] = dn_sum[...].astype(jnp.bfloat16)
-
-
-def ffn(n_own, n_far, g_own, g_far, into, outof):
-    rows, width = n_own.shape
-    units = into.shape[1]
-    tile = 256
+
+    outof_grad[...] = (tn(h_own[...], g_own[...]) + tn(h_far[...], g_far[...])).astype(
+        jnp.bfloat16
+    )
+    into_grad[...] = (
+        nn(turned[:, :half], p_own[...]) + nn(turned[:, half:], p_far[...])
+    ).astype(jnp.bfloat16)
+
+
+def ffn_weights(normed, grads, hiddens, pres):
+    rows, width = normed[0].shape
+    units = hiddens[0].shape[1]
+    tile = 512
     whole = pl.BlockSpec((rows, width), lambda i: (0, 0))
-    tall = pl.BlockSpec((width, tile), lambda i: (0, i))
-    flat = pl.BlockSpec((tile, width), lambda i: (i, 0))
-    wide = jax.ShapeDtypeStruct((rows, width), jnp.float32)
-    thin = jax.ShapeDtypeStruct((rows, width), jnp.bfloat16)
+    thin = pl.BlockSpec((rows, tile), lambda i: (0, i))
     return pl.pallas_call(
-        ffn_kernel,
+        ffn_weights_kernel,
         grid=(units // tile,),
-        in_specs=[whole, whole, whole, whole, tall, flat],
-        out_specs=[whole, whole, whole, whole, flat, tall],
+        in_specs=[whole] * 4 + [thin] * 4,
+        out_specs=[
+            pl.BlockSpec((tile, width), lambda i: (i, 0)),
+            pl.BlockSpec((width, tile), lambda i: (0, i)),
+        ],
         out_shape=[
-            wide,
-            thin,
-            wide,
-            thin,
-            jax.ShapeDtypeStruct(outof.shape, jnp.bfloat16),
-            jax.ShapeDtypeStruct(into.shape, jnp.bfloat16),
-        ],
-        scratch_shapes=[
-            pltpu.VMEM((width, 2 * rows), jnp.bfloat16),
-            pltpu.VMEM((rows, width), jnp.float32),
-            pltpu.VMEM((rows, width), jnp.float32),
-        ],
-        cost_estimate=cost(6 * 2 * 2 * rows * width * units, 24 * rows * width + 8 * width * units, 2 * rows * units),
-        compiler_params=pltpu.CompilerParams(vmem_limit_bytes=FFN_VMEM),
-    )(n_own, n_far, g_own, g_far, into, outof)
-
-
-def gather_kernel(groups, examples, tokens, facts, counts, *refs):
+            jax.ShapeDtypeStruct((units, width), jnp.bfloat16),
+            jax.ShapeDtypeStruct((width, units), jnp.bfloat16),
+        ],
+        scratch_shapes=[pltpu.VMEM((width, 2 * rows), jnp.bfloat16)],
+        cost_estimate=cost(
+            4 * 2 * rows * width * units, 8 * rows * width + 4 * width * units
+        ),
+        compiler_params=pltpu.CompilerParams(vmem_limit_bytes=30 * MIB),
+    )(*normed, *grads, *hiddens, *pres)
+
+
+def gather_kernel(groups, examples, tokens, memory, facts, counts, *refs):
     weights, refs = refs[:8], refs[8:]
-    tok_out, facts_out, counts_out, self_in, cross_q, cross_kv, self_out, cross_out = refs[:8]
-    raw, landed, round_in, near_send, near_get, send, get = refs[8:]
+    tok_out, mem_out, facts_out, counts_out, self_in, cross_q, cross_kv = refs[:7]
+    self_out, cross_out = refs[7:9]
+    raw, landed, round_in, near_send, near_get, send, get = refs[9:]
     index, y = lax.axis_index("dp"), lax.axis_index("mp")
     core, x, z = index % 2, (index // 2) % 2, index // 4
     deep = groups // 4
@@ -835,6 +977,8 @@
 
     token_copy = remote(tokens, landed, (send, get), 40, turned)
     facts_copy = remote(facts, facts_out, (send, get), 41, turned)
+    early = memory.at[pl.ds(0, mem_out.shape[0])]
+    memory_copy = remote(early, mem_out, (send, get), 42 + len(rounds), turned)
 
     @pl.when(core != y)
     def _():
@@ -842,6 +986,7 @@
         for w in range(8):
             along_y(w).start()
         token_copy.start()
+        memory_copy.start()
 
     @pl.when(core == y)
     def _():
@@ -850,13 +995,17 @@
         for w in range(8):
             pltpu.make_async_copy(weights[w], homes[w], near_get.at[2 + w]).start()
 
+    def count_copy(i):
+        return remote(counts_out, round_in.at[i], (near_send, get), 42 + i, rounds[i])
+
+    def count_round(w):
+        if w % 2 == 1 and w // 2 < len(rounds):
+            count_copy(w // 2).start()
+        if w % 2 == 0 and 0 < w <= 2 * len(rounds):
+            count_copy(w // 2 - 1).wait()
+            counts_out[...] += round_in[w // 2 - 1]
+
     counts_out[...] = counts[...]
-    for i, partner in enumerate(rounds):
-        swap = remote(counts_out, round_in.at[i], (near_send, get), 42 + i, partner)
-        swap.start()
-        swap.wait()
-        counts_out[...] += round_in[i]
-
     @pl.when(core == y)
     def _():
         pltpu.make_async_copy(tokens, landed, near_get.at[0]).wait()
@@ -864,19 +1013,24 @@
         for w in range(8):
             pltpu.make_async_copy(weights[w], homes[w], near_get.at[2 + w]).wait()
 
+    def share(w):
+        if w < 8:
+            along_y(w).wait()
+            for which in range(2):
+                direct(w, which).start()
+        if w > 0:
+            for which in range(2):
+                direct(w - 1, which).wait()
+            for which in range(2):
+                passed(w - 1, which).start()
+
+    for w in range(9):
+        pl.when(core != y)(functools.partial(share, w))
+        count_round(w)
+
     @pl.when(core != y)
     def _():
         facts_copy.wait()
-        for w in range(9):
-            if w < 8:
-                along_y(w).wait()
-                for which in range(2):
-                    direct(w, which).start()
-            if w > 0:
-                for which in range(2):
-                    direct(w - 1, which).wait()
-                for which in range(2):
-                    passed(w - 1, which).start()
         token_copy.wait()
 
     rows = landed.shape[0]
@@ -894,6 +1048,7 @@
         for w in range(8):
             for which in range(2):
                 passed(w, which).wait()
+        memory_copy.wait()
 
     for h in range(raw.shape[2] // 128):
         for i in range(3):
@@ -906,7 +1061,7 @@
             ]
 
 
-def gather(tokens, facts, counts, weights, groups, examples):
+def gather(tokens, memory, facts, counts, weights, groups, examples):
     rows, width = tokens.shape
     inner = weights[0].shape[1]
     rounds = 2 + (groups // 4).bit_length() - 1
@@ -918,10 +1073,11 @@
 
     return pl.pallas_call(
         functools.partial(gather_kernel, groups, examples),
-        in_specs=[anywhere, whole, whole] + [anywhere] * 8,
-        out_specs=[whole] * 8,
+        in_specs=[anywhere, anywhere, whole, whole] + [anywhere] * 8,
+        out_specs=[whole] * 9,
         out_shape=[
             half(examples, rows // examples, width),
+            half(memory.shape[0] // 4, width),
             jax.ShapeDtypeStruct(facts.shape, facts.dtype),
             jax.ShapeDtypeStruct(counts.shape, counts.dtype),
             half(width, 3 * inner),
@@ -936,14 +1092,14 @@
             pltpu.VMEM((rounds,) + counts.shape, counts.dtype),
             pltpu.SemaphoreType.DMA((42 + rounds,)),
             pltpu.SemaphoreType.DMA((10,)),
-            pltpu.SemaphoreType.DMA((42,)),
-            pltpu.SemaphoreType.DMA((42 + rounds,)),
+            pltpu.SemaphoreType.DMA((43 + rounds,)),
+            pltpu.SemaphoreType.DMA((43 + rounds,)),
         ],
         cost_estimate=cost(0, 150 * MIB),
         compiler_params=pltpu.CompilerParams(
             collective_id=1, has_side_effects=True, vmem_limit_bytes=SETTLE_VMEM
         ),
-    )(tokens, facts, counts, *weights)
+    )(tokens, memory, facts, counts, *weights)
 
 
 def add_low(left, right):
@@ -954,29 +1110,39 @@
     return lax.dynamic_index_in_dim(value, index, 0, keepdims=False)
 
 
+axis_of = {"zh": 0, "zl": 1, "x": 2, "core": 3}
+
+
+def part_sent(total, name, place):
+    return lax.dynamic_index_in_dim(total, 1 - place[name], axis_of[name])
+
+
 def part_out(total, name, place, net):
-    view = total.reshape(2, total.shape[0] // 2, *total.shape[1:])
-    return permute(pick(view, 1 - place[name]), net[name])
+    return permute(part_sent(total, name, place), net[name])
 
 
 def part_in(total, arrived, name, place):
-    view = total.reshape(2, total.shape[0] // 2, *total.shape[1:])
-    return add_low(pick(view, place[name]), arrived)
+    kept = lax.dynamic_index_in_dim(total, place[name], axis_of[name])
+    return add_low(kept, arrived)
 
 
 def halve(total, name, place, net):
     return part_in(total, part_out(total, name, place, net), name, place)
 
 
-def beside(own, arrived):
-    return jnp.concatenate([own, arrived], axis=0)
+def by_device(value):
+    return value.reshape(2, 2, 2, 2, value.shape[0] // 16, value.shape[1])
 
 
 def tie(*values):
     return lax.optimization_barrier(values)
 
 
-def settle_kernel(groups, value, small, out, small_out, first, second, third, small_in, send, receive, small_send, small_get):
+def settle_kernel(groups, *refs):
+    count = len(refs) - 13
+    parts, small, refs = refs[:count], refs[count], refs[count + 1 :]
+    out, small_out, value, first, second, third, small_in = refs[:7]
+    send, receive, small_send, small_get, load = refs[7:]
     index, y = lax.axis_index("dp"), lax.axis_index("mp")
     core, x, z = index % 2, (index // 2) % 2, index // 4
     deep = groups // 4
@@ -988,6 +1154,13 @@
     def part(k):
         return pl.ds(pl.multiple_of(k * rows, rows), rows)
 
+    loads, starts = [], [0]
+    for i, ref in enumerate(parts):
+        size = ref.shape[1]
+        target = value.at[:, pl.ds(starts[-1], size)]
+        loads.append(pltpu.make_async_copy(ref, target, load.at[i]))
+        loads[-1].start()
+        starts.append(starts[-1] + size)
     partners = [at(1 - core, y, x, z), at(core, 1 - y, x, z), at(1 - core, 1 - y, x, z)]
     partners.append(at(core, y, 1 - x, z))
     for step in range(1, deep):
@@ -1086,7 +1259,9 @@
 
         return carry
 
-    lax.fori_loop(0, chunks, start, 0)
+    for i in range(count):
+        loads[i].wait()
+        lax.fori_loop(starts[i] // rows, starts[i + 1] // rows, start, 0)
     for i in range(1, len(rounds)):
         small_round(i)
 
@@ -1188,36 +1363,40 @@
     lax.fori_loop(0, chunks, finish_sends, 0)
 
 
-def settle(value, small, groups):
-    count, rows, width = value.shape
-    chunk = 32
+def settle(parts, small, groups):
+    count, _, width = parts[0].shape
+    kind = parts[0].dtype
+    rows = sum(part.shape[1] for part in parts)
+    chunk = 16
     chunks = rows // chunk
     deep = groups // 4
     rounds = 3 + deep.bit_length() - 1
     whole = pl.BlockSpec(memory_space=pltpu.VMEM)
     return pl.pallas_call(
         functools.partial(settle_kernel, groups),
-        in_specs=[whole, whole],
+        in_specs=[pl.BlockSpec(memory_space=pl.ANY)] * len(parts) + [whole],
         out_specs=[whole, whole],
         out_shape=[
-            jax.ShapeDtypeStruct(value.shape, value.dtype),
+            jax.ShapeDtypeStruct((count, rows, width), kind),
             jax.ShapeDtypeStruct((2,) + small.shape, small.dtype),
         ],
         scratch_shapes=[
-            pltpu.VMEM((chunks, 2, count // 2, chunk, width), value.dtype),
-            pltpu.VMEM((chunks, deep, chunk, width), value.dtype),
-            pltpu.VMEM((chunks, deep - 1, chunk, width), value.dtype),
+            pltpu.VMEM((count, rows, width), kind),
+            pltpu.VMEM((chunks, 2, count // 2, chunk, width), kind),
+            pltpu.VMEM((chunks, deep, chunk, width), kind),
+            pltpu.VMEM((chunks, deep - 1, chunk, width), kind),
             pltpu.VMEM((rounds,) + small.shape, small.dtype),
             pltpu.SemaphoreType.DMA((chunks, 12)),
             pltpu.SemaphoreType.DMA((chunks, 12)),
             pltpu.SemaphoreType.DMA((rounds,)),
             pltpu.SemaphoreType.DMA((rounds,)),
-        ],
-        cost_estimate=cost(0, 60 * value.size),
+            pltpu.SemaphoreType.DMA((len(parts),)),
+        ],
+        cost_estimate=cost(0, 60 * count * rows * width),
         compiler_params=pltpu.CompilerParams(
             collective_id=0, has_side_effects=True, vmem_limit_bytes=SETTLE_VMEM
         ),
-    )(value, small)
+    )(*parts, small)
 
 
 def unpack_kernel(pairs, source, key, val, cross_out, self_out, cross_q, *self_in):
@@ -1258,42 +1437,27 @@
     )(value)
 
 
-def finish_kernel(info, *refs):
-    target = refs[4]
-    rows = refs[0].shape[1]
-    which = 2 * ((pl.program_id(0) >> 1) ^ info[1]) + ((pl.program_id(0) & 1) ^ (info[0] >> 2))
-
-    for held in range(4):
-
-        @pl.when(which == held)
-        def _():
-            for i in range(4):
-                target[rows * i : rows * (i + 1), :] = refs[held][i ^ (info[0] & 3)].astype(
-                    jnp.float32
-                )
-
-
-def finish(done, order, place, shape):
-    count, rows, width = done[0].shape
-    mine = place[order[0]] * 4 + place[order[1]] * 2
-    info = jnp.stack([mine, place["core"]])
+def widen_kernel(source, target):
+    target[...] = source[...].astype(jnp.float32)
+
+
+def widen(value, shape):
+    rows, width = shape
+    block = rows // 4
+    spec = pl.BlockSpec((block, width), lambda i: (i, 0))
     return pl.pallas_call(
-        finish_kernel,
-        grid_spec=pltpu.PrefetchScalarGridSpec(
-            num_scalar_prefetch=1,
-            grid=(4,),
-            in_specs=[pl.BlockSpec((4, rows, width), lambda i, s: (0, 0, 0))] * 4,
-            out_specs=pl.BlockSpec((shape[0] // 4, shape[1]), lambda i, s: (i, 0)),
-        ),
+        widen_kernel,
+        grid=(4,),
+        in_specs=[spec],
+        out_specs=spec,
         out_shape=jax.ShapeDtypeStruct(shape, jnp.float32),
-        cost_estimate=cost(0, 4 * done[0].size * 12),
+        cost_estimate=cost(0, 6 * rows * width),
         compiler_params=pltpu.CompilerParams(vmem_limit_bytes=ATTEND_VMEM),
-    )(info, *done)
-
-
-def pieces(*values):
-    split = [v.reshape(16, v.shape[0] // 16, v.shape[1]) for v in values]
-    return split[0] if len(split) == 1 else jnp.concatenate(split, axis=1)
+    )(value.reshape(shape))
+
+
+def pieces(value):
+    return value.reshape(16, value.shape[0] // 16, value.shape[1])
 
 
 def low(value):
@@ -1359,14 +1523,18 @@
     )
     facts = jnp.pad(facts, ((0, 8 - facts.shape[0]), (0, 0)))
     counts = jnp.broadcast_to(jnp.sum(target_lengths).astype(jnp.float32), (8, 128))
-    tok, facts, counts, self_in, cross_q, cross_kv, self_out, cross_out = gather(
+    mem_near = permute(memory, net["give"])
+    held = gather(
         tokens,
+        memory,
         facts,
         counts,
         [query_self, key_self, value_self, query_cross, key_cross, value_cross, out_self, out_cross],
         groups,
         examples,
     )
+    tok, mem_first, facts, counts, self_in, cross_q, cross_kv = held[:7]
+    self_out, cross_out = held[7:]
     tok = tok.reshape(rows, width)
     target_len = facts[0, :examples].astype(jnp.int32)
     memory_len = facts[0, examples : 2 * examples].astype(jnp.int32)
@@ -1374,9 +1542,9 @@
     group_count = jnp.sum(target_len).astype(jnp.float32)
     token_scale = groups * group_count / counts[0, 0]
     self_info = jnp.concatenate([core[None], target_len])
-    cross_info = jnp.concatenate([core[None], memory_len])
-    memory_after, tok = tie(memory, tok)
-    mem_raw = turn(memory_after)
+    mem_sent, tok = tie(memory[mem_first.shape[0] :], tok)
+    mem_rest = turn(mem_sent)
+    first_far = permute(mem_first, net["take"])
 
     span = 2 * half_pos
     distance = jnp.arange(span, dtype=jnp.int32)
@@ -1393,77 +1561,84 @@
     qkv = low(nn(flat(n1), self_in)).reshape(2, rows, -1)
     cot_after, qkv = tie(cotangent, qkv)
     cot_raw = turn(cot_after)
-    a1 = self_forward(self_info, qkv, bias, examples)
-    r1 = tok_float + (nn(a1[0], self_out) + swap(nn(a1[1], self_out)))
-
-    mem = reorder(False, memory, mem_raw, place["settled"], examples)
-    mem_far = swap(mem)
-    kv, kv_far = low(nn(mem, cross_kv)), low(nn(mem_far, cross_kv))
+    a1, mixed_one, level_one = self_forward(self_info, qkv, bias, examples)
+    r1 = tok_float + (nn(a1[0], self_out) + swap(low(nn(a1[1], self_out))).astype(jnp.float32))
+
+    rest_far = permute(mem_rest, net["take"])
+    mem, kv = memory_rows(
+        place["y"],
+        settled,
+        [mem_near, memory, mem_first, first_far, mem_rest, rest_far],
+        cross_kv,
+        examples,
+    )
+    mem = mem.reshape(2, -1, width)
+    kv = kv.reshape(2, -1, 2 * inner)
     n2 = both(low(rms_norm(r1, norm_cross.astype(jnp.float32))))
     q2 = low(nn(flat(n2), cross_q)).reshape(2, rows, -1)
 
+    kv, cot_raw = tie(kv, cot_raw)
     cot = reorder(False, cotangent, cot_raw, place["settled"], examples)
     positions = core * half_pos + jnp.arange(half_pos, dtype=jnp.int32)
     live = (positions[None, :] < target_len[:, None]).astype(jnp.float32).reshape(rows, 1)
     dy = cot.astype(jnp.float32) * live * token_scale
-    gy, q2 = tie(low(dy), q2)
+    gy = low(dy)
     gy_far = permute(gy, net["y"])
 
-    a2 = cross_forward(cross_info, q2, kv, kv_far, examples)
+    a2, mixed_two, level_two = cross_forward(memory_len, q2, kv, examples)
     a2, gy_far = tie(a2, gy_far)
-    r2 = r1 + (nn(a2[0], cross_out) + swap(nn(a2[1], cross_out)))
+    r2 = r1 + (nn(a2[0], cross_out) + swap(low(nn(a2[1], cross_out))).astype(jnp.float32))
 
     n3 = low(rms_norm(r2, norm_ffn.astype(jnp.float32)))
     n3_far = permute(n3, net["y"])
-    out_own, out_far, dn_own, dn_far, ffn_out_part, ffn_in_part = ffn(
-        n3, n3_far, gy, gy_far, ffn_in, ffn_out
-    )
+    out_own, dn_own, h_own, p_own = ffn_rows(n3, gy, ffn_in, ffn_out, jnp.float32)
+    out_own, n3_far = tie(out_own, n3_far)
+    out_far, dn_far, h_far, p_far = ffn_rows(n3_far, gy_far, ffn_in, ffn_out, jnp.bfloat16)
     dn_far = permute(dn_far, net["y"])
-    first = pieces(ffn_out_part)
-    second = pieces(ffn_in_part)
-    first, second = halve(first, "core", place, net), halve(second, "core", place, net)
-    first_in, second_in = part_out(first, "x", place, net), part_out(second, "zl", place, net)
+    ffn_out_part, ffn_in_part = ffn_weights(
+        (n3, n3_far), (gy, gy_far), (h_own, h_far), (p_own, p_far)
+    )
+    dn_far, ffn_out_part = tie(dn_far, ffn_out_part)
+    first = lax.psum_scatter(ffn_out_part, "dp", scatter_dimension=0, tiled=True)
+    second = lax.psum_scatter(ffn_in_part, "dp", scatter_dimension=0, tiled=True)
     dn3 = dn_own + dn_far.astype(jnp.float32)
     back, gain_three = norm_backward(r2, norm_ffn, dn3)
     dr2 = dy + back
 
     g2 = both(low(dr2))
     da2 = low(nt(flat(g2), cross_out)).reshape(2, rows, -1)
+    da2, out_far = tie(da2, out_far)
     out_far = permute(out_far, net["y"])
-    dq2, dkv, dkv_far = cross_backward(cross_info, q2, kv, kv_far, da2, examples)
-    dq2, first_in, second_in, out_far = tie(dq2, first_in, second_in, out_far)
-    first = part_in(first, first_in, "x", place)
-    second = part_in(second, second_in, "zl", place)
-    first_in, second_in = part_out(first, "zl", place, net), part_out(second, "zh", place, net)
+    dq2, dkv = cross_backward(memory_len, q2, kv, da2, mixed_two, level_two, examples)
+    dkv, out_far = tie(dkv, out_far)
     block_out = low(r2 + (out_own + out_far.astype(jnp.float32)))
     block_back = turn(block_out)
-    memory_grad = low(
-        nt(dkv, cross_kv) + swap(low(nt(dkv_far, cross_kv))).astype(jnp.float32)
-    )
+    dkv_swapped = swap(low(nt(pick(dkv, 1 - core), cross_kv)))
+    cross_kv_part = low(tn(flat(mem), flat(dkv)))
+    dkv_swapped, cross_kv_part = tie(dkv_swapped, cross_kv_part)
+    memory_grad = low(nt(pick(dkv, core), cross_kv) + dkv_swapped.astype(jnp.float32))
+    memory_grad, cross_kv_part, dq2, first = tie(memory_grad, cross_kv_part, dq2, first)
+    first = lax.all_gather(first, "dp", axis=0, tiled=True)
     memory_back = turn(memory_grad)
-    dn2 = nt(dq2[0], cross_q) + swap(nt(dq2[1], cross_q))
+    dn2 = nt(dq2[0], cross_q) + swap(low(nt(dq2[1], cross_q))).astype(jnp.float32)
     back, gain_two = norm_backward(r1, norm_cross, dn2)
     dr1 = dr2 + back
-    cross_kv_part = low(tn(mem, dkv) + tn(mem_far, dkv_far))
     cross_out_part = low(tn(flat(a2), flat(g2)))
     cross_q_part = low(tn(flat(dq2), flat(n2)))
 
     g1 = both(low(dr1))
     self_out_part = low(tn(flat(a1), flat(g1)))
     da1 = low(nt(flat(g1), self_out)).reshape(2, rows, -1)
-    head_parts = pieces(cross_kv_part, cross_out_part, self_out_part, cross_q_part)
-    da1, first_in, second_in, head_parts, memory_grad = tie(
-        da1, first_in, second_in, head_parts, memory_grad
-    )
-    first = part_in(first, first_in, "zl", place)
-    second = part_in(second, second_in, "zh", place)
-    first_in, second_in = permute(first, net["zh"]), permute(second, net["x"])
-    dqkv, by_distance = self_backward(self_info, qkv, bias, da1, examples)
-    dqkv, first_in, second_in = tie(dqkv, first_in, second_in)
-    first, second = add_low(first, first_in), add_low(second, second_in)
-    first_in, second_in = permute(first, net["zl"]), permute(second, net["zh"])
+    head_parts = [cross_kv_part, cross_out_part, self_out_part, cross_q_part]
+    da1, head_parts = tie(da1, head_parts)
+    dqkv, by_distance = self_backward(
+        self_info, qkv, bias, da1, mixed_one, level_one, examples
+    )
     self_in_part = low(tn(flat(dqkv), flat(n1)))
-    dn1 = nt(dqkv[0], self_in) + swap(nt(dqkv[1], self_in))
+    dqkv, self_in_part, memory_back, block_back = tie(
+        dqkv, self_in_part, memory_back, block_back
+    )
+    dn1 = nt(dqkv[0], self_in) + swap(low(nt(dqkv[1], self_in))).astype(jnp.float32)
     back, gain_one = norm_backward(tok_float, norm_self, dn1)
     tokens_grad = low(dr1 + back)
     tokens_back = turn(tokens_grad)
@@ -1475,17 +1650,13 @@
     small = jnp.concatenate(
         [gain_one[None], gain_two[None], gain_three[None], bias_row, jnp.zeros((4, width))], axis=0
     )
-    head_parts = jnp.concatenate([head_parts, pieces(self_in_part)], axis=1)
-    head_parts, small, first_in, second_in = tie(head_parts, small, first_in, second_in)
-    first, second = beside(first, first_in), beside(second, second_in)
-    first_in, second_in = permute(first, net["x"]), permute(second, net["zl"])
-    first_far, second_far = swap(first), swap(second)
+    head_parts = [pieces(part) for part in head_parts + [self_in_part]]
+    head_parts, second = tie(head_parts, second)
+    second = lax.all_gather(second, "dp", axis=0, tiled=True)
     heads_done, small = settle(head_parts, small, groups)
-    small, first_in, second_in, first_far, second_far = tie(
-        small, first_in, second_in, first_far, second_far
-    )
-    first = (first, first_in, first_far, swap(first_in))
-    second = (second, second_in, second_far, swap(second_in))
+    small, first, second, block_back, tokens_back, memory_back = tie(
+        small, first, second, block_back, tokens_back, memory_back
+    )
     gains = small[0, :3] + small[1, :3]
     bias_sum = jnp.where(settled == 1, small[0, 3], small[1, 3])
     bias_grad = bias_sum[: bias_part.size].reshape(bias_part.shape)
@@ -1493,8 +1664,8 @@
     tokens_grad = reorder(True, tokens_grad, tokens_back, place["settled"], examples)
     memory_grad = reorder(True, memory_grad, memory_back, place["settled"], examples)
 
-    ffn_out_grad = finish(first, ("x", "zl"), place, ffn_out.shape)
-    ffn_in_grad = finish(second, ("zl", "zh"), place, ffn_in.shape)
+    ffn_out_grad = widen(first, ffn_out.shape)
+    ffn_in_grad = widen(second, ffn_in.shape)
     (
         key_cross_grad,
         value_cross_grad,

time: 706 us -> 620 us (0.88)
  waiting for transfers between devices: 113 us -> 69.3 us
  other arithmetic: 53.5 us -> 23.8 us
  Pallas kernels: 386 us -> 362 us
  local copies, waits for them, and re-layouts: 24.3 us -> 46.8 us
  matrix products: 85.4 us -> 64.6 us
  between operations: 4.43 us -> 17.4 us
    ppermute x35 -> x21, waiting for transfers between devices: 113 us -> 60.4 us  [permute(): return lax.ppermute(value, ('dp', 'mp'), pairs)]
    unnamed x149 -> x171, local copies, waits for them, and re-layouts: 16.6 us -> 40.6 us
    dot_general x8 -> x6, matrix products: 26.6 us -> 8.08 us  [nn(): return jnp.dot(left, right, preferred_element_type=jnp.float32)]
    concatenate x5 -> x0, other arithmetic: 18 us -> none  [the longest x1 8.26 us: on_chip_group(): head_parts = jnp.concatenate([head_parts, pieces(self_in_part)], axis=1)]
    pallas_call x1, Pallas kernels: 41.7 us -> 26.6 us  [cross_backward(): pl.pallas_call(cross_backward_kernel, grid=(examples, pairs), in_specs=[S...]
    pallas_call x6 -> x9, Pallas kernels: 231 us -> 245 us  [the longest x1 164 us: settle(): pl.pallas_call(functools.partial(settle_kernel, groups), in_specs=[pl.Blo...]
    pallas_call x1, Pallas kernels: 32.6 us -> 20.8 us  [cross_forward(): pl.pallas_call(cross_forward_kernel, grid=(examples, pairs), in_specs=[SM...]
    pallas_call x5 -> x4, Pallas kernels: 21.3 us -> 9.88 us  [reorder(): pl.pallas_call(functools.partial(reorder_kernel, inverse, examples), grid...]
  transfers between devices with their start and end apart: 35 -> 25, of which waited for: 12 -> 10; matrix products, arithmetic and copies ran while one was open for 20% -> 14% of each run, Pallas kernels for 42% -> 46%
where the time goes in v2:
time: 620 us; the launch traced here: 611 us
  Pallas kernels  362 us (58%)
  waiting for transfers between devices  69.3 us (11%)
  matrix products  64.6 us (10%)
  local copies, waits for them, and re-layouts  46.8 us (8%)
  starting transfers between devices  27.1 us (4%)
  other arithmetic  23.8 us (4%)
  between operations  17.4 us (3%)
    pallas_call x1, Pallas kernels, settle(): pl.pallas_call(functools.partial(settle_kernel, groups), in_specs=[pl.Blo...  164 us
    ppermute x21, waiting for transfers between devices, permute(): return lax.ppermute(value, ('dp', 'mp'), pairs)  60.4 us
    pallas_call x1, Pallas kernels, gather(): pl.pallas_call(functools.partial(gather_kernel, groups, examples), in_spe...  53.9 us
    unnamed x171, local copies, waits for them, and re-layouts  40.6 us
    dot_general x5, matrix products, tn(): lax.dot_general(left, right, (((0,), (0,)), ((), ())), preferred_element_...  31.3 us
    ppermute x21, starting transfers between devices, permute(): return lax.ppermute(value, ('dp', 'mp'), pairs)  26.8 us
    pallas_call x1, Pallas kernels, cross_backward(): pl.pallas_call(cross_backward_kernel, grid=(examples, pairs), in_specs=[S...  26.6 us
    dot_general x8, matrix products, nt(): lax.dot_general(left, right, (((1,), (1,)), ((), ())), preferred_element_...  24.9 us
  transfers between devices with their start and end apart: 25, of which 10 were waited for; matrix products, arithmetic and copies ran while one was open for 14% of the time, Pallas kernels for 46%

profile of v2, /device:TPU:6, one launch (start us, length us, event | category | flops | bytes accessed | tf_op | source)
XLA Modules:
  0.0 610.8 jit_solution(10173204523160056141)
XLA Ops:
  10.8 3.9 slice.70
  14.7 53.9 %shard_map.323 = (bf16[4,128,1024]{2,1,0:T(8,128)(2,1)S(1)}, bf16[512,1024]{1,0:T(8,128)(2,1)S(1)}, f32[8,128]{1,0:T(8,128)S(1)}, f32[8,128]{1,0:T(8,128)S(1)}, ...) custom-call(bf16[512,1024]{1,0:T(8,128)(2,1)} %tokens.1, ...), custom_call_target="tpu_custom_call" | custom-call | bytes 157286400 | tf_op jit(solution)/shard_map/pallas_call | solution.py:1074
  70.5 3.8 collective-permute-start.5
  81.2 3.6 convolution_convert_fusion
  84.8 8.1 %shard_map.324 = (bf16[2,512,512]{2,1,0:T(8,128)(2,1)S(1)}, f32[4,4,128,256]{3,2,1,0:T(8,128)S(1)}, f32[4,4,2,256]{3,2,1,0:T(2,128)S(1)}) custom-call(s32[5]{0:T(128)S(1)} %pad_add_fusion.info, bf16[2,512,1536]{2,1,0:T(8,128)(2,1)S(1)} %bitcast.164, f32[4,2,256]{2,1,0:T(2,128)S(1)} %fusion.55.bias), custom_call_target="tpu_custom_call" | custom-call | flops 4294967296 | bytes 12582912 | tf_op jit(solution)/shard_map/pallas_call | solution.py:684
  96.4 13.2 %collective-permute-done.5.refs_4_ = bf16[1536,1024]{1,0:T(8,128)(2,1)} collective-permute-done((bf16[1536,1024]{1,0:T(8,128)(2,1)}, bf16[1536,1024]{1,0:T(8,128)(2,1)}, u32[]{:S(2)}, u32[]{:S(2)}) %collective-permute-start.5) | collective-permute-done | bytes 3145760 | tf_op jit(solution)/shard_map/ppermute | solution.py:306
  121.0 3.6 collective-permute-start.7
  129.6 18.5 %shard_map.325 = (bf16[2,4,512,1024]{3,2,1,0:T(8,128)(2,1)S(1)}, bf16[2,4,512,1024]{3,2,1,0:T(8,128)(2,1)}) custom-call(s32[2]{0:T(128)S(1)} %pad_add_fusion.1.info, bf16[2048,1024]{1,0:T(8,128)(2,1)} %collective-permute-done.3.refs_0_, bf16[2048,1024]{1,0:T(8,128)(2,1)} %refs_1_.3, bf16[512,1024]{1,0:T(8,128)(2,1)S(1)} %copy-done.34, ...), custom_call_target="tpu_custom_call" | custom-call | flops 10737418240 | bytes 25165824 | tf_op jit(solution)/shard_map/pallas_call | solution.py:418
  156.2 20.8 %shard_map.326 = (bf16[2,512,512]{2,1,0:T(8,128)(2,1)S(1)}, f32[4,4,128,256]{3,2,1,0:T(8,128)S(1)}, f32[4,4,2,256]{3,2,1,0:T(2,128)S(1)}) custom-call(s32[4]{0:T(128)S(1)} %get-tuple-element.251.info, bf16[2,512,512]{2,1,0:T(8,128)(2,1)S(1)} %bitcast.166, bf16[2,2048,1024]{2,1,0:T(8,128)(2,1)S(1)} %bitcast.161), custom_call_target="tpu_custom_call" | custom-call | flops 8589934592 | bytes 16777216 | tf_op jit(solution)/shard_map/pallas_call | solution.py:755
  184.7 11.4 %shard_map.328 = (f32[512,1024]{1,0:T(8,128)S(1)}, f32[512,1024]{1,0:T(8,128)S(1)}, bf16[512,2048]{1,0:T(8,128)(2,1)S(1)}, bf16[512,2048]{1,0:T(8,128)(2,1)S(1)}) custom-call(bf16[512,1024]{1,0:T(8,128)(2,1)S(1)} %multiply_convert_fusion.normed.n_own, bf16[512,1024]{1,0:T(8,128)(2,1)S(1)} %fusion.22.grad.g_own, bf16[1024,2048]{1,0:T(8,128)(2,1)S(1)} %copy-done.28, ...), custom_call_target="tpu_custom_call" | custom-call | flops 8589934592 | bytes 14680064 | tf_op jit(solution)/shard_map/pallas_call | solution.py:847
  197.4 9.5 %collective-permute-done.10.normed.n_far = bf16[512,1024]{1,0:T(8,128)(2,1)S(1)} collective-permute-done((bf16[512,1024]{1,0:T(8,128)(2,1)S(1)}, bf16[512,1024]{1,0:T(8,128)(2,1)S(1)}, u32[]{:S(2)}, u32[]{:S(2)}) %collective-permute-start.10) | collective-permute-done | bytes 1048608 | tf_op jit(solution)/shard_map/ppermute | solution.py:306
  206.9 11.3 %shard_map.329 = (bf16[512,1024]{1,0:T(8,128)(2,1)S(1)}, bf16[512,1024]{1,0:T(8,128)(2,1)S(1)}, bf16[512,2048]{1,0:T(8,128)(2,1)S(1)}, bf16[512,2048]{1,0:T(8,128)(2,1)S(1)}) custom-call(bf16[512,1024]{1,0:T(8,128)(2,1)S(1)} %collective-permute-done.10.normed.n_far, bf16[512,1024]{1,0:T(8,128)(2,1)S(1)} %collective-permute-done.8.grad.g_far, ...), custom_call_target="tpu_custom_call" | custom-call | flops 8589934592 | bytes 14680064 | tf_op jit(solution)/shard_map/pallas_call | solution.py:847
  219.5 11.1 %shard_map.330 = (bf16[2048,1024]{1,0:T(8,128)(2,1)S(1)}, bf16[1024,2048]{1,0:T(8,128)(2,1)S(1)}) custom-call(bf16[512,1024]{1,0:T(8,128)(2,1)S(1)} %multiply_convert_fusion.normed.n_own, bf16[512,1024]{1,0:T(8,128)(2,1)S(1)} %collective-permute-done.10.normed.n_far, bf16[512,1024]{1,0:T(8,128)(2,1)S(1)} %fusion.22.grad.g_own, ...), custom_call_target="tpu_custom_call" | custom-call | flops 8589934592 | bytes 12582912 | tf_op jit(solution)/shard_map/pallas_call | solution.py:886
  234.6 9.0 %collective-permute-done.11 = bf16[512,1024]{1,0:T(8,128)(2,1)S(1)} collective-permute-done((bf16[512,1024]{1,0:T(8,128)(2,1)S(1)}, bf16[512,1024]{1,0:T(8,128)(2,1)S(1)}, u32[]{:S(2)}, u32[]{:S(2)}) %collective-permute-start.11) | collective-permute-done | bytes 1048608 | tf_op jit(solution)/shard_map/ppermute | solution.py:306
  257.6 3.8 copy-done.39
  261.4 26.6 %shard_map.331 = (bf16[2,512,512]{2,1,0:T(8,128)(2,1)S(1)}, bf16[2,2048,1024]{2,1,0:T(8,128)(2,1)S(1)}) custom-call(s32[4]{0:T(128)S(1)} %get-tuple-element.251.info, bf16[2,512,512]{2,1,0:T(8,128)(2,1)S(1)} %bitcast.167, bf16[2,2048,1024]{2,1,0:T(8,128)(2,1)S(1)} %bitcast.162, bf16[2,512,512]{2,1,0:T(8,128)(2,1)S(1)} %bitcast.168, ...), custom_call_target="tpu_custom_call" | custom-call | flops 21474836480 | bytes 25165824 | tf_op jit(solution)/shard_map/pallas_call | solution.py:783
  288.1 6.1 %fusion.6 = bf16[2048,1024]{1,0:T(8,128)(2,1)} fusion(bf16[1024,1024]{1,0:T(8,128)(2,1)S(1)} %copy-done.31, bf16[2,2048,1024]{2,1,0:T(8,128)(2,1)S(1)} %get-tuple-element.139, s32[]{:T(128)S(6)} %select_n.18), kind=kOutput, calls=%fused_computation.13 | convolution fusion | flops 4297064448 | bytes 10485764 | tf_op jit(solution)/shard_map/dot_general | solution.py:437
  294.3 14.9 %convolution_convert_fusion.1 = bf16[1024,1024]{1,0:T(8,128)(2,1)} fusion(bf16[4096,1024]{1,0:T(8,128)(2,1)} %bitcast.160, bf16[4096,1024]{1,0:T(8,128)(2,1)} %bitcast.163), kind=kOutput, calls=%fused_computation.51 | convolution fusion | flops 8590983168 | bytes 18874368 | tf_op jit(solution)/shard_map/dot_general | solution.py:443
  309.2 7.8 %add_convert_fusion = bf16[2048,1024]{1,0:T(8,128)(2,1)} fusion(bf16[2048,1024]{1,0:T(8,128)(2,1)} %collective-permute-done.14, bf16[1024,1024]{1,0:T(8,128)(2,1)S(1)} %copy-done.32, bf16[2,2048,1024]{2,1,0:T(8,128)(2,1)S(1)} %copy-done.41, s32[]{:T(128)S(6)} %select_n.17), kind=kOutput, calls=%fused_computation | convolution fusion | flops 4301258752 | bytes 14680068 | tf_op jit(solution)/shard_map/dot_general | solution.py:437
  324.4 3.7 bitcast_convert_fusion.3
  331.8 3.6 bitcast_convert_fusion.1
  341.6 12.0 %shard_map.332 = (bf16[2,512,1536]{2,1,0:T(8,128)(2,1)S(1)}, f32[4,2,256]{2,1,0:T(2,128)S(1)}) custom-call(s32[5]{0:T(128)S(1)} %pad_add_fusion.info, bf16[2,512,1536]{2,1,0:T(8,128)(2,1)S(1)} %bitcast.165, f32[4,2,256]{2,1,0:T(2,128)S(1)} %fusion.55.bias, bf16[2,512,512]{2,1,0:T(8,128)(2,1)S(1)} %bitcast.169, f32[4,4,128,256]{3,2,1,0:T(8,128)S(1)} %copy-done.49, ...), custom_call_target="tpu_custom_call" | custom-call | flops 10737418240 | bytes 18874368 | tf_op jit(solution)/shard_map/pallas_call | solution.py:720
  353.6 6.9 %bitcast_convert_fusion = bf16[1536,1024]{1,0:T(8,128)(2,1)} fusion(bf16[2,512,1536]{2,1,0:T(8,128)(2,1)S(1)} %get-tuple-element.163, bf16[1,512,1024]{2,1,0:T(8,128)(2,1)} %bitcast.6, bf16[1,512,1024]{2,1,0:T(8,128)(2,1)S(1)} %copy-done.63), kind=kOutput, calls=%fused_computation.1 | convolution fusion | flops 3223846912 | bytes 8388608 | tf_op jit(solution)/shard_map/dot_general | solution.py:443
  360.5 19.4 %collective-permute-done.18 = bf16[512,1024]{1,0:T(8,128)(2,1)S(1)} collective-permute-done((bf16[512,1024]{1,0:T(8,128)(2,1)S(1)}, bf16[512,1024]{1,0:T(8,128)(2,1)S(1)}, u32[]{:S(2)}, u32[]{:S(2)}) %collective-permute-start.18) | collective-permute-done | bytes 1048608 | tf_op jit(solution)/shard_map/ppermute | solution.py:306
  381.9 8.8 %reduce-scatter.5.cloned.1.call-done = bf16[64,2048]{1,0:T(8,128)(2,1)} async-done(((bf16[1024,2048]{1,0:T(8,128)(2,1)}), bf16[64,2048]{1,0:T(8,128)(2,1)}) %reduce-scatter.5.cloned.1.call-update) | async-done | bytes 262160 | tf_op jit(solution)/shard_map/reduce_scatter | solution.py:1603
  390.7 4.3 fusion.31
  408.7 163.9 %shard_map.333 = (bf16[16,256,1024]{2,1,0:T(8,128)(2,1)}, f32[2,8,1024]{2,1,0:T(8,128)S(1)}) custom-call(bf16[16,64,1024]{2,1,0:T(8,128)(2,1)S(1)} %bitcast.155, bf16[16,32,1024]{2,1,0:T(8,128)(2,1)S(1)} %bitcast.157, bf16[16,32,1024]{2,1,0:T(8,128)(2,1)S(1)} %bitcast.159, bf16[16,32,1024]{2,1,0:T(8,128)(2,1)S(1)} %bitcast.158, ...), custom_call_target="tpu_custom_call" | custom-call | bytes 251658240 | tf_op jit(solution)/shard_map/pallas_call | solution.py:1375
  572.6 3.4 copy-done.2
  576.0 6.0 shard_map.337
  585.7 4.1 shard_map.338
  590.5 4.1 shard_map.339
  598.8 5.0 shard_map.336
  (285 shorter events, 107.4 us)
Async XLA Ops:
  7.2 309.9 %reduce-scatter.3.cloned.1.call-start = ((), (), s32[]{:S(2)}) async-start(), calls=%async_computation.2 | async-start | bytes 4456448 | tf_op jit(solution)/shard_map/reduce_scatter | solution.py:1602
  14.7 59.7 %copy-start.77 = (bf16[1024]{0:T(1024)(128)(2,1)S(1)}, bf16[1024]{0:T(1024)(128)(2,1)}, u32[]{:S(2)}) copy-start(bf16[1024]{0:T(1024)(128)(2,1)} %param.25) | copy-start | bytes 6148
  70.5 42.1 %copy-start = (bf16[4,128,1024]{2,1,0:T(8,128)(2,1)}, bf16[4,128,1024]{2,1,0:T(8,128)(2,1)S(1)}, u32[]{:S(2)}) copy-start(bf16[4,128,1024]{2,1,0:T(8,128)(2,1)S(1)} %get-tuple-element.101) | copy-start | bytes 3145732
  70.5 42.1 %copy-start.16 = (bf16[512,1024]{1,0:T(8,128)(2,1)}, bf16[512,1024]{1,0:T(8,128)(2,1)S(1)}, u32[]{:S(2)}) copy-start(bf16[512,1024]{1,0:T(8,128)(2,1)S(1)} %get-tuple-element.107) | copy-start | bytes 3145732
  70.5 110.0 %copy-start.13 = (bf16[512,1024]{1,0:T(8,128)(2,1)}, bf16[512,1024]{1,0:T(8,128)(2,1)S(1)}, u32[]{:S(2)}) copy-start(bf16[512,1024]{1,0:T(8,128)(2,1)S(1)} %get-tuple-element.119) | copy-start | bytes 3145732
  70.5 39.1 %collective-permute-start.5 = (bf16[1536,1024]{1,0:T(8,128)(2,1)}, bf16[1536,1024]{1,0:T(8,128)(2,1)}, u32[]{:S(2)}, u32[]{:S(2)}) collective-permute-start(bf16[1536,1024]{1,0:T(8,128)(2,1)} %slice.70), channel_id=1, source_target_pairs={{1,2},{2,1},{5,6},{6,5},{9,10},{10,9},{13,14},{14,13},{17,18},{18,... | collective-permute-start | bytes 9437192 | tf_op jit(solution)/shard_map/ppermute | solution.py:306
  76.0 3.0 collective-permute-start
  76.0 53.6 %collective-permute-start.3 = (bf16[2048,1024]{1,0:T(8,128)(2,1)}, bf16[2048,1024]{1,0:T(8,128)(2,1)}, u32[]{:S(2)}, u32[]{:S(2)}) collective-permute-start(bf16[2048,1024]{1,0:T(8,128)(2,1)} %refs_1_.3), channel_id=1, source_target_pairs={{0,2},{3,1},{4,6},{7,5},{8,10},{11,9},{12,14},{15,13},{16,18},{19,... | collective-permute-start | bytes 12582920 | tf_op jit(solution)/shard_map/ppermute | solution.py:306
  92.9 20.7 %copy-start.26 = (bf16[2,512,512]{2,1,0:T(8,128)(2,1)}, bf16[2,512,512]{2,1,0:T(8,128)(2,1)S(1)}, u32[]{:S(2)}) copy-start(bf16[2,512,512]{2,1,0:T(8,128)(2,1)S(1)} %get-tuple-element.106) | copy-start | bytes 3145732
  93.7 19.0 %collective-permute-start.1 = (bf16[512,1024]{1,0:T(8,128)(2,1)S(1)}, bf16[512,1024]{1,0:T(8,128)(2,1)S(1)}, u32[]{:S(2)}, u32[]{:S(2)}) collective-permute-start(bf16[512,1024]{1,0:T(8,128)(2,1)S(1)} %convolution_convert_fusion.7), channel_id=1, source_target_pairs={{0,2},{1,3},{2,0},{3,1},{4,6},{5,7},{6,4},{7,5},{8,10},{9,11},{10,... | collective-permute-start | bytes 3145736 | tf_op jit(solution)/shard_map/ppermute | solution.py:306
  109.6 20.0 %collective-permute-start.6 = (bf16[1536,1024]{1,0:T(8,128)(2,1)}, bf16[1536,1024]{1,0:T(8,128)(2,1)}, u32[]{:S(2)}, u32[]{:S(2)}) collective-permute-start(bf16[1536,1024]{1,0:T(8,128)(2,1)} %collective-permute-done.5.refs_4_), channel_id=1, source_target_pairs={{1,3},{2,0},{5,7},{6,4},{9,11},{10,8},{13,15},{14,12},{17,19},{18,... | collective-permute-start | bytes 9437192 | tf_op jit(solution)/shard_map/ppermute | solution.py:306
  114.8 11.6 %collective-permute-start.2 = (bf16[512,1024]{1,0:T(8,128)(2,1)}, bf16[512,1024]{1,0:T(8,128)(2,1)}, u32[]{:S(2)}, u32[]{:S(2)}) collective-permute-start(bf16[512,1024]{1,0:T(8,128)(2,1)} %multiply_convert_fusion.1), channel_id=1, source_target_pairs={{0,2},{1,3},{2,0},{3,1},{4,6},{5,7},{6,4},{7,5},{8,10},{9,11},{10,... | collective-permute-start | bytes 3145736 | tf_op jit(solution)/shard_map/ppermute | solution.py:306
  115.6 14.0 %collective-permute-start.4 = (bf16[512,1024]{1,0:T(8,128)(2,1)S(1)}, bf16[512,1024]{1,0:T(8,128)(2,1)}, u32[]{:S(2)}, u32[]{:S(2)}) collective-permute-start(bf16[512,1024]{1,0:T(8,128)(2,1)S(1)} %copy-done.34), channel_id=1, source_target_pairs={{1,3},{2,0},{5,7},{6,4},{9,11},{10,8},{13,15},{14,12},{17,19},{18,... | collective-permute-start | bytes 3145736 | tf_op jit(solution)/shard_map/ppermute | solution.py:306
  121.0 27.2 %collective-permute-start.7 = (bf16[512,1024]{1,0:T(8,128)(2,1)S(1)}, bf16[512,1024]{1,0:T(8,128)(2,1)S(1)}, u32[]{:S(2)}, u32[]{:S(2)}) collective-permute-start(bf16[512,1024]{1,0:T(8,128)(2,1)S(1)} %copy-done.15), channel_id=1, source_target_pairs={{1,2},{2,1},{5,6},{6,5},{9,10},{10,9},{13,14},{14,13},{17,18},{18,... | collective-permute-start | bytes 3145736 | tf_op jit(solution)/shard_map/ppermute | solution.py:306
  149.2 27.8 %collective-permute-start.8 = (bf16[512,1024]{1,0:T(8,128)(2,1)S(1)}, bf16[512,1024]{1,0:T(8,128)(2,1)S(1)}, u32[]{:S(2)}, u32[]{:S(2)}) collective-permute-start(bf16[512,1024]{1,0:T(8,128)(2,1)S(1)} %fusion.22.grad.g_own), channel_id=1, source_target_pairs={{0,1},{1,0},{2,3},{3,2},{4,5},{5,4},{6,7},{7,6},{8,9},{9,8},{10,11... | collective-permute-start | bytes 3145736 | tf_op jit(solution)/shard_map/ppermute | solution.py:306
  153.7 23.3 %copy-start.44 = (bf16[1024,512]{1,0:T(8,128)(2,1)}, bf16[1024,512]{1,0:T(8,128)(2,1)S(1)}, u32[]{:S(2)}) copy-start(bf16[1024,512]{1,0:T(8,128)(2,1)S(1)} %convolution_convert_fusion.4) | copy-start | bytes 3145732
  177.7 2.7 collective-permute-start.9
  181.6 25.3 %collective-permute-start.10 = (bf16[512,1024]{1,0:T(8,128)(2,1)S(1)}, bf16[512,1024]{1,0:T(8,128)(2,1)S(1)}, u32[]{:S(2)}, u32[]{:S(2)}) collective-permute-start(bf16[512,1024]{1,0:T(8,128)(2,1)S(1)} %multiply_convert_fusion.normed.n_own), channel_id=1, source_target_pairs={{0,1},{1,0},{2,3},{3,2},{4,5},{5,4},{6,7},{7,6},{8,9},{9,8},{10,11... | collective-permute-start | bytes 3145736 | tf_op jit(solution)/shard_map/ppermute | solution.py:306
  219.2 24.4 %collective-permute-start.11 = (bf16[512,1024]{1,0:T(8,128)(2,1)S(1)}, bf16[512,1024]{1,0:T(8,128)(2,1)S(1)}, u32[]{:S(2)}, u32[]{:S(2)}) collective-permute-start(bf16[512,1024]{1,0:T(8,128)(2,1)S(1)} %get-tuple-element.125), channel_id=1, source_target_pairs={{0,1},{1,0},{2,3},{3,2},{4,5},{5,4},{6,7},{7,6},{8,9},{9,8},{10,11... | collective-permute-start | bytes 3145736 | tf_op jit(solution)/shard_map/ppermute | solution.py:306
  244.6 146.1 %reduce-scatter.5.cloned.1.call-start = ((), (), s32[]{:S(2)}) async-start(), calls=%async_computation.3 | async-start | bytes 4456448 | tf_op jit(solution)/shard_map/reduce_scatter | solution.py:1603
  249.9 3.2 collective-permute-start.12
  250.0 332.1 %all-gather.3.cloned.1.call-start = ((), (), s32[]{:S(2)}) async-start(), calls=%async_computation.4 | async-start | bytes 4456448 | tf_op jit(solution)/shard_map/all_gather | solution.py:1621
  256.4 31.6 %collective-permute-start.13 = (bf16[512,1024]{1,0:T(8,128)(2,1)S(1)}, bf16[512,1024]{1,0:T(8,128)(2,1)S(1)}, u32[]{:S(2)}, u32[]{:S(2)}) collective-permute-start(bf16[512,1024]{1,0:T(8,128)(2,1)S(1)} %copy-done.36), channel_id=1, source_target_pairs={{0,1},{1,0},{2,3},{3,2},{4,5},{5,4},{6,7},{7,6},{8,9},{9,8},{10,11... | collective-permute-start | bytes 3145736 | tf_op jit(solution)/shard_map/ppermute | solution.py:306
  261.4 26.7 %copy-start.31 = (bf16[1024,1024]{1,0:T(8,128)(2,1)S(1)}, bf16[1024,1024]{1,0:T(8,128)(2,1)}, u32[]{:S(2)}) copy-start(bf16[1024,1024]{1,0:T(8,128)(2,1)} %get-tuple-element.111.refs_6_) | copy-start | bytes 6291460
  294.2 15.0 %collective-permute-start.14 = (bf16[2048,1024]{1,0:T(8,128)(2,1)}, bf16[2048,1024]{1,0:T(8,128)(2,1)}, u32[]{:S(2)}, u32[]{:S(2)}) collective-permute-start(bf16[2048,1024]{1,0:T(8,128)(2,1)} %fusion.6), channel_id=1, source_target_pairs={{0,2},{1,3},{2,0},{3,1},{4,6},{5,7},{6,4},{7,5},{8,10},{9,11},{10,... | collective-permute-start | bytes 12582920 | tf_op jit(solution)/shard_map/ppermute | solution.py:306
  317.1 265.0 %all-gather.5.cloned.1.call-start = ((), (), s32[]{:S(2)}) async-start(), calls=%async_computation.5 | async-start | bytes 4456448 | tf_op jit(solution)/shard_map/all_gather | solution.py:1655
  318.1 2.7 collective-permute-start.15
  318.5 61.4 %collective-permute-start.17 = (bf16[2048,1024]{1,0:T(8,128)(2,1)}, bf16[2048,1024]{1,0:T(8,128)(2,1)S(1)}, u32[]{:S(2)}, u32[]{:S(2)}) collective-permute-start(bf16[2048,1024]{1,0:T(8,128)(2,1)} %add_convert_fusion), channel_id=1, source_target_pairs={{1,2},{2,1},{5,6},{6,5},{9,10},{10,9},{13,14},{14,13},{17,18},{18,... | collective-permute-start | bytes 12582920 | tf_op jit(solution)/shard_map/ppermute | solution.py:306
  324.0 11.4 %collective-permute-start.16 = (bf16[512,1024]{1,0:T(8,128)(2,1)S(1)}, bf16[512,1024]{1,0:T(8,128)(2,1)S(1)}, u32[]{:S(2)}, u32[]{:S(2)}) collective-permute-start(bf16[512,1024]{1,0:T(8,128)(2,1)S(1)} %get-tuple-element.242), channel_id=1, source_target_pairs={{0,2},{1,3},{2,0},{3,1},{4,6},{5,7},{6,4},{7,5},{8,10},{9,11},{10,... | collective-permute-start | bytes 3145736 | tf_op jit(solution)/shard_map/ppermute | solution.py:306
  328.8 51.1 %collective-permute-start.18 = (bf16[512,1024]{1,0:T(8,128)(2,1)S(1)}, bf16[512,1024]{1,0:T(8,128)(2,1)S(1)}, u32[]{:S(2)}, u32[]{:S(2)}) collective-permute-start(bf16[512,1024]{1,0:T(8,128)(2,1)S(1)} %add_convert_fusion.1), channel_id=1, source_target_pairs={{1,2},{2,1},{5,6},{6,5},{9,10},{10,9},{13,14},{14,13},{17,18},{18,... | collective-permute-start | bytes 3145736 | tf_op jit(solution)/shard_map/ppermute | solution.py:306
  395.1 2.7 collective-permute-start.19
  400.7 181.3 %collective-permute-start.20 = (bf16[512,1024]{1,0:T(8,128)(2,1)S(1)}, bf16[512,1024]{1,0:T(8,128)(2,1)}, u32[]{:S(2)}, u32[]{:S(2)}) collective-permute-start(bf16[512,1024]{1,0:T(8,128)(2,1)S(1)} %fusion.18), channel_id=1, source_target_pairs={{1,2},{2,1},{5,6},{6,5},{9,10},{10,9},{13,14},{14,13},{17,18},{18,... | collective-permute-start | bytes 3145736 | tf_op jit(solution)/shard_map/ppermute | solution.py:306
  (78 other events, 353.1 us)
Sparse Core Ops, SparseCore 0:
  244.7 70.0 reduce-scatter.2
  319.2 71.4 reduce-scatter.4
  392.8 53.8 all-gather.2
  448.7 82.0 all-gather.4

commit v3 on v2

--- a/solution.py
+++ b/solution.py
@@ -532,56 +532,6 @@
         self_store(core, result, out_scratch, out, example)
 
 
-def self_backward_kernel(
-    examples,
-    info,
-    rows,
-    bias,
-    grads,
-    mixed,
-    level,
-    out,
-    out_bias,
-    scratch,
-    grad_scratch,
-    out_scratch,
-):
-    core = info[0]
-    size = scratch.shape[1]
-    slopes = jnp.concatenate(
-        [toeplitz(bias[0, head : head + 1, :], size) for head in range(2)], axis=1
-    )
-    sums = None
-    for example in range(examples):
-        joined = self_heads(core, rows, scratch, example)
-        query, keys, values = joined[:, :128], joined[:, 128:256], joined[:, 256:]
-        grad = self_heads(core, grads, grad_scratch, example)
-        products = grad.astype(jnp.float32).T * mixed[0, example]
-        inner = jnp.concatenate(
-            [jnp.sum(head_rows(products, head), axis=0, keepdims=True) for head in range(2)],
-            axis=1,
-        )
-        levels = jnp.concatenate([level[0, example, 0:1, :], level[0, example, 1:2, :]], axis=1)
-        mask = self_masks(size, info[1 + example])
-        heads, grad_heads = side_by_side(query), side_by_side(grad)
-        scores = nt(keys, heads) + slopes + jnp.concatenate([mask, mask], axis=1)
-        probs = jnp.exp(scores - levels)
-        grad_scores = (probs * (nt(values, grad_heads) - inner)).astype(jnp.bfloat16)
-        square = grad_scores.astype(jnp.float32)
-        sums = square if sums is None else sums + square
-        result = jnp.concatenate(
-            [
-                heads_joined(*own_blocks(nn(keys.T, grad_scores), size)),
-                nn(grad_scores, heads),
-                nn(probs.astype(jnp.bfloat16), grad_heads),
-            ],
-            axis=1,
-        ).astype(jnp.bfloat16)
-        self_store(core, result, out_scratch, out, example)
-    for head in range(2):
-        out_bias[0, head : head + 1, :] = diagonals(sums[:, size * head : size * (head + 1)])
-
-
 def by_length(length, span, body):
     quarter = span // 4
     for part in range(1, 5):
@@ -712,41 +662,6 @@
     )(info, rows, bias)
 
 
-def self_backward(info, rows, bias, grads, mixed, level, examples):
-    _, count, width = rows.shape
-    pairs, size = width // 384, count // examples
-    row = pl.BlockSpec((1, 2, 2 * size), lambda h: (h, 0, 0))
-    wide = pl.BlockSpec((2, count, 384), lambda h: (0, 0, h))
-    return pl.pallas_call(
-        functools.partial(self_backward_kernel, examples),
-        grid=(pairs,),
-        in_specs=[
-            SMEM_SPEC,
-            wide,
-            row,
-            pl.BlockSpec((2, count, 128), lambda h: (0, 0, h)),
-            pl.BlockSpec((1, examples, 128, 2 * size), lambda h: (h, 0, 0, 0)),
-            pl.BlockSpec((1, examples, 2, 2 * size), lambda h: (h, 0, 0, 0)),
-        ],
-        out_specs=[wide, row],
-        out_shape=[
-            jax.ShapeDtypeStruct(rows.shape, jnp.bfloat16),
-            jax.ShapeDtypeStruct((pairs, 2, 2 * size), jnp.float32),
-        ],
-        scratch_shapes=[
-            pltpu.VMEM((examples, 2 * size, 384), jnp.bfloat16),
-            pltpu.VMEM((examples, 2 * size, 128), jnp.bfloat16),
-            pltpu.VMEM((examples, 2 * size, 384), jnp.bfloat16),
-        ],
-        cost_estimate=cost(
-            5 * 2 * examples * 2 * pairs * (2 * size) ** 2 * 256 * 2,
-            12 * rows.size,
-            examples * 2 * pairs * (2 * size) ** 2,
-        ),
-        compiler_params=pltpu.CompilerParams(vmem_limit_bytes=ATTEND_VMEM),
-    )(info, rows, bias, grads, mixed, level)
-
-
 def cross_forward(info, queries, kv, examples):
     _, count, width = queries.shape
     pairs, size, span = width // 128, count // examples, kv.shape[1] // examples
@@ -859,43 +774,33 @@
     )(normed, grad, into, outof)
 
 
-def ffn_weights_kernel(
-    n_own, n_far, g_own, g_far, h_own, h_far, p_own, p_far, outof_grad, into_grad, turned
-):
-    half = n_own.shape[0]
-
-    @pl.when(pl.program_id(0) == 0)
+def ffn_weights_kernel(n_own, n_far, g_own, g_far, h_own, h_far, p_own, p_far, out):
+    step = pl.program_id(0)
+    half = pl.num_programs(0) // 2
+
+    @pl.when(step < half)
     def _():
-        turned[:, :half] = n_own[...].T
-        turned[:, half:] = n_far[...].T
-
-    outof_grad[...] = (tn(h_own[...], g_own[...]) + tn(h_far[...], g_far[...])).astype(
-        jnp.bfloat16
-    )
-    into_grad[...] = (
-        nn(turned[:, :half], p_own[...]) + nn(turned[:, half:], p_far[...])
-    ).astype(jnp.bfloat16)
+        out[...] = (tn(h_own[...], g_own[...]) + tn(h_far[...], g_far[...])).astype(out.dtype)
+
+    @pl.when(step >= half)
+    def _():
+        out[...] = (tn(p_own[...], n_own[...]) + tn(p_far[...], n_far[...])).astype(out.dtype)
 
 
 def ffn_weights(normed, grads, hiddens, pres):
     rows, width = normed[0].shape
     units = hiddens[0].shape[1]
     tile = 512
+    steps = units // tile
     whole = pl.BlockSpec((rows, width), lambda i: (0, 0))
-    thin = pl.BlockSpec((rows, tile), lambda i: (0, i))
+    first = pl.BlockSpec((rows, tile), lambda i: (0, jnp.minimum(i, steps - 1)))
+    second = pl.BlockSpec((rows, tile), lambda i: (0, jnp.maximum(i - steps, 0)))
     return pl.pallas_call(
         ffn_weights_kernel,
-        grid=(units // tile,),
-        in_specs=[whole] * 4 + [thin] * 4,
-        out_specs=[
-            pl.BlockSpec((tile, width), lambda i: (i, 0)),
-            pl.BlockSpec((width, tile), lambda i: (0, i)),
-        ],
-        out_shape=[
-            jax.ShapeDtypeStruct((units, width), jnp.bfloat16),
-            jax.ShapeDtypeStruct((width, units), jnp.bfloat16),
-        ],
-        scratch_shapes=[pltpu.VMEM((width, 2 * rows), jnp.bfloat16)],
+        grid=(2 * steps,),
+        in_specs=[whole] * 4 + [first] * 2 + [second] * 2,
+        out_specs=pl.BlockSpec((tile, width), lambda i: (i, 0)),
+        out_shape=jax.ShapeDtypeStruct((2 * units, width), jnp.bfloat16),
         cost_estimate=cost(
             4 * 2 * rows * width * units, 8 * rows * width + 4 * width * units
         ),
@@ -1110,39 +1015,17 @@
     return lax.dynamic_index_in_dim(value, index, 0, keepdims=False)
 
 
-axis_of = {"zh": 0, "zl": 1, "x": 2, "core": 3}
-
-
-def part_sent(total, name, place):
-    return lax.dynamic_index_in_dim(total, 1 - place[name], axis_of[name])
-
-
-def part_out(total, name, place, net):
-    return permute(part_sent(total, name, place), net[name])
-
-
-def part_in(total, arrived, name, place):
-    kept = lax.dynamic_index_in_dim(total, place[name], axis_of[name])
-    return add_low(kept, arrived)
-
-
-def halve(total, name, place, net):
-    return part_in(total, part_out(total, name, place, net), name, place)
-
-
-def by_device(value):
-    return value.reshape(2, 2, 2, 2, value.shape[0] // 16, value.shape[1])
-
-
 def tie(*values):
     return lax.optimization_barrier(values)
 
 
-def settle_kernel(groups, *refs):
-    count = len(refs) - 13
-    parts, small, refs = refs[:count], refs[count], refs[count + 1 :]
-    out, small_out, value, first, second, third, small_in = refs[:7]
-    send, receive, small_send, small_get, load = refs[7:]
+def settle_kernel(groups, examples, *refs):
+    parts, small, info, qkv = refs[:4], refs[4], refs[5], refs[6]
+    bias, grads, mixed, level, normed, self_in, tok, grad_rest, gain = refs[7:16]
+    out, small_out, tok_grad, tok_back = refs[16:20]
+    value, first, second, third, small_in, rows_held, placed, grad_placed, result = refs[20:29]
+    far_sent, far_found, send, receive, small_send, small_get, load, single = refs[29:]
+    count = len(parts)
     index, y = lax.axis_index("dp"), lax.axis_index("mp")
     core, x, z = index % 2, (index // 2) % 2, index // 4
     deep = groups // 4
@@ -1154,6 +1037,8 @@
     def part(k):
         return pl.ds(pl.multiple_of(k * rows, rows), rows)
 
+    fetch = pltpu.make_async_copy(qkv, rows_held, load.at[count])
+    fetch.start()
     loads, starts = [], [0]
     for i, ref in enumerate(parts):
         size = ref.shape[1]
@@ -1229,8 +1114,8 @@
     rounds.append(at(1 - core, y, x, z))
     small_out[0] = small[...]
 
-    def small_round(i):
-        swap = pltpu.make_async_remote_copy(
+    def small_copy(i):
+        return pltpu.make_async_remote_copy(
             src_ref=small_out.at[0],
             dst_ref=small_in.at[i],
             send_sem=small_send.at[i],
@@ -1238,14 +1123,100 @@
             device_id=rounds[i],
             device_id_type=MESH,
         )
-        swap.start()
-        swap.wait()
+
+    def small_wait(i):
+        small_copy(i).wait()
         if i < len(rounds) - 1:
             small_out[0] = small_out[0] + small_in[i]
         else:
             small_out[1] = small_in[i]
 
-    small_round(0)
+    def single_copy(i, source, target, device):
+        return pltpu.make_async_remote_copy(
+            src_ref=source,
+            dst_ref=target,
+            send_sem=single.at[i, 0],
+            recv_sem=single.at[i, 1],
+            device_id=device,
+            device_id_type=MESH,
+        )
+
+    far_copy = single_copy(0, far_sent, far_found, at(1 - core, y, x, z))
+    turn_copy = single_copy(1, tok_grad, tok_back, at(1 - core, 1 - y, x, z))
+    width = tok.shape[1]
+
+    def attend(pair):
+        size = placed.shape[1]
+        half = size // 2
+        columns = slice(384 * pair, 384 * (pair + 1))
+        near = pl.ds(pl.multiple_of(core * half, half), half)
+        away = pl.ds(pl.multiple_of((1 - core) * half, half), half)
+        slopes = jnp.concatenate(
+            [toeplitz(bias[pair, head : head + 1, :], size) for head in range(2)], axis=1
+        )
+        sums = None
+        for example in range(examples):
+            held = slice(half * example, half * (example + 1))
+            placed[example, near, :] = rows_held[0, held, columns]
+            placed[example, away, :] = rows_held[1, held, columns]
+            grad_placed[example, near, :] = grads[0, held, 128 * pair : 128 * (pair + 1)]
+            grad_placed[example, away, :] = grads[1, held, 128 * pair : 128 * (pair + 1)]
+            joined, grad = placed[example], grad_placed[example]
+            query, keys, values = joined[:, :128], joined[:, 128:256], joined[:, 256:]
+            products = grad.astype(jnp.float32).T * mixed[pair, example]
+            inner = jnp.concatenate(
+                [jnp.sum(head_rows(products, head), axis=0, keepdims=True) for head in range(2)],
+                axis=1,
+            )
+            levels = jnp.concatenate(
+                [level[pair, example, 0:1, :], level[pair, example, 1:2, :]], axis=1
+            )
+            mask = self_masks(size, info[example])
+            heads, grad_heads = side_by_side(query), side_by_side(grad)
+            scores = nt(keys, heads) + slopes + jnp.concatenate([mask, mask], axis=1)
+            probs = jnp.exp(scores - levels)
+            grad_scores = (probs * (nt(values, grad_heads) - inner)).astype(jnp.bfloat16)
+            square = grad_scores.astype(jnp.float32)
+            sums = square if sums is None else sums + square
+            result[example] = jnp.concatenate(
+                [
+                    heads_joined(*own_blocks(nn(keys.T, grad_scores), size)),
+                    nn(grad_scores, heads),
+                    nn(probs.astype(jnp.bfloat16), grad_heads),
+                ],
+                axis=1,
+            ).astype(jnp.bfloat16)
+            rows_held[0, held, columns] = result[example, near, :]
+            rows_held[1, held, columns] = result[example, away, :]
+        for head in range(2):
+            at_column = 512 * (pair % 2) + 256 * head
+            small_out[0, 4 + pair // 2 : 5 + pair // 2, at_column : at_column + size] = diagonals(
+                sums[:, size * head : size * (head + 1)]
+            )
+        both_rows = rows_held[:, :, columns].reshape(-1, 384)
+        piece = tn(both_rows, normed[...].reshape(-1, width)).astype(jnp.bfloat16)
+        value[4 * pair : 4 * pair + 4, starts[count] :, :] = piece.reshape(4, 96, width)
+
+    def heads_sent():
+        lax.fori_loop(starts[count] // rows, chunks, start, 0)
+        far_sent[...] = nt(rows_held[1], self_in[...]).astype(jnp.bfloat16)
+        far_copy.start()
+
+    def tokens_done():
+        far_copy.wait()
+        back = nt(rows_held[0], self_in[...]) + far_found[...].astype(jnp.float32)
+        held = tok[...].astype(jnp.float32)
+        size = lax.rsqrt(jnp.mean(held * held, axis=-1, keepdims=True) + epsilon)
+        small_out[0, 0:1, :] = jnp.sum(back * held * size, axis=0, keepdims=True)
+        back = back * gain[...]
+        inner = jnp.mean(back * held, axis=-1, keepdims=True)
+        back = back * size - held * (size * size * size * inner)
+        tok_grad[...] = (grad_rest[...] + back).astype(jnp.bfloat16)
+        small_copy(0).start()
+
+        @pl.when(core != y)
+        def _():
+            turn_copy.start()
 
     def start(k, carry):
         @pl.when(core == y)
@@ -1262,13 +1233,24 @@
     for i in range(count):
         loads[i].wait()
         lax.fori_loop(starts[i] // rows, starts[i + 1] // rows, start, 0)
-    for i in range(1, len(rounds)):
-        small_round(i)
+    fetch.wait()
 
     def total(left, right):
         return (left.astype(jnp.float32) + right.astype(jnp.float32)).astype(jnp.bfloat16)
 
+    pairs = bias.shape[0]
+    work = [functools.partial(attend, pair) for pair in range(pairs)] + [heads_sent, tokens_done]
+
     def tick(t, carry):
+        for i, piece_of_work in enumerate(work):
+            pl.when(t == i)(piece_of_work)
+        for i in range(len(rounds) - 1):
+
+            @pl.when(t == chunks + 1 + i)
+            def _():
+                small_wait(i)
+                small_copy(i + 1).start()
+
         @pl.when(t < chunks)
         def _():
             k = jnp.minimum(t, chunks - 1)
@@ -1341,6 +1323,12 @@
         return carry
 
     lax.fori_loop(0, chunks + 5, tick, 0)
+    small_wait(len(rounds) - 1)
+
+    @pl.when(core != y)
+    def _():
+        turn_copy.wait()
+
 
     def finish_sends(k, carry):
         @pl.when(core == y)
@@ -1363,22 +1351,28 @@
     lax.fori_loop(0, chunks, finish_sends, 0)
 
 
-def settle(parts, small, groups):
+def settle(parts, small, info, attention, rows_in, groups, examples):
+    qkv, bias, grads, mixed, level = attention
+    normed, self_in, tok, grad_rest, gain = rows_in
     count, _, width = parts[0].shape
     kind = parts[0].dtype
-    rows = sum(part.shape[1] for part in parts)
+    rows = sum(part.shape[1] for part in parts) + qkv.shape[2] // count
     chunk = 16
     chunks = rows // chunk
     deep = groups // 4
     rounds = 3 + deep.bit_length() - 1
+    size = 2 * qkv.shape[1] // examples
     whole = pl.BlockSpec(memory_space=pltpu.VMEM)
+    anywhere = pl.BlockSpec(memory_space=pl.ANY)
     return pl.pallas_call(
-        functools.partial(settle_kernel, groups),
-        in_specs=[pl.BlockSpec(memory_space=pl.ANY)] * len(parts) + [whole],
-        out_specs=[whole, whole],
+        functools.partial(settle_kernel, groups, examples),
+        in_specs=[anywhere] * len(parts) + [whole, SMEM_SPEC, anywhere] + [whole] * 9,
+        out_specs=[whole] * 4,
         out_shape=[
             jax.ShapeDtypeStruct((count, rows, width), kind),
             jax.ShapeDtypeStruct((2,) + small.shape, small.dtype),
+            jax.ShapeDtypeStruct(tok.shape, tok.dtype),
+            jax.ShapeDtypeStruct(tok.shape, tok.dtype),
         ],
         scratch_shapes=[
             pltpu.VMEM((count, rows, width), kind),
@@ -1386,17 +1380,24 @@
             pltpu.VMEM((chunks, deep, chunk, width), kind),
             pltpu.VMEM((chunks, deep - 1, chunk, width), kind),
             pltpu.VMEM((rounds,) + small.shape, small.dtype),
+            pltpu.VMEM(qkv.shape, kind),
+            pltpu.VMEM((examples, size, 384), kind),
+            pltpu.VMEM((examples, size, 128), kind),
+            pltpu.VMEM((examples, size, 384), kind),
+            pltpu.VMEM(tok.shape, kind),
+            pltpu.VMEM(tok.shape, kind),
             pltpu.SemaphoreType.DMA((chunks, 12)),
             pltpu.SemaphoreType.DMA((chunks, 12)),
             pltpu.SemaphoreType.DMA((rounds,)),
             pltpu.SemaphoreType.DMA((rounds,)),
-            pltpu.SemaphoreType.DMA((len(parts),)),
+            pltpu.SemaphoreType.DMA((len(parts) + 1,)),
+            pltpu.SemaphoreType.DMA((2, 2)),
         ],
         cost_estimate=cost(0, 60 * count * rows * width),
         compiler_params=pltpu.CompilerParams(
-            collective_id=0, has_side_effects=True, vmem_limit_bytes=SETTLE_VMEM
+            collective_id=0, has_side_effects=True, vmem_limit_bytes=62 * MIB
         ),
-    )(*parts, small)
+    )(*parts, small, info, qkv, bias, grads, mixed, level, normed, self_in, tok, grad_rest, gain)
 
 
 def unpack_kernel(pairs, source, key, val, cross_out, self_out, cross_q, *self_in):
@@ -1437,23 +1438,33 @@
     )(value)
 
 
-def widen_kernel(source, target):
-    target[...] = source[...].astype(jnp.float32)
-
-
-def widen(value, shape):
-    rows, width = shape
-    block = rows // 4
-    spec = pl.BlockSpec((block, width), lambda i: (i, 0))
+def widen_kernel(first, second, out_first, out_second):
+    out_first[...] = first[...].astype(jnp.float32)
+    out_second[...] = second[...].astype(jnp.float32).T
+
+
+def widen(value):
+    rows, width = value.shape[0] // 2, value.shape[1]
+    steps = 4
+    block = rows // steps
     return pl.pallas_call(
         widen_kernel,
-        grid=(4,),
-        in_specs=[spec],
-        out_specs=spec,
-        out_shape=jax.ShapeDtypeStruct(shape, jnp.float32),
-        cost_estimate=cost(0, 6 * rows * width),
+        grid=(steps,),
+        in_specs=[
+            pl.BlockSpec((block, width), lambda i: (i, 0)),
+            pl.BlockSpec((block, width), lambda i: (steps + i, 0)),
+        ],
+        out_specs=[
+            pl.BlockSpec((block, width), lambda i: (i, 0)),
+            pl.BlockSpec((width, block), lambda i: (0, i)),
+        ],
+        out_shape=[
+            jax.ShapeDtypeStruct((rows, width), jnp.float32),
+            jax.ShapeDtypeStruct((width, rows), jnp.float32),
+        ],
+        cost_estimate=cost(0, 12 * rows * width),
         compiler_params=pltpu.CompilerParams(vmem_limit_bytes=ATTEND_VMEM),
-    )(value.reshape(shape))
+    )(value, value)
 
 
 def pieces(value):
@@ -1595,12 +1606,9 @@
     out_own, n3_far = tie(out_own, n3_far)
     out_far, dn_far, h_far, p_far = ffn_rows(n3_far, gy_far, ffn_in, ffn_out, jnp.bfloat16)
     dn_far = permute(dn_far, net["y"])
-    ffn_out_part, ffn_in_part = ffn_weights(
-        (n3, n3_far), (gy, gy_far), (h_own, h_far), (p_own, p_far)
-    )
-    dn_far, ffn_out_part = tie(dn_far, ffn_out_part)
-    first = lax.psum_scatter(ffn_out_part, "dp", scatter_dimension=0, tiled=True)
-    second = lax.psum_scatter(ffn_in_part, "dp", scatter_dimension=0, tiled=True)
+    ffn_part = ffn_weights((n3, n3_far), (gy, gy_far), (h_own, h_far), (p_own, p_far))
+    dn_far, ffn_part = tie(dn_far, ffn_part)
+    ffn_piece = lax.psum_scatter(ffn_part, "dp", scatter_dimension=0, tiled=True)
     dn3 = dn_own + dn_far.astype(jnp.float32)
     back, gain_three = norm_backward(r2, norm_ffn, dn3)
     dr2 = dy + back
@@ -1617,8 +1625,7 @@
     cross_kv_part = low(tn(flat(mem), flat(dkv)))
     dkv_swapped, cross_kv_part = tie(dkv_swapped, cross_kv_part)
     memory_grad = low(nt(pick(dkv, core), cross_kv) + dkv_swapped.astype(jnp.float32))
-    memory_grad, cross_kv_part, dq2, first = tie(memory_grad, cross_kv_part, dq2, first)
-    first = lax.all_gather(first, "dp", axis=0, tiled=True)
+    memory_grad, cross_kv_part, dq2 = tie(memory_grad, cross_kv_part, dq2)
     memory_back = turn(memory_grad)
     dn2 = nt(dq2[0], cross_q) + swap(low(nt(dq2[1], cross_q))).astype(jnp.float32)
     back, gain_two = norm_backward(r1, norm_cross, dn2)
@@ -1630,42 +1637,32 @@
     self_out_part = low(tn(flat(a1), flat(g1)))
     da1 = low(nt(flat(g1), self_out)).reshape(2, rows, -1)
     head_parts = [cross_kv_part, cross_out_part, self_out_part, cross_q_part]
-    da1, head_parts = tie(da1, head_parts)
-    dqkv, by_distance = self_backward(
-        self_info, qkv, bias, da1, mixed_one, level_one, examples
-    )
-    self_in_part = low(tn(flat(dqkv), flat(n1)))
-    dqkv, self_in_part, memory_back, block_back = tie(
-        dqkv, self_in_part, memory_back, block_back
-    )
-    dn1 = nt(dqkv[0], self_in) + swap(low(nt(dqkv[1], self_in))).astype(jnp.float32)
-    back, gain_one = norm_backward(tok_float, norm_self, dn1)
-    tokens_grad = low(dr1 + back)
-    tokens_back = turn(tokens_grad)
-
-    bias_part = jnp.einsum(
-        "hd,db->bh", by_distance.reshape(-1, span), level_hot, precision=highest
-    )
-    bias_row = jnp.pad(bias_part.reshape(1, -1), ((0, 0), (0, width - bias_part.size)))
-    small = jnp.concatenate(
-        [gain_one[None], gain_two[None], gain_three[None], bias_row, jnp.zeros((4, width))], axis=0
-    )
-    head_parts = [pieces(part) for part in head_parts + [self_in_part]]
-    head_parts, second = tie(head_parts, second)
-    second = lax.all_gather(second, "dp", axis=0, tiled=True)
-    heads_done, small = settle(head_parts, small, groups)
-    small, first, second, block_back, tokens_back, memory_back = tie(
-        small, first, second, block_back, tokens_back, memory_back
-    )
+    head_parts = [pieces(part) for part in head_parts]
+    zero = jnp.zeros((1, width), jnp.float32)
+    small = jnp.concatenate([zero, gain_two[None], gain_three[None], jnp.tile(zero, (5, 1))])
+    da1, head_parts, small, ffn_piece, block_back = tie(
+        da1, head_parts, small, ffn_piece, block_back
+    )
+    ffn_whole = lax.all_gather(ffn_piece, "dp", axis=0, tiled=True)
+
+    heads_done, small, tokens_grad, tokens_back = settle(
+        head_parts,
+        small,
+        target_len,
+        (qkv, bias, da1, mixed_one, level_one),
+        (n1, self_in, tok, dr1, norm_self.astype(jnp.float32)[None]),
+        groups,
+        examples,
+    )
+    small, ffn_whole, block_back, memory_back = tie(small, ffn_whole, block_back, memory_back)
     gains = small[0, :3] + small[1, :3]
-    bias_sum = jnp.where(settled == 1, small[0, 3], small[1, 3])
-    bias_grad = bias_sum[: bias_part.size].reshape(bias_part.shape)
+    by_distance = jnp.where(settled == 1, small[0, 4:6], small[1, 4:6]).reshape(-1, span)
+    bias_grad = jnp.einsum("hd,db->bh", by_distance, level_hot, precision=highest)
     block_out = reorder(True, block_out, block_back, place["settled"], examples)
     tokens_grad = reorder(True, tokens_grad, tokens_back, place["settled"], examples)
     memory_grad = reorder(True, memory_grad, memory_back, place["settled"], examples)
 
-    ffn_out_grad = widen(first, ffn_out.shape)
-    ffn_in_grad = widen(second, ffn_in.shape)
+    ffn_out_grad, ffn_in_grad = widen(ffn_whole)
     (
         key_cross_grad,
         value_cross_grad,

time: 620 us -> 584 us (0.942)
  local copies, waits for them, and re-layouts: 46.8 us -> 35 us
  matrix products: 64.6 us -> 53.1 us
  waiting for transfers between devices: 69.3 us -> 60.4 us
    ppermute x21 -> x19, waiting for transfers between devices: 60.4 us -> 43.7 us  [permute(): return lax.ppermute(value, ('dp', 'mp'), pairs)]
    unnamed x171 -> x138, local copies, waits for them, and re-layouts: 40.6 us -> 28.9 us
    reduce_scatter x2 -> x1, waiting for transfers between devices: 8.78 us -> 16.7 us  [on_chip_group(): lax.psum_scatter(ffn_part, 'dp', scatter_dimension=0, tiled=True)]
    dot_general x5 -> x4, matrix products: 31.3 us -> 24.4 us  [tn(): lax.dot_general(left, right, (((0,), (0,)), ((), ())), preferred_element_...]
    dot_general x8 -> x6, matrix products: 24.9 us -> 19.7 us  [nt(): lax.dot_general(left, right, (((1,), (1,)), ((), ())), preferred_element_...]
    pallas_call x5 -> x3, Pallas kernels: 195 us -> 199 us  [the longest x1 181 us: settle(): pl.pallas_call(functools.partial(settle_kernel, groups, examples), in_spe...]
    ppermute x21 -> x19, starting transfers between devices: 26.8 us -> 27.7 us  [permute(): return lax.ppermute(value, ('dp', 'mp'), pairs)]
  transfers between devices with their start and end apart: 25 -> 21, of which waited for: 10 -> 9; matrix products, arithmetic and copies ran while one was open for 14% -> 12% of each run, Pallas kernels for 46% -> 48%
where the time goes in v3:
time: 584 us; the launch traced here: 577 us
  Pallas kernels  358 us (61%)
  waiting for transfers between devices  60.4 us (10%)
  matrix products  53.1 us (9%)
  local copies, waits for them, and re-layouts  35 us (6%)
  starting transfers between devices  27.7 us (5%)
  other arithmetic  25.1 us (4%)
  between operations  17.2 us (3%)
    pallas_call x1, Pallas kernels, settle(): pl.pallas_call(functools.partial(settle_kernel, groups, examples), in_spe...  181 us
    pallas_call x1, Pallas kernels, gather(): pl.pallas_call(functools.partial(gather_kernel, groups, examples), in_spe...  54 us
    ppermute x19, waiting for transfers between devices, permute(): return lax.ppermute(value, ('dp', 'mp'), pairs)  43.7 us
    unnamed x138, local copies, waits for them, and re-layouts  28.9 us
    ppermute x19, starting transfers between devices, permute(): return lax.ppermute(value, ('dp', 'mp'), pairs)  27.7 us
    dot_general x4, matrix products, tn(): lax.dot_general(left, right, (((0,), (0,)), ((), ())), preferred_element_...  24.4 us
    pallas_call x2, Pallas kernels, ffn_rows(): pl.pallas_call(ffn_rows_kernel, grid=(units // tile,), in_specs=[whole, w...  23.6 us
    pallas_call x1, Pallas kernels, cross_backward(): pl.pallas_call(cross_backward_kernel, grid=(examples, pairs), in_specs=[S...  21.1 us
  transfers between devices with their start and end apart: 21, of which 9 were waited for; matrix products, arithmetic and copies ran while one was open for 12% of the time, Pallas kernels for 48%

profile of v3, /device:TPU:6, one launch (start us, length us, event | category | flops | bytes accessed | tf_op | source)
XLA Modules:
  0.0 577.1 jit_solution(4660740117478077691)
XLA Ops:
  10.8 3.9 slice.57
  14.7 54.0 %shard_map.323 = (bf16[4,128,1024]{2,1,0:T(8,128)(2,1)S(1)}, bf16[512,1024]{1,0:T(8,128)(2,1)S(1)}, f32[8,128]{1,0:T(8,128)S(1)}, f32[8,128]{1,0:T(8,128)S(1)}, ...) custom-call(bf16[512,1024]{1,0:T(8,128)(2,1)} %tokens.1, ...), custom_call_target="tpu_custom_call" | custom-call | bytes 157286400 | tf_op jit(solution)/shard_map/pallas_call | solution.py:979
  70.6 3.8 collective-permute-start.5
  81.3 3.6 convolution_convert_fusion
  85.0 8.0 %shard_map.324 = (bf16[2,512,512]{2,1,0:T(8,128)(2,1)S(1)}, f32[4,4,128,256]{3,2,1,0:T(8,128)S(1)}, f32[4,4,2,256]{3,2,1,0:T(2,128)S(1)}) custom-call(s32[5]{0:T(128)S(1)} %pad_add_fusion.info, bf16[2,512,1536]{2,1,0:T(8,128)(2,1)S(1)} %bitcast.135, f32[4,2,256]{2,1,0:T(2,128)S(1)} %fusion.39.bias.refs_7_), custom_call_target="tpu_custom_call" | custom-call | flops 4294967296 | bytes 12582912 | tf_op jit(solution)/shard_map/pallas_call | solution.py:634
  96.2 13.6 %collective-permute-done.5.refs_4_ = bf16[1536,1024]{1,0:T(8,128)(2,1)} collective-permute-done((bf16[1536,1024]{1,0:T(8,128)(2,1)}, bf16[1536,1024]{1,0:T(8,128)(2,1)}, u32[]{:S(2)}, u32[]{:S(2)}) %collective-permute-start.5) | collective-permute-done | bytes 3145760 | tf_op jit(solution)/shard_map/ppermute | solution.py:306
  121.1 3.6 collective-permute-start.7
  126.6 3.1 pad_maximum_fusion.1
  129.7 18.5 %shard_map.325 = (bf16[2,4,512,1024]{3,2,1,0:T(8,128)(2,1)S(1)}, bf16[2,4,512,1024]{3,2,1,0:T(8,128)(2,1)}) custom-call(s32[2]{0:T(128)S(1)} %pad_add_fusion.1.info, bf16[2048,1024]{1,0:T(8,128)(2,1)} %collective-permute-done.3.refs_0_, bf16[2048,1024]{1,0:T(8,128)(2,1)} %refs_1_.3, bf16[512,1024]{1,0:T(8,128)(2,1)S(1)} %copy-done.32, ...), custom_call_target="tpu_custom_call" | custom-call | flops 10737418240 | bytes 25165824 | tf_op jit(solution)/shard_map/pallas_call | solution.py:418
  156.3 16.8 %shard_map.326 = (bf16[2,512,512]{2,1,0:T(8,128)(2,1)S(1)}, f32[4,4,128,256]{3,2,1,0:T(8,128)S(1)}, f32[4,4,2,256]{3,2,1,0:T(2,128)S(1)}) custom-call(s32[4]{0:T(128)S(1)} %get-tuple-element.176.info, bf16[2,512,512]{2,1,0:T(8,128)(2,1)S(1)} %bitcast.144, bf16[2,2048,1024]{2,1,0:T(8,128)(2,1)S(1)} %bitcast.141), custom_call_target="tpu_custom_call" | custom-call | flops 8589934592 | bytes 16777216 | tf_op jit(solution)/shard_map/pallas_call | solution.py:670
  180.8 11.4 %shard_map.328 = (f32[512,1024]{1,0:T(8,128)S(1)}, f32[512,1024]{1,0:T(8,128)S(1)}, bf16[512,2048]{1,0:T(8,128)(2,1)S(1)}, bf16[512,2048]{1,0:T(8,128)(2,1)S(1)}) custom-call(bf16[512,1024]{1,0:T(8,128)(2,1)S(1)} %multiply_convert_fusion.normed.n_own, bf16[512,1024]{1,0:T(8,128)(2,1)S(1)} %fusion.17.grad.g_own, bf16[1024,2048]{1,0:T(8,128)(2,1)S(1)} %copy-done.27, ...), custom_call_target="tpu_custom_call" | custom-call | flops 8589934592 | bytes 14680064 | tf_op jit(solution)/shard_map/pallas_call | solution.py:762
  193.6 9.5 %collective-permute-done.10.normed.n_far = bf16[512,1024]{1,0:T(8,128)(2,1)S(1)} collective-permute-done((bf16[512,1024]{1,0:T(8,128)(2,1)S(1)}, bf16[512,1024]{1,0:T(8,128)(2,1)S(1)}, u32[]{:S(2)}, u32[]{:S(2)}) %collective-permute-start.10) | collective-permute-done | bytes 1048608 | tf_op jit(solution)/shard_map/ppermute | solution.py:306
  203.0 12.2 %shard_map.329 = (bf16[512,1024]{1,0:T(8,128)(2,1)S(1)}, bf16[512,1024]{1,0:T(8,128)(2,1)}, bf16[512,2048]{1,0:T(8,128)(2,1)S(1)}, bf16[512,2048]{1,0:T(8,128)(2,1)S(1)}) custom-call(bf16[512,1024]{1,0:T(8,128)(2,1)S(1)} %collective-permute-done.10.normed.n_far, bf16[512,1024]{1,0:T(8,128)(2,1)S(1)} %collective-permute-done.8.grad.g_far, ...), custom_call_target="tpu_custom_call" | custom-call | flops 8589934592 | bytes 14680064 | tf_op jit(solution)/shard_map/pallas_call | solution.py:762
  217.9 11.1 %shard_map.330 = bf16[4096,1024]{1,0:T(8,128)(2,1)S(1)} custom-call(bf16[512,1024]{1,0:T(8,128)(2,1)S(1)} %multiply_convert_fusion.normed.n_own, bf16[512,1024]{1,0:T(8,128)(2,1)S(1)} %collective-permute-done.10.normed.n_far, bf16[512,1024]{1,0:T(8,128)(2,1)S(1)} %fusion.17.grad.g_own, bf16[512,1024]{1,0:T(8,128)(2,1)S(1)} %collective-permute-done.8.grad.g_far, ...), custom_call_target="tpu_custom_call" | custom-call | flops 8589934592 | bytes 12582912 | tf_op jit(solution)/shard_map/pallas_call | solution.py:798
  229.0 3.3 copy-done.2
  232.3 8.5 %collective-permute-done.11 = bf16[512,1024]{1,0:T(8,128)(2,1)} collective-permute-done((bf16[512,1024]{1,0:T(8,128)(2,1)}, bf16[512,1024]{1,0:T(8,128)(2,1)}, u32[]{:S(2)}, u32[]{:S(2)}) %collective-permute-start.11) | collective-permute-done | bytes 1048608 | tf_op jit(solution)/shard_map/ppermute | solution.py:306
  243.6 3.8 fusion.49
  255.3 4.1 copy-done.37
  259.3 21.1 %shard_map.331 = (bf16[2,512,512]{2,1,0:T(8,128)(2,1)S(1)}, bf16[2,2048,1024]{2,1,0:T(8,128)(2,1)S(1)}) custom-call(s32[4]{0:T(128)S(1)} %get-tuple-element.176.info, bf16[2,512,512]{2,1,0:T(8,128)(2,1)S(1)} %bitcast.145, bf16[2,2048,1024]{2,1,0:T(8,128)(2,1)S(1)} %bitcast.142, bf16[2,512,512]{2,1,0:T(8,128)(2,1)S(1)} %bitcast.146, ...), custom_call_target="tpu_custom_call" | custom-call | flops 21474836480 | bytes 25165824 | tf_op jit(solution)/shard_map/pallas_call | solution.py:698
  280.5 6.1 %fusion.6 = bf16[2048,1024]{1,0:T(8,128)(2,1)} fusion(bf16[1024,1024]{1,0:T(8,128)(2,1)S(1)} %copy-done.30, bf16[2,2048,1024]{2,1,0:T(8,128)(2,1)S(1)} %get-tuple-element.128, s32[]{:T(128)S(6)} %select_n.20), kind=kOutput, calls=%fused_computation.7 | convolution fusion | flops 4297064448 | bytes 10485764 | tf_op jit(solution)/shard_map/dot_general | solution.py:437
  286.7 14.9 %convolution_convert_fusion.1 = bf16[1024,1024]{1,0:T(8,128)(2,1)} fusion(bf16[4096,1024]{1,0:T(8,128)(2,1)} %bitcast.140, bf16[4096,1024]{1,0:T(8,128)(2,1)} %bitcast.143), kind=kOutput, calls=%fused_computation.41 | convolution fusion | flops 8590983168 | bytes 18874368 | tf_op jit(solution)/shard_map/dot_general | solution.py:443
  301.6 8.2 %add_convert_fusion = bf16[2048,1024]{1,0:T(8,128)(2,1)} fusion(bf16[2048,1024]{1,0:T(8,128)(2,1)} %collective-permute-done.14, bf16[1024,1024]{1,0:T(8,128)(2,1)S(1)} %copy-done.30, bf16[2,2048,1024]{2,1,0:T(8,128)(2,1)S(1)} %copy-done.39, s32[]{:T(128)S(6)} %select_n.19), kind=kOutput, calls=%fused_computation | convolution fusion | flops 4301258752 | bytes 14680068 | tf_op jit(solution)/shard_map/dot_general | solution.py:437
  316.9 3.8 bitcast_convert_fusion.2
  323.9 3.5 bitcast_convert_fusion
  333.9 3.7 collective-permute-done.17
  338.5 16.7 %reduce-scatter.2.cloned.1.call-done = bf16[256,1024]{1,0:T(8,128)(2,1)} async-done(((bf16[4096,1024]{1,0:T(8,128)(2,1)}), bf16[256,1024]{1,0:T(8,128)(2,1)}) %reduce-scatter.2.cloned.1.call-update) | async-done | bytes 524304 | tf_op jit(solution)/shard_map/reduce_scatter | solution.py:1611
  357.2 180.8 %shard_map.332 = (bf16[16,256,1024]{2,1,0:T(8,128)(2,1)}, f32[2,8,1024]{2,1,0:T(8,128)}, bf16[512,1024]{1,0:T(8,128)(2,1)}, bf16[512,1024]{1,0:T(8,128)(2,1)}) custom-call(bf16[16,64,1024]{2,1,0:T(8,128)(2,1)} %bitcast.150, bf16[16,32,1024]{2,1,0:T(8,128)(2,1)} %bitcast.154, bf16[16,32,1024]{2,1,0:T(8,128)(2,1)} %bitcast.156, ...), custom_call_target="tpu_custom_call" | custom-call | bytes 251658240 | tf_op jit(solution)/shard_map/pallas_call | solution.py:1367
  538.0 3.4 copy-done.3
  541.4 6.0 %shard_map.336 = (f32[1024,512]{1,0:T(8,128)}, f32[1024,512]{1,0:T(8,128)}, f32[512,1024]{1,0:T(8,128)}, f32[512,1024]{1,0:T(8,128)}, f32[1024,512]{1,0:T(8,128)...) custom-call(bf16[16,256,1024]{2,1,0:T(8,128)(2,1)S(1)} %copy-done.3), custom_call_target="tpu_custom_call" | custom-call | bytes 25165824 | tf_op jit(solution)/shard_map/pallas_call | solution.py:1430
  550.5 3.4 copy-done
  553.9 7.0 %shard_map.337 = (f32[2048,1024]{1,0:T(8,128)}, f32[1024,2048]{1,0:T(8,128)}) custom-call(bf16[4096,1024]{1,0:T(8,128)(2,1)S(1)} %copy-done, bf16[4096,1024]{1,0:T(8,128)(2,1)S(1)} %copy-done), custom_call_target="tpu_custom_call" | custom-call | bytes 25165824 | tf_op jit(solution)/shard_map/pallas_call | solution.py:1450
  562.5 7.5 %shard_map.335 = bf16[2048,1024]{1,0:T(8,128)(2,1)} custom-call(s32[1]{0:T(128)} %bitcast.info, bf16[4,512,1024]{2,1,0:T(8,128)(2,1)S(1)} %bitcast.133, bf16[4,512,1024]{2,1,0:T(8,128)(2,1)} %bitcast.55.arrived), custom_call_target="tpu_custom_call" | custom-call | flops 1073741824 | bytes 8388608 | tf_op jit(solution)/shard_map/pallas_call | solution.py:356
  (233 shorter events, 81.0 us)
Async XLA Ops:
  7.2 348.0 %reduce-scatter.2.cloned.1.call-start = ((), (), s32[]{:S(2)}) async-start(), calls=%async_computation.1 | async-start | bytes 8912896 | tf_op jit(solution)/shard_map/reduce_scatter | solution.py:1611
  14.7 59.8 %copy-start.63 = (bf16[1024]{0:T(1024)(128)(2,1)S(1)}, bf16[1024]{0:T(1024)(128)(2,1)}, u32[]{:S(2)}) copy-start(bf16[1024]{0:T(1024)(128)(2,1)} %param.25) | copy-start | bytes 6148
  70.6 42.1 %copy-start.1 = (bf16[4,128,1024]{2,1,0:T(8,128)(2,1)}, bf16[4,128,1024]{2,1,0:T(8,128)(2,1)S(1)}, u32[]{:S(2)}) copy-start(bf16[4,128,1024]{2,1,0:T(8,128)(2,1)S(1)} %get-tuple-element.91) | copy-start | bytes 3145732
  70.6 42.1 %copy-start.16 = (bf16[512,1024]{1,0:T(8,128)(2,1)}, bf16[512,1024]{1,0:T(8,128)(2,1)S(1)}, u32[]{:S(2)}) copy-start(bf16[512,1024]{1,0:T(8,128)(2,1)S(1)} %get-tuple-element.97) | copy-start | bytes 3145732
  70.6 106.0 %copy-start.9 = (bf16[512,1024]{1,0:T(8,128)(2,1)}, bf16[512,1024]{1,0:T(8,128)(2,1)S(1)}, u32[]{:S(2)}) copy-start(bf16[512,1024]{1,0:T(8,128)(2,1)S(1)} %get-tuple-element.109) | copy-start | bytes 3145732
  70.6 39.1 %collective-permute-start.5 = (bf16[1536,1024]{1,0:T(8,128)(2,1)}, bf16[1536,1024]{1,0:T(8,128)(2,1)}, u32[]{:S(2)}, u32[]{:S(2)}) collective-permute-start(bf16[1536,1024]{1,0:T(8,128)(2,1)} %slice.57), channel_id=1, source_target_pairs={{1,2},{2,1},{5,6},{6,5},{9,10},{10,9},{13,14},{14,13},{17,18},{18,... | collective-permute-start | bytes 9437192 | tf_op jit(solution)/shard_map/ppermute | solution.py:306
  76.1 3.0 collective-permute-start
  76.1 53.6 %collective-permute-start.3 = (bf16[2048,1024]{1,0:T(8,128)(2,1)}, bf16[2048,1024]{1,0:T(8,128)(2,1)}, u32[]{:S(2)}, u32[]{:S(2)}) collective-permute-start(bf16[2048,1024]{1,0:T(8,128)(2,1)} %refs_1_.3), channel_id=1, source_target_pairs={{0,2},{3,1},{4,6},{7,5},{8,10},{11,9},{12,14},{15,13},{16,18},{19,... | collective-permute-start | bytes 12582920 | tf_op jit(solution)/shard_map/ppermute | solution.py:306
  77.6 43.4 %copy-start.62 = (s32[4]{0:T(128)}, s32[4]{0:T(128)S(1)}, u32[]{:S(2)}) copy-start(s32[4]{0:T(128)S(1)} %get-tuple-element.177.refs_5_) | copy-start | bytes 52
  93.0 20.7 %copy-start.6 = (f32[4,4,128,256]{3,2,1,0:T(8,128)}, f32[4,4,128,256]{3,2,1,0:T(8,128)S(1)}, u32[]{:S(2)}) copy-start(f32[4,4,128,256]{3,2,1,0:T(8,128)S(1)} %get-tuple-element.142.refs_9_) | copy-start | bytes 6291460
  93.0 20.7 %copy-start.23 = (bf16[2,512,512]{2,1,0:T(8,128)(2,1)}, bf16[2,512,512]{2,1,0:T(8,128)(2,1)S(1)}, u32[]{:S(2)}) copy-start(bf16[2,512,512]{2,1,0:T(8,128)(2,1)S(1)} %get-tuple-element.96) | copy-start | bytes 3145732
  93.0 20.7 %copy-start.25 = (f32[4,4,2,256]{3,2,1,0:T(2,128)}, f32[4,4,2,256]{3,2,1,0:T(2,128)S(1)}, u32[]{:S(2)}) copy-start(f32[4,4,2,256]{3,2,1,0:T(2,128)S(1)} %get-tuple-element.143.refs_10_) | copy-start | bytes 98308
  93.1 19.7 %copy-start.64 = (bf16[1024]{0:T(1024)(128)(2,1)S(1)}, bf16[1024]{0:T(1024)(128)(2,1)}, u32[]{:S(2)}) copy-start(bf16[1024]{0:T(1024)(128)(2,1)} %param.31) | copy-start | bytes 6148
  93.8 19.0 %collective-permute-start.1 = (bf16[512,1024]{1,0:T(8,128)(2,1)S(1)}, bf16[512,1024]{1,0:T(8,128)(2,1)S(1)}, u32[]{:S(2)}, u32[]{:S(2)}) collective-permute-start(bf16[512,1024]{1,0:T(8,128)(2,1)S(1)} %convolution_convert_fusion.7), channel_id=1, source_target_pairs={{0,2},{1,3},{2,0},{3,1},{4,6},{5,7},{6,4},{7,5},{8,10},{9,11},{10,... | collective-permute-start | bytes 3145736 | tf_op jit(solution)/shard_map/ppermute | solution.py:306
  109.7 20.0 %collective-permute-start.6 = (bf16[1536,1024]{1,0:T(8,128)(2,1)}, bf16[1536,1024]{1,0:T(8,128)(2,1)}, u32[]{:S(2)}, u32[]{:S(2)}) collective-permute-start(bf16[1536,1024]{1,0:T(8,128)(2,1)} %collective-permute-done.5.refs_4_), channel_id=1, source_target_pairs={{1,3},{2,0},{5,7},{6,4},{9,11},{10,8},{13,15},{14,12},{17,19},{18,... | collective-permute-start | bytes 9437192 | tf_op jit(solution)/shard_map/ppermute | solution.py:306
  115.0 11.5 %collective-permute-start.2 = (bf16[512,1024]{1,0:T(8,128)(2,1)}, bf16[512,1024]{1,0:T(8,128)(2,1)}, u32[]{:S(2)}, u32[]{:S(2)}) collective-permute-start(bf16[512,1024]{1,0:T(8,128)(2,1)} %multiply_convert_fusion.1), channel_id=1, source_target_pairs={{0,2},{1,3},{2,0},{3,1},{4,6},{5,7},{6,4},{7,5},{8,10},{9,11},{10,... | collective-permute-start | bytes 3145736 | tf_op jit(solution)/shard_map/ppermute | solution.py:306
  115.8 13.9 %collective-permute-start.4 = (bf16[512,1024]{1,0:T(8,128)(2,1)S(1)}, bf16[512,1024]{1,0:T(8,128)(2,1)}, u32[]{:S(2)}, u32[]{:S(2)}) collective-permute-start(bf16[512,1024]{1,0:T(8,128)(2,1)S(1)} %copy-done.32), channel_id=1, source_target_pairs={{1,3},{2,0},{5,7},{6,4},{9,11},{10,8},{13,15},{14,12},{17,19},{18,... | collective-permute-start | bytes 3145736 | tf_op jit(solution)/shard_map/ppermute | solution.py:306
  121.1 27.2 %collective-permute-start.7 = (bf16[512,1024]{1,0:T(8,128)(2,1)S(1)}, bf16[512,1024]{1,0:T(8,128)(2,1)S(1)}, u32[]{:S(2)}, u32[]{:S(2)}) collective-permute-start(bf16[512,1024]{1,0:T(8,128)(2,1)S(1)} %copy-done.11), channel_id=1, source_target_pairs={{1,2},{2,1},{5,6},{6,5},{9,10},{10,9},{13,14},{14,13},{17,18},{18,... | collective-permute-start | bytes 3145736 | tf_op jit(solution)/shard_map/ppermute | solution.py:306
  149.3 23.8 %collective-permute-start.8 = (bf16[512,1024]{1,0:T(8,128)(2,1)S(1)}, bf16[512,1024]{1,0:T(8,128)(2,1)S(1)}, u32[]{:S(2)}, u32[]{:S(2)}) collective-permute-start(bf16[512,1024]{1,0:T(8,128)(2,1)S(1)} %fusion.17.grad.g_own), channel_id=1, source_target_pairs={{0,1},{1,0},{2,3},{3,2},{4,5},{5,4},{6,7},{7,6},{8,9},{9,8},{10,11... | collective-permute-start | bytes 3145736 | tf_op jit(solution)/shard_map/ppermute | solution.py:306
  153.8 19.3 %copy-start.40 = (bf16[1024,512]{1,0:T(8,128)(2,1)}, bf16[1024,512]{1,0:T(8,128)(2,1)S(1)}, u32[]{:S(2)}) copy-start(bf16[1024,512]{1,0:T(8,128)(2,1)S(1)} %convolution_convert_fusion.4) | copy-start | bytes 3145732
  173.9 2.7 collective-permute-start.9
  177.8 25.3 %collective-permute-start.10 = (bf16[512,1024]{1,0:T(8,128)(2,1)S(1)}, bf16[512,1024]{1,0:T(8,128)(2,1)S(1)}, u32[]{:S(2)}, u32[]{:S(2)}) collective-permute-start(bf16[512,1024]{1,0:T(8,128)(2,1)S(1)} %multiply_convert_fusion.normed.n_own), channel_id=1, source_target_pairs={{0,1},{1,0},{2,3},{3,2},{4,5},{5,4},{6,7},{7,6},{8,9},{9,8},{10,11... | collective-permute-start | bytes 3145736 | tf_op jit(solution)/shard_map/ppermute | solution.py:306
  216.2 24.7 %collective-permute-start.11 = (bf16[512,1024]{1,0:T(8,128)(2,1)}, bf16[512,1024]{1,0:T(8,128)(2,1)}, u32[]{:S(2)}, u32[]{:S(2)}) collective-permute-start(bf16[512,1024]{1,0:T(8,128)(2,1)} %get-tuple-element.115), channel_id=1, source_target_pairs={{0,1},{1,0},{2,3},{3,2},{4,5},{5,4},{6,7},{7,6},{8,9},{9,8},{10,11... | collective-permute-start | bytes 3145736 | tf_op jit(solution)/shard_map/ppermute | solution.py:306
  247.4 2.9 collective-permute-start.12
  247.4 301.7 %all-gather.2.cloned.1.call-start = ((), (), s32[]{:S(2)}) async-start(), calls=%async_computation.2 | async-start | bytes 8912896 | tf_op jit(solution)/shard_map/all_gather | solution.py:1646
  253.5 27.0 %collective-permute-start.13 = (bf16[512,1024]{1,0:T(8,128)(2,1)S(1)}, bf16[512,1024]{1,0:T(8,128)(2,1)S(1)}, u32[]{:S(2)}, u32[]{:S(2)}) collective-permute-start(bf16[512,1024]{1,0:T(8,128)(2,1)S(1)} %copy-done.34), channel_id=1, source_target_pairs={{0,1},{1,0},{2,3},{3,2},{4,5},{5,4},{6,7},{7,6},{8,9},{9,8},{10,11... | collective-permute-start | bytes 3145736 | tf_op jit(solution)/shard_map/ppermute | solution.py:306
  259.3 21.2 %copy-start.30 = (bf16[1024,1024]{1,0:T(8,128)(2,1)S(1)}, bf16[1024,1024]{1,0:T(8,128)(2,1)}, u32[]{:S(2)}) copy-start(bf16[1024,1024]{1,0:T(8,128)(2,1)} %get-tuple-element.101.refs_6_) | copy-start | bytes 6291460
  286.6 14.9 %collective-permute-start.14 = (bf16[2048,1024]{1,0:T(8,128)(2,1)}, bf16[2048,1024]{1,0:T(8,128)(2,1)}, u32[]{:S(2)}, u32[]{:S(2)}) collective-permute-start(bf16[2048,1024]{1,0:T(8,128)(2,1)} %fusion.6), channel_id=1, source_target_pairs={{0,2},{1,3},{2,0},{3,1},{4,6},{5,7},{6,4},{7,5},{8,10},{9,11},{10,... | collective-permute-start | bytes 12582920 | tf_op jit(solution)/shard_map/ppermute | solution.py:306
  310.5 2.9 collective-permute-start.15
  316.6 11.6 %collective-permute-start.16 = (bf16[512,1024]{1,0:T(8,128)(2,1)S(1)}, bf16[512,1024]{1,0:T(8,128)(2,1)S(1)}, u32[]{:S(2)}, u32[]{:S(2)}) collective-permute-start(bf16[512,1024]{1,0:T(8,128)(2,1)S(1)} %get-tuple-element.169), channel_id=1, source_target_pairs={{0,2},{1,3},{2,0},{3,1},{4,6},{5,7},{6,4},{7,5},{8,10},{9,11},{10,... | collective-permute-start | bytes 3145736 | tf_op jit(solution)/shard_map/ppermute | solution.py:306
  321.4 16.1 %collective-permute-start.17 = (bf16[512,1024]{1,0:T(8,128)(2,1)S(1)}, bf16[512,1024]{1,0:T(8,128)(2,1)S(1)}, u32[]{:S(2)}, u32[]{:S(2)}) collective-permute-start(bf16[512,1024]{1,0:T(8,128)(2,1)S(1)} %add_convert_fusion.1), channel_id=1, source_target_pairs={{1,2},{2,1},{5,6},{6,5},{9,10},{10,9},{13,14},{14,13},{17,18},{18,... | collective-permute-start | bytes 3145736 | tf_op jit(solution)/shard_map/ppermute | solution.py:306
  355.2 193.9 %collective-permute-start.18 = (bf16[2048,1024]{1,0:T(8,128)(2,1)}, bf16[2048,1024]{1,0:T(8,128)(2,1)}, u32[]{:S(2)}, u32[]{:S(2)}) collective-permute-start(bf16[2048,1024]{1,0:T(8,128)(2,1)} %add_convert_fusion), channel_id=1, source_target_pairs={{1,2},{2,1},{5,6},{6,5},{9,10},{10,9},{13,14},{14,13},{17,18},{18,... | collective-permute-start | bytes 12582920 | tf_op jit(solution)/shard_map/ppermute | solution.py:306
  (58 other events, 234.5 us)
Sparse Core Ops, SparseCore 0:
  247.5 107.6 reduce-scatter.1
  357.4 89.8 all-gather.1

commit v4 on v3

--- a/solution.py
+++ b/solution.py
@@ -307,21 +307,24 @@
 
 
 def reorder_kernel(inverse, examples, info, held, arrived, target):
+    block = 256
+    chunk = block // examples
+
     def write(source):
-        if inverse:
-            value = source[...].reshape(-1, source.shape[2])
-        else:
-            value = source[...]
-        rows = value.shape[0]
-        chunk = rows // examples
-        high = lax.broadcasted_iota(jnp.int32, (rows, rows), 0)
-        low = lax.broadcasted_iota(jnp.int32, (rows, rows), 1)
+        high = lax.broadcasted_iota(jnp.int32, (block, block), 0)
+        low = lax.broadcasted_iota(jnp.int32, (block, block), 1)
         if inverse:
             hot = low == (high % examples) * chunk + high // examples
+            for i in range(target.shape[0] // block):
+                value = source[:, chunk * i : chunk * (i + 1), :].reshape(block, -1)
+                moved = nn(hot.astype(jnp.bfloat16), value).astype(jnp.bfloat16)
+                target[block * i : block * (i + 1), :] = moved
         else:
             hot = low == (high % chunk) * examples + high // chunk
-        moved = nn(hot.astype(jnp.bfloat16), value).astype(jnp.bfloat16)
-        target[...] = moved.reshape(target.shape)
+            for i in range(source.shape[0] // block):
+                value = source[block * i : block * (i + 1), :]
+                moved = nn(hot.astype(jnp.bfloat16), value).astype(jnp.bfloat16)
+                target[:, chunk * i : chunk * (i + 1), :] = moved.reshape(examples, chunk, -1)
 
     @pl.when(info[0] == 1)
     def _():
@@ -334,7 +337,7 @@
 
 def reorder(inverse, held, arrived, settled, examples):
     rows, width = held.shape
-    block = 256
+    block = min(rows, 512)
     flat = pl.BlockSpec((block, width), lambda i, s: (i, 0))
     flat_shape = (rows, width)
     split_shape = (examples, rows // examples, width)
@@ -556,57 +559,69 @@
 
 def cross_forward_kernel(info, queries, kv, out, mixed, level):
     length = info[pl.program_id(0)]
-    query = queries[...].reshape(-1, 128)
-    count = query.shape[0]
+    count = 2 * queries.shape[1]
     span = 2 * kv.shape[1]
-    heads = side_by_side(query)
 
     def body(keys):
-        joined = kv[...].reshape(span, 256)[:keys]
-        scores = masked_tail(nt(joined[:, :128], heads), length, span // 4)
-        top = jnp.max(scores, axis=0, keepdims=True)
-        weights = jnp.exp(scores - top)
-        total = jnp.sum(weights, axis=0, keepdims=True)
-        probs = (weights * (1.0 / total)).astype(jnp.bfloat16)
-        sums = nn(joined[:, 128:].T, probs)
-        parts = own_blocks(sums, count)
-        levels = top + jnp.log(total)
-        for head in range(2):
-            mixed[0, 0, HEAD_DIM * head : HEAD_DIM * (head + 1), :] = parts[head]
-            level[0, 0, head : head + 1, :] = levels[:, count * head : count * (head + 1)]
-        out[...] = heads_joined(*parts).astype(jnp.bfloat16).reshape(out.shape)
+        for pair in range(queries.shape[2] // 128):
+            columns = slice(128 * pair, 128 * (pair + 1))
+            heads = side_by_side(queries[:, :, columns].reshape(-1, 128))
+            joined = kv[:, :, 256 * pair : 256 * (pair + 1)].reshape(span, 256)[:keys]
+            scores = masked_tail(nt(joined[:, :128], heads), length, span // 4)
+            top = jnp.max(scores, axis=0, keepdims=True)
+            weights = jnp.exp(scores - top)
+            total = jnp.sum(weights, axis=0, keepdims=True)
+            probs = (weights * (1.0 / total)).astype(jnp.bfloat16)
+            parts = own_blocks(nn(joined[:, 128:].T, probs), count)
+            levels = top + jnp.log(total)
+            for head in range(2):
+                mixed[0, pair, HEAD_DIM * head : HEAD_DIM * (head + 1), :] = parts[head]
+                level[0, pair, head : head + 1, :] = levels[:, count * head : count * (head + 1)]
+            out[:, :, columns] = (
+                heads_joined(*parts).astype(jnp.bfloat16).reshape(2, count // 2, 128)
+            )
 
     by_length(length, span, body)
 
 
 def cross_backward_kernel(info, queries, kv, grads, mixed, level, dq, dkv):
     length = info[pl.program_id(0)]
-    query = queries[...].reshape(-1, 128)
-    count = query.shape[0]
-    grad = grads[...].reshape(-1, 128)
+    count = 2 * queries.shape[1]
     span = 2 * kv.shape[1]
-    heads, grad_heads = side_by_side(query), side_by_side(grad)
-    products = grad.astype(jnp.float32).T * mixed[0, 0]
-    inner = jnp.concatenate(
-        [jnp.sum(head_rows(products, head), axis=0, keepdims=True) for head in range(2)], axis=1
-    )
-    levels = jnp.concatenate([level[0, 0, 0:1, :], level[0, 0, 1:2, :]], axis=1)
 
     def body(keys):
-        joined = kv[...].reshape(span, 256)[:keys]
-        scores = masked_tail(nt(joined[:, :128], heads), length, span // 4)
-        probs = jnp.exp(scores - levels)
-        grad_scores = (probs * (nt(joined[:, 128:], grad_heads) - inner)).astype(jnp.bfloat16)
-        result = jnp.concatenate(
-            [nn(grad_scores, heads), nn(probs.astype(jnp.bfloat16), grad_heads)], axis=1
-        ).astype(jnp.bfloat16)
-        if keys < span:
+        for pair in range(queries.shape[2] // 128):
+            columns = slice(128 * pair, 128 * (pair + 1))
+            wide = slice(256 * pair, 256 * (pair + 1))
+            grad = grads[:, :, columns].reshape(-1, 128)
+            heads = side_by_side(queries[:, :, columns].reshape(-1, 128))
+            grad_heads = side_by_side(grad)
+            products = grad.astype(jnp.float32).T * mixed[0, pair]
+            inner = jnp.concatenate(
+                [jnp.sum(head_rows(products, head), axis=0, keepdims=True) for head in range(2)],
+                axis=1,
+            )
+            levels = jnp.concatenate([level[0, pair, 0:1, :], level[0, pair, 1:2, :]], axis=1)
+            joined = kv[:, :, wide].reshape(span, 256)[:keys]
+            scores = masked_tail(nt(joined[:, :128], heads), length, span // 4)
+            probs = jnp.exp(scores - levels)
+            grad_scores = (probs * (nt(joined[:, 128:], grad_heads) - inner)).astype(
+                jnp.bfloat16
+            )
             result = jnp.concatenate(
-                [result, jnp.zeros((span - keys, 256), jnp.bfloat16)], axis=0
+                [nn(grad_scores, heads), nn(probs.astype(jnp.bfloat16), grad_heads)], axis=1
+            ).astype(jnp.bfloat16)
+            if keys < span:
+                result = jnp.concatenate(
+                    [result, jnp.zeros((span - keys, 256), jnp.bfloat16)], axis=0
+                )
+            dkv[:, :, wide] = result.reshape(2, span // 2, 256)
+            sums = nn(joined[:, :128].T, grad_scores)
+            dq[:, :, columns] = (
+                heads_joined(*own_blocks(sums, count))
+                .astype(jnp.bfloat16)
+                .reshape(2, count // 2, 128)
             )
-        dkv[...] = result.reshape(dkv.shape)
-        sums = nn(joined[:, :128].T, grad_scores)
-        dq[...] = heads_joined(*own_blocks(sums, count)).astype(jnp.bfloat16).reshape(dq.shape)
 
     by_length(length, span, body)
 
@@ -665,16 +680,16 @@
 def cross_forward(info, queries, kv, examples):
     _, count, width = queries.shape
     pairs, size, span = width // 128, count // examples, kv.shape[1] // examples
-    thin = pl.BlockSpec((2, size, 128), lambda e, h: (0, e, h))
-    wide = pl.BlockSpec((2, span, 256), lambda e, h: (0, e, h))
+    thin = pl.BlockSpec((2, size, 256), lambda e, h: (0, e, h))
+    wide = pl.BlockSpec((2, span, 512), lambda e, h: (0, e, h))
     return pl.pallas_call(
         cross_forward_kernel,
-        grid=(examples, pairs),
+        grid=(examples, pairs // 2),
         in_specs=[SMEM_SPEC, thin, wide],
         out_specs=[
             thin,
-            pl.BlockSpec((1, 1, 128, 2 * size), lambda e, h: (e, h, 0, 0)),
-            pl.BlockSpec((1, 1, 2, 2 * size), lambda e, h: (e, h, 0, 0)),
+            pl.BlockSpec((1, 2, 128, 2 * size), lambda e, h: (e, h, 0, 0)),
+            pl.BlockSpec((1, 2, 2, 2 * size), lambda e, h: (e, h, 0, 0)),
         ],
         out_shape=[
             jax.ShapeDtypeStruct(queries.shape, jnp.bfloat16),
@@ -686,25 +701,25 @@
             4 * kv.size,
             examples * 2 * pairs * 4 * size * span,
         ),
-        compiler_params=pltpu.CompilerParams(vmem_limit_bytes=ATTEND_VMEM),
+        compiler_params=pltpu.CompilerParams(vmem_limit_bytes=32 * MIB),
     )(info, queries, kv)
 
 
 def cross_backward(info, queries, kv, grads, mixed, level, examples):
     _, count, width = queries.shape
     pairs, size, span = width // 128, count // examples, kv.shape[1] // examples
-    thin = pl.BlockSpec((2, size, 128), lambda e, h: (0, e, h))
-    wide = pl.BlockSpec((2, span, 256), lambda e, h: (0, e, h))
+    thin = pl.BlockSpec((2, size, 256), lambda e, h: (0, e, h))
+    wide = pl.BlockSpec((2, span, 512), lambda e, h: (0, e, h))
     return pl.pallas_call(
         cross_backward_kernel,
-        grid=(examples, pairs),
+        grid=(examples, pairs // 2),
         in_specs=[
             SMEM_SPEC,
             thin,
             wide,
             thin,
-            pl.BlockSpec((1, 1, 128, 2 * size), lambda e, h: (e, h, 0, 0)),
-            pl.BlockSpec((1, 1, 2, 2 * size), lambda e, h: (e, h, 0, 0)),
+            pl.BlockSpec((1, 2, 128, 2 * size), lambda e, h: (e, h, 0, 0)),
+            pl.BlockSpec((1, 2, 2, 2 * size), lambda e, h: (e, h, 0, 0)),
         ],
         out_specs=[thin, wide],
         out_shape=[
@@ -716,7 +731,7 @@
             6 * kv.size,
             examples * 2 * pairs * 4 * size * span,
         ),
-        compiler_params=pltpu.CompilerParams(vmem_limit_bytes=ATTEND_VMEM),
+        compiler_params=pltpu.CompilerParams(vmem_limit_bytes=58 * MIB),
     )(info, queries, kv, grads, mixed, level)
 
 
@@ -1022,9 +1037,10 @@
 def settle_kernel(groups, examples, *refs):
     parts, small, info, qkv = refs[:4], refs[4], refs[5], refs[6]
     bias, grads, mixed, level, normed, self_in, tok, grad_rest, gain = refs[7:16]
-    out, small_out, tok_grad, tok_back = refs[16:20]
+    result_out, small_out, tok_grad, tok_back = refs[16:20]
     value, first, second, third, small_in, rows_held, placed, grad_placed, result = refs[20:29]
-    far_sent, far_found, send, receive, small_send, small_get, load, single = refs[29:]
+    far_sent, far_found, send, receive, small_send, small_get, load, single = refs[29:37]
+    out, leave = refs[37:]
     count = len(parts)
     index, y = lax.axis_index("dp"), lax.axis_index("mp")
     core, x, z = index % 2, (index // 2) % 2, index // 4
@@ -1241,6 +1257,9 @@
     pairs = bias.shape[0]
     work = [functools.partial(attend, pair) for pair in range(pairs)] + [heads_sent, tokens_done]
 
+    def leaving(k):
+        return pltpu.make_async_copy(out.at[:, part(k)], result_out.at[:, part(k)], leave.at[k])
+
     def tick(t, carry):
         for i, piece_of_work in enumerate(work):
             pl.when(t == i)(piece_of_work)
@@ -1319,6 +1338,7 @@
         @pl.when(t >= 5)
         def _():
             back_core(t - 5).wait_recv()
+            leaving(t - 5).start()
 
         return carry
 
@@ -1346,6 +1366,7 @@
             back_z(k, step).wait_send()
         back_x(k).wait_send()
         back_core(k).wait_send()
+        leaving(k).wait()
         return carry
 
     lax.fori_loop(0, chunks, finish_sends, 0)
@@ -1367,7 +1388,7 @@
     return pl.pallas_call(
         functools.partial(settle_kernel, groups, examples),
         in_specs=[anywhere] * len(parts) + [whole, SMEM_SPEC, anywhere] + [whole] * 9,
-        out_specs=[whole] * 4,
+        out_specs=[anywhere] + [whole] * 3,
         out_shape=[
             jax.ShapeDtypeStruct((count, rows, width), kind),
             jax.ShapeDtypeStruct((2,) + small.shape, small.dtype),
@@ -1392,6 +1413,8 @@
             pltpu.SemaphoreType.DMA((rounds,)),
             pltpu.SemaphoreType.DMA((len(parts) + 1,)),
             pltpu.SemaphoreType.DMA((2, 2)),
+            pltpu.VMEM((count, rows, width), kind),
+            pltpu.SemaphoreType.DMA((chunks,)),
         ],
         cost_estimate=cost(0, 60 * count * rows * width),
         compiler_params=pltpu.CompilerParams(
@@ -1434,7 +1457,7 @@
         out_specs=[by_row, by_row, by_out, by_out] + [by_column] * 4,
         out_shape=[tall, tall, flat, flat] + [tall] * 4,
         cost_estimate=cost(0, 6 * value.size),
-        compiler_params=pltpu.CompilerParams(vmem_limit_bytes=ATTEND_VMEM),
+        compiler_params=pltpu.CompilerParams(vmem_limit_bytes=58 * MIB),
     )(value)
 
 
@@ -1463,7 +1486,7 @@
             jax.ShapeDtypeStruct((width, rows), jnp.float32),
         ],
         cost_estimate=cost(0, 12 * rows * width),
-        compiler_params=pltpu.CompilerParams(vmem_limit_bytes=ATTEND_VMEM),
+        compiler_params=pltpu.CompilerParams(vmem_limit_bytes=58 * MIB),
     )(value, value)
 
 
@@ -1575,6 +1598,10 @@
     a1, mixed_one, level_one = self_forward(self_info, qkv, bias, examples)
     r1 = tok_float + (nn(a1[0], self_out) + swap(low(nn(a1[1], self_out))).astype(jnp.float32))
 
+    n2 = low(rms_norm(r1, norm_cross.astype(jnp.float32)))
+    mem_rest, n2 = tie(mem_rest, n2)
+    n2 = both(n2)
+    q2 = low(nn(flat(n2), cross_q)).reshape(2, rows, -1)
     rest_far = permute(mem_rest, net["take"])
     mem, kv = memory_rows(
         place["y"],
@@ -1585,9 +1612,6 @@
     )
     mem = mem.reshape(2, -1, width)
     kv = kv.reshape(2, -1, 2 * inner)
-    n2 = both(low(rms_norm(r1, norm_cross.astype(jnp.float32))))
-    q2 = low(nn(flat(n2), cross_q)).reshape(2, rows, -1)
-
     kv, cot_raw = tie(kv, cot_raw)
     cot = reorder(False, cotangent, cot_raw, place["settled"], examples)
     positions = core * half_pos + jnp.arange(half_pos, dtype=jnp.int32)

time: 584 us -> 576 us (0.986)
  local copies, waits for them, and re-layouts: 35 us -> 23.9 us
    unnamed x138 -> x122, local copies, waits for them, and re-layouts: 28.9 us -> 17.8 us
  transfers between devices with their start and end apart: 21 -> 21, of which waited for: 9 -> 11; matrix products, arithmetic and copies ran while one was open for 12% -> 12% of each run, Pallas kernels for 48% -> 48%
where the time goes in v4:
time: 576 us; the launch traced here: 568 us
  Pallas kernels  359 us (62%)
  waiting for transfers between devices  61.4 us (11%)
  matrix products  57.4 us (10%)
  starting transfers between devices  26.7 us (5%)
  local copies, waits for them, and re-layouts  23.9 us (4%)
  other arithmetic  22 us (4%)
  between operations  17.1 us (3%)
    pallas_call x1, Pallas kernels, settle(): pl.pallas_call(functools.partial(settle_kernel, groups, examples), in_spe...  178 us
    pallas_call x1, Pallas kernels, gather(): pl.pallas_call(functools.partial(gather_kernel, groups, examples), in_spe...  53.9 us
    ppermute x19, waiting for transfers between devices, permute(): return lax.ppermute(value, ('dp', 'mp'), pairs)  48.9 us
    ppermute x19, starting transfers between devices, permute(): return lax.ppermute(value, ('dp', 'mp'), pairs)  26.6 us
    dot_general x4, matrix products, tn(): lax.dot_general(left, right, (((0,), (0,)), ((), ())), preferred_element_...  25.1 us
    pallas_call x2, Pallas kernels, ffn_rows(): pl.pallas_call(ffn_rows_kernel, grid=(units // tile,), in_specs=[whole, w...  23.9 us
    dot_general x6, matrix products, nt(): lax.dot_general(left, right, (((1,), (1,)), ((), ())), preferred_element_...  23.3 us
    pallas_call x1, Pallas kernels, cross_backward(): pl.pallas_call(cross_backward_kernel, grid=(examples, pairs // 2), in_spe...  21.5 us
  transfers between devices with their start and end apart: 21, of which 11 were waited for; matrix products, arithmetic and copies ran while one was open for 12% of the time, Pallas kernels for 48%

profile of v4, /device:TPU:6, one launch (start us, length us, event | category | flops | bytes accessed | tf_op | source)
XLA Modules:
  0.0 567.9 jit_solution(17195777144163486290)
XLA Ops:
  10.8 3.9 slice.57
  14.7 53.9 %shard_map.323 = (bf16[4,128,1024]{2,1,0:T(8,128)(2,1)S(1)}, bf16[512,1024]{1,0:T(8,128)(2,1)S(1)}, f32[8,128]{1,0:T(8,128)S(1)}, f32[8,128]{1,0:T(8,128)S(1)}, ...) custom-call(bf16[512,1024]{1,0:T(8,128)(2,1)} %tokens.1, ...), custom_call_target="tpu_custom_call" | custom-call | bytes 157286400 | tf_op jit(solution)/shard_map/pallas_call | solution.py:994
  72.5 3.7 collective-permute-start.2
  79.3 3.6 convolution_convert_fusion
  83.0 8.0 %shard_map.324 = (bf16[2,512,512]{2,1,0:T(8,128)(2,1)S(1)}, f32[4,4,128,256]{3,2,1,0:T(8,128)S(1)}, f32[4,4,2,256]{3,2,1,0:T(2,128)S(1)}) custom-call(s32[5]{0:T(128)S(1)} %pad_add_fusion.info, bf16[2,512,1536]{2,1,0:T(8,128)(2,1)S(1)} %bitcast.134, f32[4,2,256]{2,1,0:T(2,128)S(1)} %fusion.39.bias.refs_7_), custom_call_target="tpu_custom_call" | custom-call | flops 4294967296 | bytes 12582912 | tf_op jit(solution)/shard_map/pallas_call | solution.py:649
  96.8 14.6 %collective-permute-done.2.refs_4_ = bf16[1536,1024]{1,0:T(8,128)(2,1)} collective-permute-done((bf16[1536,1024]{1,0:T(8,128)(2,1)}, bf16[1536,1024]{1,0:T(8,128)(2,1)}, u32[]{:S(2)}, u32[]{:S(2)}) %collective-permute-start.2) | collective-permute-done | bytes 3145760 | tf_op jit(solution)/shard_map/ppermute | solution.py:306
  111.5 3.0 collective-permute-start.6
  114.5 3.4 collective-permute-start.5
  120.5 3.8 collective-permute-start.7
  126.6 18.3 %shard_map.325 = (bf16[2,4,512,1024]{3,2,1,0:T(8,128)(2,1)S(1)}, bf16[2,4,512,1024]{3,2,1,0:T(8,128)(2,1)}) custom-call(s32[2]{0:T(128)S(1)} %pad_add_fusion.1.info, bf16[2048,1024]{1,0:T(8,128)(2,1)} %collective-permute-done.4.refs_0_, bf16[2048,1024]{1,0:T(8,128)(2,1)} %refs_1_.3, bf16[512,1024]{1,0:T(8,128)(2,1)S(1)} %copy-done.31, ...), custom_call_target="tpu_custom_call" | custom-call | flops 10737418240 | bytes 25165824 | tf_op jit(solution)/shard_map/pallas_call | solution.py:421
  148.6 3.3 copy-done.35
  151.9 15.4 %shard_map.326 = (bf16[2,512,512]{2,1,0:T(8,128)(2,1)S(1)}, f32[4,4,128,256]{3,2,1,0:T(8,128)S(1)}, f32[4,4,2,256]{3,2,1,0:T(2,128)S(1)}) custom-call(s32[4]{0:T(128)S(1)} %get-tuple-element.180.info, bf16[2,512,512]{2,1,0:T(8,128)(2,1)S(1)} %bitcast.142, bf16[2,2048,1024]{2,1,0:T(8,128)(2,1)S(1)} %bitcast.141), custom_call_target="tpu_custom_call" | custom-call | flops 8589934592 | bytes 16777216 | tf_op jit(solution)/shard_map/pallas_call | solution.py:685
  177.3 11.4 %shard_map.328 = (f32[512,1024]{1,0:T(8,128)S(1)}, f32[512,1024]{1,0:T(8,128)S(1)}, bf16[512,2048]{1,0:T(8,128)(2,1)S(1)}, bf16[512,2048]{1,0:T(8,128)(2,1)S(1)}) custom-call(bf16[512,1024]{1,0:T(8,128)(2,1)S(1)} %multiply_convert_fusion.normed.n_own, bf16[512,1024]{1,0:T(8,128)(2,1)S(1)} %fusion.17.grad.g_own, bf16[1024,2048]{1,0:T(8,128)(2,1)S(1)} %copy-done.26, ...), custom_call_target="tpu_custom_call" | custom-call | flops 8589934592 | bytes 14680064 | tf_op jit(solution)/shard_map/pallas_call | solution.py:777
  190.0 9.5 %collective-permute-done.10.normed.n_far = bf16[512,1024]{1,0:T(8,128)(2,1)S(1)} collective-permute-done((bf16[512,1024]{1,0:T(8,128)(2,1)S(1)}, bf16[512,1024]{1,0:T(8,128)(2,1)S(1)}, u32[]{:S(2)}, u32[]{:S(2)}) %collective-permute-start.10) | collective-permute-done | bytes 1048608 | tf_op jit(solution)/shard_map/ppermute | solution.py:306
  199.5 12.6 %shard_map.329 = (bf16[512,1024]{1,0:T(8,128)(2,1)S(1)}, bf16[512,1024]{1,0:T(8,128)(2,1)}, bf16[512,2048]{1,0:T(8,128)(2,1)S(1)}, bf16[512,2048]{1,0:T(8,128)(2,1)S(1)}) custom-call(bf16[512,1024]{1,0:T(8,128)(2,1)S(1)} %collective-permute-done.10.normed.n_far, bf16[512,1024]{1,0:T(8,128)(2,1)S(1)} %collective-permute-done.8.grad.g_far, ...), custom_call_target="tpu_custom_call" | custom-call | flops 8589934592 | bytes 14680064 | tf_op jit(solution)/shard_map/pallas_call | solution.py:777
  214.8 11.1 %shard_map.330 = bf16[4096,1024]{1,0:T(8,128)(2,1)S(1)} custom-call(bf16[512,1024]{1,0:T(8,128)(2,1)S(1)} %multiply_convert_fusion.normed.n_own, bf16[512,1024]{1,0:T(8,128)(2,1)S(1)} %collective-permute-done.10.normed.n_far, bf16[512,1024]{1,0:T(8,128)(2,1)S(1)} %fusion.17.grad.g_own, bf16[512,1024]{1,0:T(8,128)(2,1)S(1)} %collective-permute-done.8.grad.g_far, ...), custom_call_target="tpu_custom_call" | custom-call | flops 8589934592 | bytes 12582912 | tf_op jit(solution)/shard_map/pallas_call | solution.py:813
  225.9 3.3 copy-done.1
  229.2 8.5 %collective-permute-done.11 = bf16[512,1024]{1,0:T(8,128)(2,1)} collective-permute-done((bf16[512,1024]{1,0:T(8,128)(2,1)}, bf16[512,1024]{1,0:T(8,128)(2,1)}, u32[]{:S(2)}, u32[]{:S(2)}) %collective-permute-start.11) | collective-permute-done | bytes 1048608 | tf_op jit(solution)/shard_map/ppermute | solution.py:306
  240.5 3.7 fusion.49
  252.6 21.5 %shard_map.331 = (bf16[2,512,512]{2,1,0:T(8,128)(2,1)}, bf16[2,2048,1024]{2,1,0:T(8,128)(2,1)}) custom-call(s32[4]{0:T(128)} %copy-done.25, bf16[2,512,512]{2,1,0:T(8,128)(2,1)} %bitcast.143, bf16[2,2048,1024]{2,1,0:T(8,128)(2,1)} %bitcast.140, bf16[2,512,512]{2,1,0:T(8,128)(2,1)} %bitcast.168, f32[4,4,128,256]{3,2,1,0:T(8,128)} %copy-done.37, ...), custom_call_target="tpu_custom_call" | custom-call | flops 21474836480 | bytes 25165824 | tf_op jit(solution)/shard_map/pallas_call | solution.py:713
  276.1 9.0 %fusion.6 = bf16[2048,1024]{1,0:T(8,128)(2,1)} fusion(bf16[1024,1024]{1,0:T(8,128)(2,1)S(1)} %copy-done.29, bf16[2,2048,1024]{2,1,0:T(8,128)(2,1)} %get-tuple-element.132, s32[]{:T(128)S(6)} %select_n.20), kind=kOutput, calls=%fused_computation.7 | convolution fusion | flops 4297064448 | bytes 10485764 | tf_op jit(solution)/shard_map/dot_general | solution.py:440
  285.1 15.4 %convolution_convert_fusion.1 = bf16[1024,1024]{1,0:T(8,128)(2,1)} fusion(bf16[4096,1024]{1,0:T(8,128)(2,1)} %bitcast.139, bf16[4096,1024]{1,0:T(8,128)(2,1)} %bitcast.167), kind=kOutput, calls=%fused_computation.41 | convolution fusion | flops 8590983168 | bytes 18874368 | tf_op jit(solution)/shard_map/dot_general | solution.py:446
  300.5 7.9 %add_convert_fusion = bf16[2048,1024]{1,0:T(8,128)(2,1)} fusion(bf16[2048,1024]{1,0:T(8,128)(2,1)} %collective-permute-done.14, bf16[1024,1024]{1,0:T(8,128)(2,1)S(1)} %copy-done.29, bf16[2,2048,1024]{2,1,0:T(8,128)(2,1)S(1)} %copy-done.59, s32[]{:T(128)S(6)} %select_n.19), kind=kOutput, calls=%fused_computation | convolution fusion | flops 4301258752 | bytes 14680068 | tf_op jit(solution)/shard_map/dot_general | solution.py:440
  315.5 3.7 bitcast_convert_fusion.2
  319.8 3.0 collective-permute-start.17
  322.8 3.8 bitcast_convert_fusion
  333.0 2.9 collective-permute-done.17
  336.9 12.5 %reduce-scatter.2.cloned.1.call-done = bf16[256,1024]{1,0:T(8,128)(2,1)} async-done(((bf16[4096,1024]{1,0:T(8,128)(2,1)}), bf16[256,1024]{1,0:T(8,128)(2,1)}) %reduce-scatter.2.cloned.1.call-update) | async-done | bytes 524304 | tf_op jit(solution)/shard_map/reduce_scatter | solution.py:1635
  351.4 178.4 %shard_map.332 = (bf16[16,256,1024]{2,1,0:T(8,128)(2,1)}, f32[2,8,1024]{2,1,0:T(8,128)}, bf16[512,1024]{1,0:T(8,128)(2,1)}, bf16[512,1024]{1,0:T(8,128)(2,1)}) custom-call(bf16[16,64,1024]{2,1,0:T(8,128)(2,1)} %bitcast.147, bf16[16,32,1024]{2,1,0:T(8,128)(2,1)} %bitcast.151, bf16[16,32,1024]{2,1,0:T(8,128)(2,1)} %bitcast.153, ...), custom_call_target="tpu_custom_call" | custom-call | bytes 251658240 | tf_op jit(solution)/shard_map/pallas_call | solution.py:1388
  529.9 9.7 %shard_map.336 = (f32[1024,512]{1,0:T(8,128)}, f32[1024,512]{1,0:T(8,128)}, f32[512,1024]{1,0:T(8,128)}, f32[512,1024]{1,0:T(8,128)}, f32[1024,512]{1,0:T(8,128)...) custom-call(bf16[16,256,1024]{2,1,0:T(8,128)(2,1)} %get-tuple-element.157.source), custom_call_target="tpu_custom_call" | custom-call | bytes 25165824 | tf_op jit(solution)/shard_map/pallas_call | solution.py:1453
  542.5 10.1 %shard_map.337 = (f32[2048,1024]{1,0:T(8,128)}, f32[1024,2048]{1,0:T(8,128)}) custom-call(bf16[4096,1024]{1,0:T(8,128)(2,1)} %all-gather.2.cloned.1.call-done.first.second, bf16[4096,1024]{1,0:T(8,128)(2,1)} %all-gather.2.cloned.1.call-done.first.second), custom_call_target="tpu_custom_call" | custom-call | bytes 25165824 | tf_op jit(solution)/shard_map/pallas_call | solution.py:1473
  555.2 5.6 shard_map.335
  (216 shorter events, 72.4 us)
Async XLA Ops:
  7.2 342.2 %reduce-scatter.2.cloned.1.call-start = ((), (), s32[]{:S(2)}) async-start(), calls=%async_computation.1 | async-start | bytes 8912896 | tf_op jit(solution)/shard_map/reduce_scatter | solution.py:1635
  14.7 55.8 %copy-start.54 = (bf16[1024]{0:T(1024)(128)(2,1)S(1)}, bf16[1024]{0:T(1024)(128)(2,1)}, u32[]{:S(2)}) copy-start(bf16[1024]{0:T(1024)(128)(2,1)} %param.25) | copy-start | bytes 6148
  70.5 24.1 %copy-start = (bf16[4,128,1024]{2,1,0:T(8,128)(2,1)}, bf16[4,128,1024]{2,1,0:T(8,128)(2,1)S(1)}, u32[]{:S(2)}) copy-start(bf16[4,128,1024]{2,1,0:T(8,128)(2,1)S(1)} %get-tuple-element.93) | copy-start | bytes 3145732
  70.5 24.1 %copy-start.14 = (bf16[512,1024]{1,0:T(8,128)(2,1)}, bf16[512,1024]{1,0:T(8,128)(2,1)S(1)}, u32[]{:S(2)}) copy-start(bf16[512,1024]{1,0:T(8,128)(2,1)S(1)} %get-tuple-element.99) | copy-start | bytes 3145732
  70.5 102.6 %copy-start.7 = (bf16[512,1024]{1,0:T(8,128)(2,1)}, bf16[512,1024]{1,0:T(8,128)(2,1)S(1)}, u32[]{:S(2)}) copy-start(bf16[512,1024]{1,0:T(8,128)(2,1)S(1)} %get-tuple-element.113) | copy-start | bytes 3145732
  72.5 4.6 collective-permute-start
  72.5 39.0 %collective-permute-start.2 = (bf16[1536,1024]{1,0:T(8,128)(2,1)}, bf16[1536,1024]{1,0:T(8,128)(2,1)}, u32[]{:S(2)}, u32[]{:S(2)}) collective-permute-start(bf16[1536,1024]{1,0:T(8,128)(2,1)} %slice.57), channel_id=1, source_target_pairs={{1,2},{2,1},{5,6},{6,5},{9,10},{10,9},{13,14},{14,13},{17,18},{18,... | collective-permute-start | bytes 9437192 | tf_op jit(solution)/shard_map/ppermute | solution.py:306
  76.4 44.0 %copy-start.53 = (s32[4]{0:T(128)}, s32[4]{0:T(128)S(1)}, u32[]{:S(2)}) copy-start(s32[4]{0:T(128)S(1)} %get-tuple-element.181.refs_5_) | copy-start | bytes 52
  76.4 72.2 %copy-start.25 = (s32[4]{0:T(128)}, s32[4]{0:T(128)S(1)}, u32[]{:S(2)}) copy-start(s32[4]{0:T(128)S(1)} %get-tuple-element.180.info) | copy-start | bytes 52
  91.8 2.7 collective-permute-start.1
  91.9 34.3 %collective-permute-start.4 = (bf16[2048,1024]{1,0:T(8,128)(2,1)}, bf16[2048,1024]{1,0:T(8,128)(2,1)}, u32[]{:S(2)}, u32[]{:S(2)}) collective-permute-start(bf16[2048,1024]{1,0:T(8,128)(2,1)} %refs_1_.3), channel_id=1, source_target_pairs={{0,2},{3,1},{4,6},{7,5},{8,10},{11,9},{12,14},{15,13},{16,18},{19,... | collective-permute-start | bytes 12582920 | tf_op jit(solution)/shard_map/ppermute | solution.py:306
  95.5 18.9 %copy-start.42 = (f32[512,1024]{1,0:T(8,128)}, f32[512,1024]{1,0:T(8,128)S(1)}, u32[]{:S(2)}) copy-start(f32[512,1024]{1,0:T(8,128)S(1)} %get-tuple-element.183) | copy-start | bytes 6291460
  95.6 18.9 %copy-start.31 = (bf16[512,1024]{1,0:T(8,128)(2,1)S(1)}, bf16[512,1024]{1,0:T(8,128)(2,1)}, u32[]{:S(2)}) copy-start(bf16[512,1024]{1,0:T(8,128)(2,1)} %copy-done.30) | copy-start | bytes 3145732
  95.6 24.9 %copy-start.9 = (bf16[512,1024]{1,0:T(8,128)(2,1)S(1)}, bf16[512,1024]{1,0:T(8,128)(2,1)}, u32[]{:S(2)}) copy-start(bf16[512,1024]{1,0:T(8,128)(2,1)} %held.1) | copy-start | bytes 3145732
  111.5 14.8 %collective-permute-start.6 = (bf16[1536,1024]{1,0:T(8,128)(2,1)}, bf16[1536,1024]{1,0:T(8,128)(2,1)}, u32[]{:S(2)}, u32[]{:S(2)}) collective-permute-start(bf16[1536,1024]{1,0:T(8,128)(2,1)} %collective-permute-done.2.refs_4_), channel_id=1, source_target_pairs={{1,3},{2,0},{5,7},{6,4},{9,11},{10,8},{13,15},{14,12},{17,19},{18,... | collective-permute-start | bytes 9437192 | tf_op jit(solution)/shard_map/ppermute | solution.py:306
  114.5 9.9 %collective-permute-start.3 = (bf16[512,1024]{1,0:T(8,128)(2,1)}, bf16[512,1024]{1,0:T(8,128)(2,1)}, u32[]{:S(2)}, u32[]{:S(2)}) collective-permute-start(bf16[512,1024]{1,0:T(8,128)(2,1)} %multiply_convert_fusion.1), channel_id=1, source_target_pairs={{0,2},{1,3},{2,0},{3,1},{4,6},{5,7},{6,4},{7,5},{8,10},{9,11},{10,... | collective-permute-start | bytes 3145736 | tf_op jit(solution)/shard_map/ppermute | solution.py:306
  114.5 11.8 %collective-permute-start.5 = (bf16[512,1024]{1,0:T(8,128)(2,1)S(1)}, bf16[512,1024]{1,0:T(8,128)(2,1)}, u32[]{:S(2)}, u32[]{:S(2)}) collective-permute-start(bf16[512,1024]{1,0:T(8,128)(2,1)S(1)} %copy-done.31), channel_id=1, source_target_pairs={{1,3},{2,0},{5,7},{6,4},{9,11},{10,8},{13,15},{14,12},{17,19},{18,... | collective-permute-start | bytes 3145736 | tf_op jit(solution)/shard_map/ppermute | solution.py:306
  120.5 24.3 %collective-permute-start.7 = (bf16[512,1024]{1,0:T(8,128)(2,1)S(1)}, bf16[512,1024]{1,0:T(8,128)(2,1)S(1)}, u32[]{:S(2)}, u32[]{:S(2)}) collective-permute-start(bf16[512,1024]{1,0:T(8,128)(2,1)S(1)} %copy-done.9), channel_id=1, source_target_pairs={{1,2},{2,1},{5,6},{6,5},{9,10},{10,9},{13,14},{14,13},{17,18},{18,... | collective-permute-start | bytes 3145736 | tf_op jit(solution)/shard_map/ppermute | solution.py:306
  145.8 23.8 %collective-permute-start.8 = (bf16[512,1024]{1,0:T(8,128)(2,1)S(1)}, bf16[512,1024]{1,0:T(8,128)(2,1)S(1)}, u32[]{:S(2)}, u32[]{:S(2)}) collective-permute-start(bf16[512,1024]{1,0:T(8,128)(2,1)S(1)} %fusion.17.grad.g_own), channel_id=1, source_target_pairs={{0,1},{1,0},{2,3},{3,2},{4,5},{5,4},{6,7},{7,6},{8,9},{9,8},{10,11... | collective-permute-start | bytes 3145736 | tf_op jit(solution)/shard_map/ppermute | solution.py:306
  148.6 18.6 %copy-start.36 = (bf16[1024,512]{1,0:T(8,128)(2,1)}, bf16[1024,512]{1,0:T(8,128)(2,1)S(1)}, u32[]{:S(2)}) copy-start(bf16[1024,512]{1,0:T(8,128)(2,1)S(1)} %convolution_convert_fusion.4) | copy-start | bytes 3145732
  170.3 2.7 collective-permute-start.9
  174.2 25.3 %collective-permute-start.10 = (bf16[512,1024]{1,0:T(8,128)(2,1)S(1)}, bf16[512,1024]{1,0:T(8,128)(2,1)S(1)}, u32[]{:S(2)}, u32[]{:S(2)}) collective-permute-start(bf16[512,1024]{1,0:T(8,128)(2,1)S(1)} %multiply_convert_fusion.normed.n_own), channel_id=1, source_target_pairs={{0,1},{1,0},{2,3},{3,2},{4,5},{5,4},{6,7},{7,6},{8,9},{9,8},{10,11... | collective-permute-start | bytes 3145736 | tf_op jit(solution)/shard_map/ppermute | solution.py:306
  213.0 24.7 %collective-permute-start.11 = (bf16[512,1024]{1,0:T(8,128)(2,1)}, bf16[512,1024]{1,0:T(8,128)(2,1)}, u32[]{:S(2)}, u32[]{:S(2)}) collective-permute-start(bf16[512,1024]{1,0:T(8,128)(2,1)} %get-tuple-element.119), channel_id=1, source_target_pairs={{0,1},{1,0},{2,3},{3,2},{4,5},{5,4},{6,7},{7,6},{8,9},{9,8},{10,11... | collective-permute-start | bytes 3145736 | tf_op jit(solution)/shard_map/ppermute | solution.py:306
  244.2 2.9 collective-permute-start.12
  244.2 296.9 %all-gather.2.cloned.1.call-start = ((), (), s32[]{:S(2)}) async-start(), calls=%async_computation.2 | async-start | bytes 8912896 | tf_op jit(solution)/shard_map/all_gather | solution.py:1670
  250.9 25.2 %collective-permute-start.13 = (bf16[512,1024]{1,0:T(8,128)(2,1)S(1)}, bf16[512,1024]{1,0:T(8,128)(2,1)S(1)}, u32[]{:S(2)}, u32[]{:S(2)}) collective-permute-start(bf16[512,1024]{1,0:T(8,128)(2,1)S(1)} %copy-done.33), channel_id=1, source_target_pairs={{0,1},{1,0},{2,3},{3,2},{4,5},{5,4},{6,7},{7,6},{8,9},{9,8},{10,11... | collective-permute-start | bytes 3145736 | tf_op jit(solution)/shard_map/ppermute | solution.py:306
  252.6 23.5 %copy-start.29 = (bf16[1024,1024]{1,0:T(8,128)(2,1)S(1)}, bf16[1024,1024]{1,0:T(8,128)(2,1)}, u32[]{:S(2)}) copy-start(bf16[1024,1024]{1,0:T(8,128)(2,1)} %get-tuple-element.105.refs_6_) | copy-start | bytes 6291460
  285.1 15.4 %collective-permute-start.14 = (bf16[2048,1024]{1,0:T(8,128)(2,1)}, bf16[2048,1024]{1,0:T(8,128)(2,1)}, u32[]{:S(2)}, u32[]{:S(2)}) collective-permute-start(bf16[2048,1024]{1,0:T(8,128)(2,1)} %fusion.6), channel_id=1, source_target_pairs={{0,2},{1,3},{2,0},{3,1},{4,6},{5,7},{6,4},{7,5},{8,10},{9,11},{10,... | collective-permute-start | bytes 12582920 | tf_op jit(solution)/shard_map/ppermute | solution.py:306
  309.1 2.8 collective-permute-start.15
  315.1 12.2 %collective-permute-start.16 = (bf16[512,1024]{1,0:T(8,128)(2,1)S(1)}, bf16[512,1024]{1,0:T(8,128)(2,1)S(1)}, u32[]{:S(2)}, u32[]{:S(2)}) collective-permute-start(bf16[512,1024]{1,0:T(8,128)(2,1)S(1)} %get-tuple-element.173), channel_id=1, source_target_pairs={{0,2},{1,3},{2,0},{3,1},{4,6},{5,7},{6,4},{7,5},{8,10},{9,11},{10,... | collective-permute-start | bytes 3145736 | tf_op jit(solution)/shard_map/ppermute | solution.py:306
  319.8 16.1 %collective-permute-start.17 = (bf16[512,1024]{1,0:T(8,128)(2,1)S(1)}, bf16[512,1024]{1,0:T(8,128)(2,1)S(1)}, u32[]{:S(2)}, u32[]{:S(2)}) collective-permute-start(bf16[512,1024]{1,0:T(8,128)(2,1)S(1)} %add_convert_fusion.1), channel_id=1, source_target_pairs={{1,2},{2,1},{5,6},{6,5},{9,10},{10,9},{13,14},{14,13},{17,18},{18,... | collective-permute-start | bytes 3145736 | tf_op jit(solution)/shard_map/ppermute | solution.py:306
  349.5 191.6 %collective-permute-start.18 = (bf16[2048,1024]{1,0:T(8,128)(2,1)}, bf16[2048,1024]{1,0:T(8,128)(2,1)}, u32[]{:S(2)}, u32[]{:S(2)}) collective-permute-start(bf16[2048,1024]{1,0:T(8,128)(2,1)} %add_convert_fusion), channel_id=1, source_target_pairs={{1,2},{2,1},{5,6},{6,5},{9,10},{10,9},{13,14},{14,13},{17,18},{18,... | collective-permute-start | bytes 12582920 | tf_op jit(solution)/shard_map/ppermute | solution.py:306
  (50 other events, 232.4 us)
Sparse Core Ops, SparseCore 0:
  244.3 105.0 reduce-scatter.1
  351.6 89.8 all-gather.1

commit v5 on v4

--- a/solution.py
+++ b/solution.py
@@ -306,17 +306,21 @@
     return lax.ppermute(value, ("dp", "mp"), pairs)
 
 
-def reorder_kernel(inverse, examples, info, held, arrived, target):
+def reorder_kernel(inverse, examples, info, held, *refs):
+    arrived, target = refs[:-1], refs[-1]
     block = 256
     chunk = block // examples
 
-    def write(source):
+    def write(*sources):
+        source = sources[0]
         high = lax.broadcasted_iota(jnp.int32, (block, block), 0)
         low = lax.broadcasted_iota(jnp.int32, (block, block), 1)
         if inverse:
             hot = low == (high % examples) * chunk + high // examples
             for i in range(target.shape[0] // block):
-                value = source[:, chunk * i : chunk * (i + 1), :].reshape(block, -1)
+                held_rows = slice(chunk * i, chunk * (i + 1))
+                value = jnp.concatenate([part[:, held_rows, :] for part in sources], axis=0)
+                value = value.reshape(block, -1)
                 moved = nn(hot.astype(jnp.bfloat16), value).astype(jnp.bfloat16)
                 target[block * i : block * (i + 1), :] = moved
         else:
@@ -332,7 +336,7 @@
 
     @pl.when(info[0] == 0)
     def _():
-        write(arrived)
+        write(*arrived)
 
 
 def reorder(inverse, held, arrived, settled, examples):
@@ -342,12 +346,14 @@
     flat_shape = (rows, width)
     split_shape = (examples, rows // examples, width)
     split_block = (examples, block // examples, width)
+    arrived = arrived if isinstance(arrived, tuple) else (arrived,)
     if inverse:
-        held, arrived = held.reshape(split_shape), arrived.reshape(split_shape)
-        in_specs = [
-            pl.BlockSpec(split_block, lambda i, s: (0, i * s[0], 0)),
-            pl.BlockSpec(split_block, lambda i, s: (0, i * (1 - s[0]), 0)),
-        ]
+        held = held.reshape(split_shape)
+        share = examples // len(arrived)
+        arrived = [part.reshape((share,) + split_shape[1:]) for part in arrived]
+        in_specs = [pl.BlockSpec(split_block, lambda i, s: (0, i * s[0], 0))] + [
+            pl.BlockSpec((share,) + split_block[1:], lambda i, s: (0, i * (1 - s[0]), 0))
+        ] * len(arrived)
         out_spec, out_shape = flat, flat_shape
     else:
         in_specs = [
@@ -367,7 +373,7 @@
         out_shape=jax.ShapeDtypeStruct(out_shape, held.dtype),
         cost_estimate=cost(2 * rows * width * block, 4 * rows * width),
         compiler_params=pltpu.CompilerParams(vmem_limit_bytes=SMALL_VMEM),
-    )(settled, held, arrived).reshape(flat_shape)
+    )(settled, held, *arrived).reshape(flat_shape)
 
 
 def memory_kernel(examples, info, *refs):
@@ -1650,7 +1656,8 @@
     dkv_swapped, cross_kv_part = tie(dkv_swapped, cross_kv_part)
     memory_grad = low(nt(pick(dkv, core), cross_kv) + dkv_swapped.astype(jnp.float32))
     memory_grad, cross_kv_part, dq2 = tie(memory_grad, cross_kv_part, dq2)
-    memory_back = turn(memory_grad)
+    half = memory_grad.shape[0] // 2
+    memory_back, memory_late = turn(memory_grad[:half]), turn(memory_grad[half:])
     dn2 = nt(dq2[0], cross_q) + swap(low(nt(dq2[1], cross_q))).astype(jnp.float32)
     back, gain_two = norm_backward(r1, norm_cross, dn2)
     dr1 = dr2 + back
@@ -1664,8 +1671,8 @@
     head_parts = [pieces(part) for part in head_parts]
     zero = jnp.zeros((1, width), jnp.float32)
     small = jnp.concatenate([zero, gain_two[None], gain_three[None], jnp.tile(zero, (5, 1))])
-    da1, head_parts, small, ffn_piece, block_back = tie(
-        da1, head_parts, small, ffn_piece, block_back
+    da1, head_parts, small, ffn_piece, block_back, memory_back = tie(
+        da1, head_parts, small, ffn_piece, block_back, memory_back
     )
     ffn_whole = lax.all_gather(ffn_piece, "dp", axis=0, tiled=True)
 
@@ -1678,7 +1685,8 @@
         groups,
         examples,
     )
-    small, ffn_whole, block_back, memory_back = tie(small, ffn_whole, block_back, memory_back)
+    small, ffn_whole, block_back, memory_late = tie(small, ffn_whole, block_back, memory_late)
+    memory_back = (memory_back, memory_late)
     gains = small[0, :3] + small[1, :3]
     by_distance = jnp.where(settled == 1, small[0, 4:6], small[1, 4:6]).reshape(-1, span)
     bias_grad = jnp.einsum("hd,db->bh", by_distance, level_hot, precision=highest)

time: 576 us -> 571 us (level)
  Pallas kernels: 359 us -> 347 us
    ppermute x19 -> x20, waiting for transfers between devices: 48.9 us -> 62.6 us  [permute(): return lax.ppermute(value, ('dp', 'mp'), pairs)]
    reduce_scatter x1, waiting for transfers between devices: 12.5 us -> 0.01 us  [on_chip_group(): lax.psum_scatter(ffn_part, 'dp', scatter_dimension=0, tiled=True)]
    pallas_call x1, Pallas kernels: 178 us -> 170 us  [settle(): pl.pallas_call(functools.partial(settle_kernel, groups, examples), in_spe...]
    ppermute x19 -> x20, starting transfers between devices: 26.6 us -> 30 us  [permute(): return lax.ppermute(value, ('dp', 'mp'), pairs)]
    unnamed x122 -> x128, local copies, waits for them, and re-layouts: 17.8 us -> 19.3 us
  transfers between devices with their start and end apart: 21 -> 22, of which waited for: 11 -> 9; matrix products, arithmetic and copies ran while one was open for 12% -> 12% of each run, Pallas kernels for 48% -> 47%
where the time goes in v5:
time: 571 us; the launch traced here: 562 us
  Pallas kernels  347 us (61%)
  waiting for transfers between devices  62.7 us (11%)
  matrix products  56.1 us (10%)
  starting transfers between devices  30.1 us (5%)
  local copies, waits for them, and re-layouts  27.2 us (5%)
  other arithmetic  22.1 us (4%)
  between operations  17.2 us (3%)
    pallas_call x1, Pallas kernels, settle(): pl.pallas_call(functools.partial(settle_kernel, groups, examples), in_spe...  170 us
    ppermute x20, waiting for transfers between devices, permute(): return lax.ppermute(value, ('dp', 'mp'), pairs)  62.6 us
    pallas_call x1, Pallas kernels, gather(): pl.pallas_call(functools.partial(gather_kernel, groups, examples), in_spe...  53.8 us
    ppermute x20, starting transfers between devices, permute(): return lax.ppermute(value, ('dp', 'mp'), pairs)  30 us
    dot_general x4, matrix products, tn(): lax.dot_general(left, right, (((0,), (0,)), ((), ())), preferred_element_...  25.1 us
    pallas_call x2, Pallas kernels, ffn_rows(): pl.pallas_call(ffn_rows_kernel, grid=(units // tile,), in_specs=[whole, w...  24 us
    dot_general x6, matrix products, nt(): lax.dot_general(left, right, (((1,), (1,)), ((), ())), preferred_element_...  22 us
    pallas_call x1, Pallas kernels, cross_backward(): pl.pallas_call(cross_backward_kernel, grid=(examples, pairs // 2), in_spe...  19.4 us
  transfers between devices with their start and end apart: 22, of which 9 were waited for; matrix products, arithmetic and copies ran while one was open for 12% of the time, Pallas kernels for 47%

profile of v5, /device:TPU:6, one launch (start us, length us, event | category | flops | bytes accessed | tf_op | source)
XLA Modules:
  0.0 562.5 jit_solution(18226876096649403148)
XLA Ops:
  10.8 3.9 slice.63
  14.7 53.8 %shard_map.323 = (bf16[4,128,1024]{2,1,0:T(8,128)(2,1)S(1)}, bf16[512,1024]{1,0:T(8,128)(2,1)S(1)}, f32[8,128]{1,0:T(8,128)S(1)}, f32[8,128]{1,0:T(8,128)S(1)}, ...) custom-call(bf16[512,1024]{1,0:T(8,128)(2,1)} %tokens.1, ...), custom_call_target="tpu_custom_call" | custom-call | bytes 157286400 | tf_op jit(solution)/shard_map/pallas_call | solution.py:1000
  72.5 3.7 collective-permute-start.2
  79.3 3.6 convolution_convert_fusion
  83.0 8.1 %shard_map.324 = (bf16[2,512,512]{2,1,0:T(8,128)(2,1)S(1)}, f32[4,4,128,256]{3,2,1,0:T(8,128)S(1)}, f32[4,4,2,256]{3,2,1,0:T(2,128)S(1)}) custom-call(s32[5]{0:T(128)S(1)} %pad_add_fusion.info, bf16[2,512,1536]{2,1,0:T(8,128)(2,1)S(1)} %bitcast.135, f32[4,2,256]{2,1,0:T(2,128)S(1)} %fusion.39.bias.refs_7_), custom_call_target="tpu_custom_call" | custom-call | flops 4294967296 | bytes 12582912 | tf_op jit(solution)/shard_map/pallas_call | solution.py:655
  96.8 14.6 %collective-permute-done.2.refs_4_ = bf16[1536,1024]{1,0:T(8,128)(2,1)} collective-permute-done((bf16[1536,1024]{1,0:T(8,128)(2,1)}, bf16[1536,1024]{1,0:T(8,128)(2,1)}, u32[]{:S(2)}, u32[]{:S(2)}) %collective-permute-start.2) | collective-permute-done | bytes 3145760 | tf_op jit(solution)/shard_map/ppermute | solution.py:306
  114.4 3.4 collective-permute-start.5
  120.5 3.8 collective-permute-start.7
  126.5 18.3 %shard_map.325 = (bf16[2,4,512,1024]{3,2,1,0:T(8,128)(2,1)S(1)}, bf16[2,4,512,1024]{3,2,1,0:T(8,128)(2,1)}) custom-call(s32[2]{0:T(128)S(1)} %pad_add_fusion.1.info, bf16[2048,1024]{1,0:T(8,128)(2,1)} %collective-permute-done.4.refs_0_, bf16[2048,1024]{1,0:T(8,128)(2,1)} %refs_1_.3, bf16[512,1024]{1,0:T(8,128)(2,1)S(1)} %copy-done.34, ...), custom_call_target="tpu_custom_call" | custom-call | flops 10737418240 | bytes 25165824 | tf_op jit(solution)/shard_map/pallas_call | solution.py:427
  148.6 3.3 copy-done.38
  151.8 13.8 %shard_map.326 = (bf16[2,512,512]{2,1,0:T(8,128)(2,1)S(1)}, f32[4,4,128,256]{3,2,1,0:T(8,128)S(1)}, f32[4,4,2,256]{3,2,1,0:T(2,128)S(1)}) custom-call(s32[4]{0:T(128)S(1)} %get-tuple-element.184.info, bf16[2,512,512]{2,1,0:T(8,128)(2,1)S(1)} %bitcast.144, bf16[2,2048,1024]{2,1,0:T(8,128)(2,1)S(1)} %bitcast.143), custom_call_target="tpu_custom_call" | custom-call | flops 8589934592 | bytes 16777216 | tf_op jit(solution)/shard_map/pallas_call | solution.py:691
  165.7 3.9 collective-permute-done.8.grad.g_far
  177.3 11.4 %shard_map.328 = (f32[512,1024]{1,0:T(8,128)S(1)}, f32[512,1024]{1,0:T(8,128)S(1)}, bf16[512,2048]{1,0:T(8,128)(2,1)S(1)}, bf16[512,2048]{1,0:T(8,128)(2,1)S(1)}) custom-call(bf16[512,1024]{1,0:T(8,128)(2,1)S(1)} %multiply_convert_fusion.normed.n_own, bf16[512,1024]{1,0:T(8,128)(2,1)S(1)} %fusion.17.grad.g_own, bf16[1024,2048]{1,0:T(8,128)(2,1)S(1)} %copy-done.29, ...), custom_call_target="tpu_custom_call" | custom-call | flops 8589934592 | bytes 14680064 | tf_op jit(solution)/shard_map/pallas_call | solution.py:783
  190.0 9.5 %collective-permute-done.10.normed.n_far = bf16[512,1024]{1,0:T(8,128)(2,1)S(1)} collective-permute-done((bf16[512,1024]{1,0:T(8,128)(2,1)S(1)}, bf16[512,1024]{1,0:T(8,128)(2,1)S(1)}, u32[]{:S(2)}, u32[]{:S(2)}) %collective-permute-start.10) | collective-permute-done | bytes 1048608 | tf_op jit(solution)/shard_map/ppermute | solution.py:306
  199.5 12.6 %shard_map.329 = (bf16[512,1024]{1,0:T(8,128)(2,1)S(1)}, bf16[512,1024]{1,0:T(8,128)(2,1)}, bf16[512,2048]{1,0:T(8,128)(2,1)S(1)}, bf16[512,2048]{1,0:T(8,128)(2,1)S(1)}) custom-call(bf16[512,1024]{1,0:T(8,128)(2,1)S(1)} %collective-permute-done.10.normed.n_far, bf16[512,1024]{1,0:T(8,128)(2,1)S(1)} %collective-permute-done.8.grad.g_far, ...), custom_call_target="tpu_custom_call" | custom-call | flops 8589934592 | bytes 14680064 | tf_op jit(solution)/shard_map/pallas_call | solution.py:783
  214.8 11.1 %shard_map.330 = bf16[4096,1024]{1,0:T(8,128)(2,1)S(1)} custom-call(bf16[512,1024]{1,0:T(8,128)(2,1)S(1)} %multiply_convert_fusion.normed.n_own, bf16[512,1024]{1,0:T(8,128)(2,1)S(1)} %collective-permute-done.10.normed.n_far, bf16[512,1024]{1,0:T(8,128)(2,1)S(1)} %fusion.17.grad.g_own, bf16[512,1024]{1,0:T(8,128)(2,1)S(1)} %collective-permute-done.8.grad.g_far, ...), custom_call_target="tpu_custom_call" | custom-call | flops 8589934592 | bytes 12582912 | tf_op jit(solution)/shard_map/pallas_call | solution.py:819
  225.9 3.3 copy-done.3
  229.2 8.5 %collective-permute-done.11 = bf16[512,1024]{1,0:T(8,128)(2,1)} collective-permute-done((bf16[512,1024]{1,0:T(8,128)(2,1)}, bf16[512,1024]{1,0:T(8,128)(2,1)}, u32[]{:S(2)}, u32[]{:S(2)}) %collective-permute-start.11) | collective-permute-done | bytes 1048608 | tf_op jit(solution)/shard_map/ppermute | solution.py:306
  240.4 3.8 fusion.49
  252.6 19.4 %shard_map.331 = (bf16[2,512,512]{2,1,0:T(8,128)(2,1)}, bf16[2,2048,1024]{2,1,0:T(8,128)(2,1)}) custom-call(s32[4]{0:T(128)} %copy-done.28, bf16[2,512,512]{2,1,0:T(8,128)(2,1)} %bitcast.145, bf16[2,2048,1024]{2,1,0:T(8,128)(2,1)} %bitcast.142, bf16[2,512,512]{2,1,0:T(8,128)(2,1)} %bitcast.170, f32[4,4,128,256]{3,2,1,0:T(8,128)} %copy-done.40, ...), custom_call_target="tpu_custom_call" | custom-call | flops 21474836480 | bytes 25165824 | tf_op jit(solution)/shard_map/pallas_call | solution.py:719
  272.0 4.1 collective-permute-done.13
  276.1 9.0 %fusion.6 = bf16[2048,1024]{1,0:T(8,128)(2,1)} fusion(bf16[1024,1024]{1,0:T(8,128)(2,1)S(1)} %copy-done.32, bf16[2,2048,1024]{2,1,0:T(8,128)(2,1)} %get-tuple-element.133, s32[]{:T(128)S(6)} %select_n.20), kind=kOutput, calls=%fused_computation.7 | convolution fusion | flops 4297064448 | bytes 10485764 | tf_op jit(solution)/shard_map/dot_general | solution.py:446
  285.1 15.4 %convolution_convert_fusion.1 = bf16[1024,1024]{1,0:T(8,128)(2,1)} fusion(bf16[4096,1024]{1,0:T(8,128)(2,1)} %bitcast.141, bf16[4096,1024]{1,0:T(8,128)(2,1)} %bitcast.169), kind=kOutput, calls=%fused_computation.41 | convolution fusion | flops 8590983168 | bytes 18874368 | tf_op jit(solution)/shard_map/dot_general | solution.py:452
  300.5 6.6 %add_convert_fusion = bf16[2048,1024]{1,0:T(8,128)(2,1)S(1)} fusion(bf16[2048,1024]{1,0:T(8,128)(2,1)} %collective-permute-done.14, bf16[1024,1024]{1,0:T(8,128)(2,1)S(1)} %copy-done.32, bf16[2,2048,1024]{2,1,0:T(8,128)(2,1)S(1)} %copy-done.62, s32[]{:T(128)S(6)} %select_n.19), kind=kOutput, calls=%fused_computation | convolution fusion | flops 4301258752 | bytes 14680068 | tf_op jit(solution)/shard_map/dot_general | solution.py:446
  310.3 3.2 collective-permute-start.18
  316.7 3.6 bitcast_convert_fusion.2
  323.5 3.8 bitcast_convert_fusion
  333.7 15.3 %collective-permute-done.17 = bf16[512,1024]{1,0:T(8,128)(2,1)S(1)} collective-permute-done((bf16[512,1024]{1,0:T(8,128)(2,1)S(1)}, bf16[512,1024]{1,0:T(8,128)(2,1)S(1)}, u32[]{:S(2)}, u32[]{:S(2)}) %collective-permute-start.17) | collective-permute-done | bytes 1048608 | tf_op jit(solution)/shard_map/ppermute | solution.py:306
  354.4 170.4 %shard_map.332 = (bf16[16,256,1024]{2,1,0:T(8,128)(2,1)}, f32[2,8,1024]{2,1,0:T(8,128)}, bf16[512,1024]{1,0:T(8,128)(2,1)}, bf16[512,1024]{1,0:T(8,128)(2,1)}) custom-call(bf16[16,64,1024]{2,1,0:T(8,128)(2,1)} %bitcast.149, bf16[16,32,1024]{2,1,0:T(8,128)(2,1)} %bitcast.153, bf16[16,32,1024]{2,1,0:T(8,128)(2,1)} %bitcast.155, ...), custom_call_target="tpu_custom_call" | custom-call | bytes 251658240 | tf_op jit(solution)/shard_map/pallas_call | solution.py:1394
  524.8 9.7 %shard_map.336 = (f32[1024,512]{1,0:T(8,128)}, f32[1024,512]{1,0:T(8,128)}, f32[512,1024]{1,0:T(8,128)}, f32[512,1024]{1,0:T(8,128)}, f32[1024,512]{1,0:T(8,128)...) custom-call(bf16[16,256,1024]{2,1,0:T(8,128)(2,1)} %get-tuple-element.159.source), custom_call_target="tpu_custom_call" | custom-call | bytes 25165824 | tf_op jit(solution)/shard_map/pallas_call | solution.py:1459
  537.5 10.1 %shard_map.337 = (f32[2048,1024]{1,0:T(8,128)}, f32[1024,2048]{1,0:T(8,128)}) custom-call(bf16[4096,1024]{1,0:T(8,128)(2,1)} %all-gather.2.cloned.1.call-done.first.second, bf16[4096,1024]{1,0:T(8,128)(2,1)} %all-gather.2.cloned.1.call-done.first.second), custom_call_target="tpu_custom_call" | custom-call | bytes 25165824 | tf_op jit(solution)/shard_map/pallas_call | solution.py:1479
  550.3 5.1 shard_map.335
  (225 shorter events, 75.4 us)
Async XLA Ops:
  7.2 344.1 %reduce-scatter.2.cloned.1.call-start = ((), (), s32[]{:S(2)}) async-start(), calls=%async_computation.1 | async-start | bytes 8912896 | tf_op jit(solution)/shard_map/reduce_scatter | solution.py:1641
  14.7 55.8 %copy-start.57 = (bf16[1024]{0:T(1024)(128)(2,1)S(1)}, bf16[1024]{0:T(1024)(128)(2,1)}, u32[]{:S(2)}) copy-start(bf16[1024]{0:T(1024)(128)(2,1)} %param.25) | copy-start | bytes 6148
  70.5 24.1 %copy-start = (bf16[4,128,1024]{2,1,0:T(8,128)(2,1)}, bf16[4,128,1024]{2,1,0:T(8,128)(2,1)S(1)}, u32[]{:S(2)}) copy-start(bf16[4,128,1024]{2,1,0:T(8,128)(2,1)S(1)} %get-tuple-element.94) | copy-start | bytes 3145732
  70.5 24.1 %copy-start.17 = (bf16[512,1024]{1,0:T(8,128)(2,1)}, bf16[512,1024]{1,0:T(8,128)(2,1)S(1)}, u32[]{:S(2)}) copy-start(bf16[512,1024]{1,0:T(8,128)(2,1)S(1)} %get-tuple-element.100) | copy-start | bytes 3145732
  70.5 102.6 %copy-start.10 = (bf16[512,1024]{1,0:T(8,128)(2,1)}, bf16[512,1024]{1,0:T(8,128)(2,1)S(1)}, u32[]{:S(2)}) copy-start(bf16[512,1024]{1,0:T(8,128)(2,1)S(1)} %get-tuple-element.114) | copy-start | bytes 3145732
  72.5 4.6 collective-permute-start
  72.5 39.0 %collective-permute-start.2 = (bf16[1536,1024]{1,0:T(8,128)(2,1)}, bf16[1536,1024]{1,0:T(8,128)(2,1)}, u32[]{:S(2)}, u32[]{:S(2)}) collective-permute-start(bf16[1536,1024]{1,0:T(8,128)(2,1)} %slice.63), channel_id=1, source_target_pairs={{1,2},{2,1},{5,6},{6,5},{9,10},{10,9},{13,14},{14,13},{17,18},{18,... | collective-permute-start | bytes 9437192 | tf_op jit(solution)/shard_map/ppermute | solution.py:306
  76.4 44.0 %copy-start.56 = (s32[4]{0:T(128)}, s32[4]{0:T(128)S(1)}, u32[]{:S(2)}) copy-start(s32[4]{0:T(128)S(1)} %get-tuple-element.185.refs_5_) | copy-start | bytes 52
  76.4 72.1 %copy-start.28 = (s32[4]{0:T(128)}, s32[4]{0:T(128)S(1)}, u32[]{:S(2)}) copy-start(s32[4]{0:T(128)S(1)} %get-tuple-element.184.info) | copy-start | bytes 52
  91.8 2.7 collective-permute-start.1
  91.9 34.3 %collective-permute-start.4 = (bf16[2048,1024]{1,0:T(8,128)(2,1)}, bf16[2048,1024]{1,0:T(8,128)(2,1)}, u32[]{:S(2)}, u32[]{:S(2)}) collective-permute-start(bf16[2048,1024]{1,0:T(8,128)(2,1)} %refs_1_.3), channel_id=1, source_target_pairs={{0,2},{3,1},{4,6},{7,5},{8,10},{11,9},{12,14},{15,13},{16,18},{19,... | collective-permute-start | bytes 12582920 | tf_op jit(solution)/shard_map/ppermute | solution.py:306
  95.5 18.9 %copy-start.45 = (f32[512,1024]{1,0:T(8,128)}, f32[512,1024]{1,0:T(8,128)S(1)}, u32[]{:S(2)}) copy-start(f32[512,1024]{1,0:T(8,128)S(1)} %get-tuple-element.187) | copy-start | bytes 6291460
  95.5 18.9 %copy-start.34 = (bf16[512,1024]{1,0:T(8,128)(2,1)S(1)}, bf16[512,1024]{1,0:T(8,128)(2,1)}, u32[]{:S(2)}) copy-start(bf16[512,1024]{1,0:T(8,128)(2,1)} %copy-done.33) | copy-start | bytes 3145732
  95.6 24.9 %copy-start.12 = (bf16[512,1024]{1,0:T(8,128)(2,1)S(1)}, bf16[512,1024]{1,0:T(8,128)(2,1)}, u32[]{:S(2)}) copy-start(bf16[512,1024]{1,0:T(8,128)(2,1)} %held.1) | copy-start | bytes 3145732
  111.4 14.8 %collective-permute-start.6 = (bf16[1536,1024]{1,0:T(8,128)(2,1)}, bf16[1536,1024]{1,0:T(8,128)(2,1)}, u32[]{:S(2)}, u32[]{:S(2)}) collective-permute-start(bf16[1536,1024]{1,0:T(8,128)(2,1)} %collective-permute-done.2.refs_4_), channel_id=1, source_target_pairs={{1,3},{2,0},{5,7},{6,4},{9,11},{10,8},{13,15},{14,12},{17,19},{18,... | collective-permute-start | bytes 9437192 | tf_op jit(solution)/shard_map/ppermute | solution.py:306
  114.4 9.9 %collective-permute-start.3 = (bf16[512,1024]{1,0:T(8,128)(2,1)}, bf16[512,1024]{1,0:T(8,128)(2,1)}, u32[]{:S(2)}, u32[]{:S(2)}) collective-permute-start(bf16[512,1024]{1,0:T(8,128)(2,1)} %multiply_convert_fusion.1), channel_id=1, source_target_pairs={{0,2},{1,3},{2,0},{3,1},{4,6},{5,7},{6,4},{7,5},{8,10},{9,11},{10,... | collective-permute-start | bytes 3145736 | tf_op jit(solution)/shard_map/ppermute | solution.py:306
  114.4 11.8 %collective-permute-start.5 = (bf16[512,1024]{1,0:T(8,128)(2,1)S(1)}, bf16[512,1024]{1,0:T(8,128)(2,1)}, u32[]{:S(2)}, u32[]{:S(2)}) collective-permute-start(bf16[512,1024]{1,0:T(8,128)(2,1)S(1)} %copy-done.34), channel_id=1, source_target_pairs={{1,3},{2,0},{5,7},{6,4},{9,11},{10,8},{13,15},{14,12},{17,19},{18,... | collective-permute-start | bytes 3145736 | tf_op jit(solution)/shard_map/ppermute | solution.py:306
  120.5 24.3 %collective-permute-start.7 = (bf16[512,1024]{1,0:T(8,128)(2,1)S(1)}, bf16[512,1024]{1,0:T(8,128)(2,1)S(1)}, u32[]{:S(2)}, u32[]{:S(2)}) collective-permute-start(bf16[512,1024]{1,0:T(8,128)(2,1)S(1)} %copy-done.12), channel_id=1, source_target_pairs={{1,2},{2,1},{5,6},{6,5},{9,10},{10,9},{13,14},{14,13},{17,18},{18,... | collective-permute-start | bytes 3145736 | tf_op jit(solution)/shard_map/ppermute | solution.py:306
  145.8 23.8 %collective-permute-start.8 = (bf16[512,1024]{1,0:T(8,128)(2,1)S(1)}, bf16[512,1024]{1,0:T(8,128)(2,1)S(1)}, u32[]{:S(2)}, u32[]{:S(2)}) collective-permute-start(bf16[512,1024]{1,0:T(8,128)(2,1)S(1)} %fusion.17.grad.g_own), channel_id=1, source_target_pairs={{0,1},{1,0},{2,3},{3,2},{4,5},{5,4},{6,7},{7,6},{8,9},{9,8},{10,11... | collective-permute-start | bytes 3145736 | tf_op jit(solution)/shard_map/ppermute | solution.py:306
  170.3 2.7 collective-permute-start.9
  174.2 25.3 %collective-permute-start.10 = (bf16[512,1024]{1,0:T(8,128)(2,1)S(1)}, bf16[512,1024]{1,0:T(8,128)(2,1)S(1)}, u32[]{:S(2)}, u32[]{:S(2)}) collective-permute-start(bf16[512,1024]{1,0:T(8,128)(2,1)S(1)} %multiply_convert_fusion.normed.n_own), channel_id=1, source_target_pairs={{0,1},{1,0},{2,3},{3,2},{4,5},{5,4},{6,7},{7,6},{8,9},{9,8},{10,11... | collective-permute-start | bytes 3145736 | tf_op jit(solution)/shard_map/ppermute | solution.py:306
  213.0 24.7 %collective-permute-start.11 = (bf16[512,1024]{1,0:T(8,128)(2,1)}, bf16[512,1024]{1,0:T(8,128)(2,1)}, u32[]{:S(2)}, u32[]{:S(2)}) collective-permute-start(bf16[512,1024]{1,0:T(8,128)(2,1)} %get-tuple-element.120), channel_id=1, source_target_pairs={{0,1},{1,0},{2,3},{3,2},{4,5},{5,4},{6,7},{7,6},{8,9},{9,8},{10,11... | collective-permute-start | bytes 3145736 | tf_op jit(solution)/shard_map/ppermute | solution.py:306
  244.2 2.9 collective-permute-start.12
  244.2 291.8 %all-gather.2.cloned.1.call-start = ((), (), s32[]{:S(2)}) async-start(), calls=%async_computation.2 | async-start | bytes 8912896 | tf_op jit(solution)/shard_map/all_gather | solution.py:1677
  250.9 25.2 %collective-permute-start.13 = (bf16[512,1024]{1,0:T(8,128)(2,1)S(1)}, bf16[512,1024]{1,0:T(8,128)(2,1)S(1)}, u32[]{:S(2)}, u32[]{:S(2)}) collective-permute-start(bf16[512,1024]{1,0:T(8,128)(2,1)S(1)} %copy-done.36), channel_id=1, source_target_pairs={{0,1},{1,0},{2,3},{3,2},{4,5},{5,4},{6,7},{7,6},{8,9},{9,8},{10,11... | collective-permute-start | bytes 3145736 | tf_op jit(solution)/shard_map/ppermute | solution.py:306
  252.6 23.5 %copy-start.32 = (bf16[1024,1024]{1,0:T(8,128)(2,1)S(1)}, bf16[1024,1024]{1,0:T(8,128)(2,1)}, u32[]{:S(2)}) copy-start(bf16[1024,1024]{1,0:T(8,128)(2,1)} %get-tuple-element.106.refs_6_) | copy-start | bytes 6291460
  285.1 15.4 %collective-permute-start.14 = (bf16[2048,1024]{1,0:T(8,128)(2,1)}, bf16[2048,1024]{1,0:T(8,128)(2,1)}, u32[]{:S(2)}, u32[]{:S(2)}) collective-permute-start(bf16[2048,1024]{1,0:T(8,128)(2,1)} %fusion.6), channel_id=1, source_target_pairs={{0,2},{1,3},{2,0},{3,1},{4,6},{5,7},{6,4},{7,5},{8,10},{9,11},{10,... | collective-permute-start | bytes 12582920 | tf_op jit(solution)/shard_map/ppermute | solution.py:306
  307.9 5.6 %collective-permute-start.15 = (bf16[512,1024]{1,0:T(8,128)(2,1)S(1)}, bf16[512,1024]{1,0:T(8,128)(2,1)S(1)}, u32[]{:S(2)}, u32[]{:S(2)}) collective-permute-start(bf16[512,1024]{1,0:T(8,128)(2,1)S(1)} %convolution_convert_fusion.5), channel_id=1, source_target_pairs={{0,2},{1,3},{2,0},{3,1},{4,6},{5,7},{6,4},{7,5},{8,10},{9,11},{10,... | collective-permute-start | bytes 3145736 | tf_op jit(solution)/shard_map/ppermute | solution.py:306
  310.3 39.7 %collective-permute-start.18 = (bf16[1024,1024]{1,0:T(8,128)(2,1)S(1)}, bf16[1024,1024]{1,0:T(8,128)(2,1)S(1)}, u32[]{:S(2)}, u32[]{:S(2)}) collective-permute-start(bf16[1024,1024]{1,0:T(8,128)(2,1)S(1)} %get-tuple-element.180), channel_id=1, source_target_pairs={{1,2},{2,1},{5,6},{6,5},{9,10},{10,9},{13,14},{14,13},{17,18},{18,... | collective-permute-start | bytes 6291464 | tf_op jit(solution)/shard_map/ppermute | solution.py:306
  316.7 11.3 %collective-permute-start.16 = (bf16[512,1024]{1,0:T(8,128)(2,1)S(1)}, bf16[512,1024]{1,0:T(8,128)(2,1)S(1)}, u32[]{:S(2)}, u32[]{:S(2)}) collective-permute-start(bf16[512,1024]{1,0:T(8,128)(2,1)S(1)} %get-tuple-element.175), channel_id=1, source_target_pairs={{0,2},{1,3},{2,0},{3,1},{4,6},{5,7},{6,4},{7,5},{8,10},{9,11},{10,... | collective-permute-start | bytes 3145736 | tf_op jit(solution)/shard_map/ppermute | solution.py:306
  321.0 28.0 %collective-permute-start.17 = (bf16[512,1024]{1,0:T(8,128)(2,1)S(1)}, bf16[512,1024]{1,0:T(8,128)(2,1)S(1)}, u32[]{:S(2)}, u32[]{:S(2)}) collective-permute-start(bf16[512,1024]{1,0:T(8,128)(2,1)S(1)} %add_convert_fusion.1), channel_id=1, source_target_pairs={{1,2},{2,1},{5,6},{6,5},{9,10},{10,9},{13,14},{14,13},{17,18},{18,... | collective-permute-start | bytes 3145736 | tf_op jit(solution)/shard_map/ppermute | solution.py:306
  351.3 184.8 %collective-permute-start.19 = (bf16[1024,1024]{1,0:T(8,128)(2,1)}, bf16[1024,1024]{1,0:T(8,128)(2,1)}, u32[]{:S(2)}, u32[]{:S(2)}) collective-permute-start(bf16[1024,1024]{1,0:T(8,128)(2,1)} %get-tuple-element.179), channel_id=1, source_target_pairs={{1,2},{2,1},{5,6},{6,5},{9,10},{10,9},{13,14},{14,13},{17,18},{18,... | collective-permute-start | bytes 6291464 | tf_op jit(solution)/shard_map/ppermute | solution.py:306
  (54 other events, 263.0 us)
Sparse Core Ops, SparseCore 0:
  244.3 105.1 reduce-scatter.1
  351.6 105.6 all-gather.1
